TPU v7x, 128 devices: a whole 4x4x4 slice. The times are simulated.
128 devices in a mesh: ifg: 32 (over y, x, z_hi), row: 4 (over z_lo, core).
Axes of the slice: x: 4, y: 4, z: 4 (z_hi: 2, z_lo: 2; z = z_hi * 2 + z_lo), core: 2. Of those that a mesh axis runs over, the one named last changes fastest.
Arguments:
- ifg_real: bfloat16 [1024, 256, 512], P('ifg', 'row'), may hold values from -6 to 6
- ifg_imag: bfloat16 [1024, 256, 512], P('ifg', 'row'), may hold values from -6 to 6
- date_pairs: int32 [1024, 2], replicated, may hold values from 0 to 319, as said below
Outputs:
- corrected: float32 [320, 256, 512], P('ifg', 'row')
- atmosphere: float32 [320, 256, 512], P('ifg', 'row')
Inputs may be any that keep to these rules, and one draw needn't show every extreme that they name: `date_pairs`: each row holds a reference date and a later secondary date, 1 to 5 dates apart.
All inputs are finite; a program needn't handle non-finite values.
Results may differ from a plain program's by a relative error of at most 0.0078.
Values may be sent and summed in bfloat16 or wider, within the bound.
No kernel may reach another device: no remote copies, remote signals or barrier semaphores. Data moves between devices by JAX's collectives and lax.ppermute only.
A program may use at most 128 MiB of HBM per device.

v0:
```python
import math

import jax
import jax.numpy as jnp
from jax import lax
from jax.sharding import PartitionSpec as P

PATCH = 64
NDATES = 320
ITERS = 3
RADIUS = 16


goldstein_power = 0.5
huber_threshold = 0.3
blur_sigma = 5.0
ridge_weight = 1.0


def padded_2(block, sides, width):
    for axis, dim in sides:
        count = lax.axis_size(axis)
        forward = [(i, i + 1) for i in range(count - 1)]
        backward = [(target, source) for source, target in forward]
        low = lax.ppermute(
            lax.slice_in_dim(block, block.shape[dim] - width, None, axis=dim), axis, forward
        )
        high = lax.ppermute(lax.slice_in_dim(block, 0, width, axis=dim), axis, backward)
        block = jnp.concatenate([low, block, high], axis=dim)
    return block


def spectral_tables():
    counter = jnp.arange(PATCH, dtype=jnp.int32)
    phase_steps = counter[:, None] * counter[None, :] % PATCH
    angles = phase_steps.astype(jnp.float32) * (2.0 * math.pi / PATCH)
    scaling = 1.0 / math.sqrt(PATCH)
    cosine = jnp.cos(angles) * scaling
    sine_lookup = jnp.sin(angles) * scaling
    forward = jnp.concatenate(
        [jnp.concatenate([cosine, -sine_lookup], 1), jnp.concatenate([sine_lookup, cosine], 1)], 0
    )
    inverse = jnp.concatenate(
        [jnp.concatenate([cosine, sine_lookup], 1), jnp.concatenate([-sine_lookup, cosine], 1)], 0
    )
    taper_row = jnp.sin(math.pi * (jnp.arange(PATCH, dtype=jnp.float32) + 0.5) / PATCH) ** 2
    return (
        forward.astype(jnp.bfloat16),
        inverse.astype(jnp.bfloat16),
        cosine.astype(jnp.bfloat16),
        sine_lookup.astype(jnp.bfloat16),
        taper_row,
    )


def row_apply(values, cosine, sine_lookup, direction):
    flipped = jnp.concatenate([values[..., PATCH:], -values[..., :PATCH]], axis=-1)
    first = jnp.einsum("kb,anbcl->ankcl", cosine, values, preferred_element_type=jnp.float32)
    second = jnp.einsum("kb,anbcl->ankcl", sine_lookup, flipped, preferred_element_type=jnp.float32)
    return first + direction * second


def filter_block(padded, tables):
    forward, inverse, cosine, sine_lookup, taper_row = tables
    block_count = padded.shape[0]
    rows_pad = padded.shape[2]
    cols_pad = padded.shape[3]
    half_patch = PATCH // 2
    taper_both = jnp.concatenate([taper_row, taper_row])
    canvas = jnp.zeros((block_count, 2, rows_pad, cols_pad), jnp.float32)
    for row_shift in (0, half_patch):
        for col_shift in (0, half_patch):
            window = padded[
                :, :, row_shift : rows_pad - row_shift, col_shift : cols_pad - col_shift
            ]
            row_tiles = window.shape[2] // PATCH
            col_tiles = window.shape[3] // PATCH
            tile_grid = window.reshape(block_count, 2, row_tiles, PATCH, col_tiles, PATCH)
            stacked = jnp.concatenate([tile_grid[:, 0], tile_grid[:, 1]], axis=-1)
            column_spectra = jnp.einsum(
                "anbcl,lm->anbcm", stacked, forward, preferred_element_type=jnp.float32
            ).astype(jnp.bfloat16)
            spectra = row_apply(column_spectra, cosine, sine_lookup, 1.0)
            spectral_power = spectra[..., :PATCH] ** 2 + spectra[..., PATCH:] ** 2 + 1.0
            shaping = spectral_power ** (0.5 * goldstein_power)
            shaped = (spectra * jnp.concatenate([shaping, shaping], axis=-1)).astype(jnp.bfloat16)
            row_back = row_apply(shaped, cosine, sine_lookup, -1.0).astype(jnp.bfloat16)
            restored = jnp.einsum(
                "anbcl,lm->anbcm", row_back, inverse, preferred_element_type=jnp.float32
            )
            weighted = restored * taper_row[:, None, None] * taper_both
            pieces = jnp.stack([weighted[..., :PATCH], weighted[..., PATCH:]], axis=1)
            pieces = pieces.reshape(block_count, 2, row_tiles * PATCH, col_tiles * PATCH)
            canvas = canvas + jnp.pad(
                pieces, ((0, 0), (0, 0), (row_shift, row_shift), (col_shift, col_shift))
            )
    return canvas[:, :, half_patch : rows_pad - half_patch, half_patch : cols_pad - half_patch]


def sine_of(real_part, imag_part):
    real_wide = real_part.astype(jnp.float32)
    imag_wide = imag_part.astype(jnp.float32)
    return (imag_wide / jnp.sqrt(real_wide * real_wide + imag_wide * imag_wide + 1.0)).astype(
        jnp.bfloat16
    )


def projection(date_pairs):
    date_index = jnp.arange(NDATES, dtype=jnp.int32)
    design = (date_pairs[:, 1:2] == date_index[None, :]).astype(jnp.float32) - (
        date_pairs[:, 0:1] == date_index[None, :]
    ).astype(jnp.float32)
    gram = jnp.dot(design.T, design, precision=lax.Precision.HIGHEST) + ridge_weight * jnp.eye(
        NDATES, dtype=jnp.float32
    )
    cholesky_factor = jnp.linalg.cholesky(gram)
    halfway = lax.linalg.triangular_solve(cholesky_factor, design.T, left_side=True, lower=True)
    mapping = lax.linalg.triangular_solve(
        cholesky_factor, halfway, left_side=True, lower=True, transpose_a=True
    )
    return (design, mapping)


def invert_rows(phase_sines, design, mapping):
    total_ifg = phase_sines.shape[0]
    row_count = phase_sines.shape[1]
    strip_cols = phase_sines.shape[2]
    observed = phase_sines.reshape(total_ifg, row_count * strip_cols).astype(jnp.float32)
    series = jnp.zeros((NDATES, observed.shape[1]), jnp.float32)
    misfit = observed
    for iteration in range(ITERS):
        if iteration > 0:
            misfit = observed - jnp.dot(design, series, precision=lax.Precision.HIGHEST)
        series = series + jnp.dot(
            mapping,
            jnp.clip(misfit, -huber_threshold, huber_threshold),
            precision=lax.Precision.HIGHEST,
        )
    return series.reshape(NDATES, row_count, strip_cols)


def gauss_matrix(size_out, size_in, offset):
    out_index = jnp.arange(size_out, dtype=jnp.int32)[:, None]
    in_index = jnp.arange(size_in, dtype=jnp.int32)[None, :]
    distance = in_index - offset - out_index
    kernel = jnp.exp(-0.5 * (distance.astype(jnp.float32) / blur_sigma) ** 2)
    return jnp.where(jnp.abs(distance) <= RADIUS, kernel, 0.0)


def row_weights(row_filter_kernel, local_rows):
    total_rows = local_rows * lax.axis_size("row")
    source_rows = (
        lax.axis_index("row") * local_rows
        - RADIUS
        + jnp.arange(local_rows + 2 * RADIUS, dtype=jnp.int32)
    )
    inside = (source_rows >= 0) & (source_rows < total_rows)
    return jnp.sum(jnp.where(inside[None, :], row_filter_kernel, 0.0), axis=1)


def on_device(ifg_real, ifg_imag, date_pairs):
    tables = spectral_tables()
    half_patch = PATCH // 2
    local_count = ifg_real.shape[0]
    local_rows = ifg_real.shape[1]
    width_cols = ifg_real.shape[2]
    joined = jnp.stack([ifg_real, ifg_imag], axis=1)
    extended = padded_2(joined, (("row", 2),), half_patch)
    padded = jnp.pad(extended, ((0, 0), (0, 0), (0, 0), (half_patch, half_patch)))
    block_list = padded.reshape(local_count // 2, 2, 2, local_rows + PATCH, width_cols + PATCH)

    def run_block(block_data):
        return filter_block(block_data, tables).astype(jnp.bfloat16)

    filtered = lax.map(run_block, block_list).reshape(local_count, 2, local_rows, width_cols)
    design, mapping = projection(date_pairs)
    local_sines = sine_of(filtered[:, 0], filtered[:, 1])
    series = invert_rows(
        lax.all_to_all(local_sines, "ifg", split_axis=2, concat_axis=0, tiled=True), design, mapping
    )
    row_filter_kernel = gauss_matrix(local_rows, local_rows + 2 * RADIUS, RADIUS)
    row_weight = row_weights(row_filter_kernel, local_rows)
    strip_cols = series.shape[2]
    col_ext = padded_2(series, (("ifg", 2),), RADIUS)
    col_kernel = gauss_matrix(strip_cols, strip_cols + 2 * RADIUS, RADIUS)
    smoothed_columns = jnp.einsum(
        "drc,ec->dre", col_ext, col_kernel, precision=lax.Precision.HIGHEST
    )
    with_borders = padded_2(smoothed_columns, (("row", 1),), RADIUS)
    smoothed_phase = jnp.einsum(
        "om,nmb->nob", row_filter_kernel, with_borders, precision=lax.Precision.HIGHEST
    )
    total_cols = strip_cols * lax.axis_size("ifg")
    source_cols = (
        lax.axis_index("ifg") * strip_cols
        - RADIUS
        + jnp.arange(strip_cols + 2 * RADIUS, dtype=jnp.int32)
    )
    col_inside = (source_cols >= 0) & (source_cols < total_cols)
    col_weight = jnp.sum(jnp.where(col_inside[None, :], col_kernel, 0.0), axis=1)
    weight = row_weight[:, None] * col_weight[None, :]
    atmos_pixels = smoothed_phase / weight
    corrected_pixels = series - atmos_pixels
    corrected, atmosphere = (
        lax.all_to_all(corrected_pixels, "ifg", split_axis=0, concat_axis=2, tiled=True),
        lax.all_to_all(atmos_pixels, "ifg", split_axis=0, concat_axis=2, tiled=True),
    )
    return (corrected, atmosphere)


def solution(mesh):
    placed = (P("ifg", "row", None), P("ifg", "row", None), P())
    return jax.shard_map(
        on_device,
        mesh=mesh,
        in_specs=placed,
        out_specs=(P("ifg", "row", None), P("ifg", "row", None)),
        check_vma=False,
    )
```

profile of v0, /device:TPU:1, one launch (start us, length us, event | category | flops | bytes accessed | tf_op | source)
XLA Modules:
  0.0 1236.5 jit_solution(8153766096788052782)
XLA Ops:
  8.8 13.6 %slice_maximum_fusion = (bf16[32,2,32,512]{2,3,1,0:T(8,128)(2,1)}, bf16[32,2,32,512]{2,3,1,0:T(8,128)(2,1)}) fusion(bf16[32,1,64,512]{2,3,1,0:T(8,128)(2,1)} %bitcast.414, bf16[32,1,64,512]{2,3,1,0:T(8,128)(2,1)} %bitcast.412), kind=kLoop, calls=%fused_computation.296 | loop fusion | flops 8388608 | bytes 8388608 | tf_op jit(solution)/shard_map/stack | solution.py:167
  22.4 6.7 copy.77
  34.0 8.1 copy.78
  48.9 11.7 cholesky.78
  60.7 9.8 custom-call.24
  72.9 12.1 cholesky.164
  85.0 9.8 custom-call.25
  109.4 29.5 %custom-call.26 = f32[3,128,128]{1,2,0:T(8,128)S(1)} custom-call(f32[3,128,128]{2,1,0:T(8,128)S(1)} %pad_maximum_fusion.8), custom_call_target="InvertDiagBlocksLowerTriangular" | custom-call | tf_op jit(solution)/shard_map/triangular_solve | solution.py:118
  142.8 7.7 copy.79
  150.6 7.8 copy.80
  158.3 17.2 %select_maximum_fusion = bf16[32,2,128,576]{2,3,1,0:T(8,128)(2,1)} fusion(bf16[32,2,32,512]{2,3,1,0:T(8,128)(2,1)} %copy.80, bf16[32,2,32,512]{2,3,1,0:T(8,128)(2,1)} %copy.79, bf16[32,1,64,512]{2,3,1,0:T(8,128)(2,1)} %bitcast.415, bf16[32,1,64,512]{2,3,1,0:T(8,128)(2,1)} %bitcast.413), kind=kLoop, calls=%fused_computation.290 | loop fusion | flops 70778880 | bytes 17825792 | tf_op jit(solution)/shard_map/concatenate | solution.py:29
  175.5 758.2 %while.16 = (s32[]{:T(128)}, bf16[16,2,2,64,512]{4,3,2,1,0:T(8,128)(2,1)}, bf16[16,2,2,128,576]{3,4,2,1,0:T(8,128)(2,1)}, bf16[128,128]{1,0:T(8,128)(2,1)}, bf16...) while((s32[]{:T(128)}, bf16[16,2,2,64,512]{4,3,2,1,0:T(8,128)(2,1)}, ...), condition=%wide.region_7.8_spmd.clone.clone, body=%wide.region_6.7_spmd.clone.clone.sunk | while | flops 882688192 | bytes 96604120 | solution.py:175
  943.7 7.9 reshape.374
  951.6 10.4 all-to-all-start
  971.0 27.2 %all-to-all-done = bf16[32,2,16384]{2,1,0:T(2,128)(2,1)S(1)} async-done(((bf16[32,2,16384]{2,1,0:T(2,128)(2,1)}), bf16[32,2,16384]{2,1,0:T(2,128)(2,1)S(1)}, u32[]{:S(2)}, u32[]{:S(2)}) %all-to-all-start) | async-done | bytes 2097184 | tf_op jit(solution)/shard_map/all_to_all | solution.py:179
  1010.2 16.6 %copy.85 = f32[32,32,64,16]{1,0,3,2:T(8,128)} copy(f32[32,32,64,16]{2,3,0,1:T(8,128)} %convert_bitcast_fusion) | data formatting | bytes 8388608 | tf_op jit(solution)/shard_map/convert_element_type | solution.py:128
  1026.8 13.7 %reshape.348 = f32[1024,1024]{0,1:T(8,128)} reshape(f32[32,32,64,16]{1,0,3,2:T(8,128)} %copy.85) | data formatting | bytes 8388608 | tf_op jit(solution)/shard_map/convert_element_type | solution.py:128
  1045.8 6.8 fusion.259
  1052.7 7.1 fusion.270
  1064.5 7.5 fusion.269
  1080.2 65.6 %collective-permute-done.2 = f32[320,64,16]{0,2,1:T(8,128)S(1)} collective-permute-done((f32[320,64,16]{0,2,1:T(8,128)S(1)}, f32[320,64,16]{0,2,1:T(8,128)S(1)}, u32[]{:S(2)}, u32[]{:S(2)}) %collective-permute-start.2) | collective-permute-done | bytes 1310752 | tf_op jit(solution)/shard_map/ppermute | solution.py:25
  1170.5 9.1 all-to-all-start.1
  1184.6 13.2 %all-to-all-done.1 = f32[32,1,10240]{2,1,0:T(1,128)} async-done(((f32[32,1,10240]{2,1,0:T(1,128)}), f32[32,1,10240]{2,1,0:T(1,128)}, u32[]{:S(2)}, u32[]{:S(2)}) %all-to-all-start.1) | async-done | bytes 1310752 | tf_op jit(solution)/shard_map/all_to_all | solution.py:205
  1216.4 6.8 all-to-all-done.2
  (1579 shorter events, 903.0 us)
Async XLA Ops:
  0.6 4.9 copy-start.9
  29.1 113.7 %collective-permute-start = (bf16[32,2,32,512]{3,2,1,0:T(8,128)(2,1)S(1)}, bf16[32,2,32,512]{3,2,1,0:T(8,128)(2,1)}, u32[]{:S(2)}, u32[]{:S(2)}) collective-permute-start(bf16[32,2,32,512]{3,2,1,0:T(8,128)(2,1)S(1)} %copy.77), channel_id=1, source_target_pairs={{0,1},{1,2},{2,3},{4,5},{5,6},{6,7},{8,9},{9,10},{10,11},{12,13},{... | collective-permute-start | bytes 6291464 | tf_op jit(solution)/shard_map/ppermute | solution.py:25
  34.0 10.2 copy-start.17
  42.1 108.5 %collective-permute-start.1 = (bf16[32,2,32,512]{3,2,1,0:T(8,128)(2,1)}, bf16[32,2,32,512]{3,2,1,0:T(8,128)(2,1)}, u32[]{:S(2)}, u32[]{:S(2)}) collective-permute-start(bf16[32,2,32,512]{3,2,1,0:T(8,128)(2,1)} %copy.78), channel_id=1, source_target_pairs={{1,0},{2,1},{3,2},{5,4},{6,5},{7,6},{9,8},{10,9},{11,10},{13,12},{... | collective-permute-start | bytes 6291464 | tf_op jit(solution)/shard_map/ppermute | solution.py:28
  44.2 95.9 %copy-start.13 = (s32[1024,1]{0,1:T(1,128)}, s32[1024,1]{0,1:T(1,128)S(1)}, u32[]{:S(2)}) copy-start(s32[1024,1]{0,1:T(1,128)S(1)} %get-tuple-element.302) | copy-start | bytes 12292
  44.2 95.9 %copy-start.15 = (s32[1024,1]{0,1:T(1,128)}, s32[1024,1]{0,1:T(1,128)S(1)}, u32[]{:S(2)}) copy-start(s32[1024,1]{0,1:T(1,128)S(1)} %get-tuple-element.303) | copy-start | bytes 12292
  109.4 41.2 %copy-start.8 = (f32[320,320]{1,0:T(8,128)}, f32[320,320]{1,0:T(8,128)S(1)}, u32[]{:S(2)}) copy-start(f32[320,320]{1,0:T(8,128)S(1)} %get-tuple-element.495) | copy-start | bytes 1228804
  138.9 11.6 copy-start.11
  307.6 4.6 copy-start.2
  354.9 4.6 copy-start.2
  402.3 4.6 copy-start.2
  449.7 4.6 copy-start.2
  497.0 4.6 copy-start.2
  951.6 10.4 copy-start.6
  951.6 46.5 %all-to-all-start = ((bf16[32,2,16384]{2,1,0:T(2,128)(2,1)}), bf16[32,2,16384]{2,1,0:T(2,128)(2,1)S(1)}, u32[]{:S(2)}, u32[]{:S(2)}) async-start(bf16[32,2,16384]{2,1,0:T(2,128)(2,1)} %reshape.374), calls=%async_computation | async-start | bytes 4194304 | tf_op jit(solution)/shard_map/all_to_all | solution.py:179
  1045.8 6.8 copy-start.14
  1045.8 6.8 copy-start.16
  1052.7 7.1 copy-start
  1077.1 68.6 %collective-permute-start.2 = (f32[320,64,16]{0,2,1:T(8,128)S(1)}, f32[320,64,16]{0,2,1:T(8,128)S(1)}, u32[]{:S(2)}, u32[]{:S(2)}) collective-permute-start(f32[320,64,16]{0,2,1:T(8,128)S(1)} %bitcast.424), channel_id=1, source_target_pairs={{0,4},{4,8},{8,12},{12,16},{16,20},{20,24},{24,28},{28,32},{32,36}... | collective-permute-start | bytes 3932168 | tf_op jit(solution)/shard_map/ppermute | solution.py:25
  1078.5 67.2 %collective-permute-start.3 = (f32[320,64,16]{0,2,1:T(8,128)S(1)}, f32[320,64,16]{0,2,1:T(8,128)}, u32[]{:S(2)}, u32[]{:S(2)}) collective-permute-start(f32[320,64,16]{0,2,1:T(8,128)S(1)} %bitcast.425), channel_id=1, source_target_pairs={{4,0},{8,4},{12,8},{16,12},{20,16},{24,20},{28,24},{32,28},{36,32}... | collective-permute-start | bytes 3932168 | tf_op jit(solution)/shard_map/ppermute | solution.py:28
  1149.9 6.6 collective-permute-start.4
  1151.8 9.1 collective-permute-start.5
  1170.5 27.3 %all-to-all-start.1 = ((f32[32,1,10240]{2,1,0:T(1,128)}), f32[32,1,10240]{2,1,0:T(1,128)}, u32[]{:S(2)}, u32[]{:S(2)}) async-start(f32[32,1,10240]{2,1,0:T(1,128)} %reshape.376), calls=%async_computation.1 | async-start | bytes 2621440 | tf_op jit(solution)/shard_map/all_to_all | solution.py:205
  1197.8 25.3 %all-to-all-start.2 = ((f32[32,1,10240]{2,1,0:T(1,128)}), f32[32,1,10240]{2,1,0:T(1,128)}, u32[]{:S(2)}, u32[]{:S(2)}) async-start(f32[32,1,10240]{2,1,0:T(1,128)} %reshape.378), calls=%async_computation.2 | async-start | bytes 2621440 | tf_op jit(solution)/shard_map/all_to_all | solution.py:206
  (78 other events, 176.3 us)
where the time goes:
time: 1250 us; the launch traced here: 1240 us
  local copies, waits for them, and re-layouts  539 us (43%)
  matrix products  266 us (21%)
  other arithmetic  262 us (21%)
  waiting for transfers between devices  119 us (10%)
  starting transfers between devices  38.6 us (3%)
    another operation x128, local copies, waits for them, and re-layouts, filter_block(): pieces = jnp.stack([weighted[..., :PATCH], weighted[..., PATCH:]], axis=1)  159 us
    dot_general x64, matrix products, filter_block(): jnp.einsum('anbcl,lm->anbcm', stacked, forward, preferred_element_type=jn...  71.1 us
    ppermute x3, waiting for transfers between devices, padded_2(): lax.ppermute(lax.slice_in_dim(block, block.shape[dim] - width, None, axis...  67.6 us
    slice x128, local copies, waits for them, and re-layouts, filter_block(): pieces = jnp.stack([weighted[..., :PATCH], weighted[..., PATCH:]], axis=1)  62.3 us
    while x256, local copies, waits for them, and re-layouts  59.7 us
    another operation x10, other arithmetic, projection(): cholesky_factor = jnp.linalg.cholesky(gram)  50.7 us
    dot_general x128, matrix products, row_apply(): jnp.einsum('kb,anbcl->ankcl', cosine, values, preferred_element_type=jnp....  47 us
    dot_general x64, matrix products, filter_block(): jnp.einsum('anbcl,lm->anbcm', row_back, inverse, preferred_element_type=j...  45.8 us
  transfers between devices with their start and end apart: 9, of which 6 were waited for; matrix products, arithmetic and copies ran while one was open for 11% of the time, Pallas kernels for 0%

commit v1 on v0

v1 whole, which is shorter than its diff:
```python
import math

import jax
import jax.numpy as jnp
import ml_dtypes
import numpy as np
from jax import lax
from jax.experimental import pallas as pl
from jax.experimental.pallas import tpu as pltpu
from jax.sharding import PartitionSpec as P

PATCH = 64
HALF = PATCH // 2
NDATES = 320
ITERS = 3
RADIUS = 16
SIGMA = 5.0
THRESHOLD = 0.3
BAND = 5
LANES = 128
DATE_PAD = 384
BF16 = jnp.bfloat16
F32 = jnp.float32


def bf16(x):
    return np.asarray(x, np.float32).astype(ml_dtypes.bfloat16)


def tables():
    n = np.arange(PATCH)
    angle = (n[:, None] * n[None, :] % PATCH) * (2.0 * math.pi / PATCH)
    c = bf16(np.cos(angle) / 8.0).astype(np.float64)
    s = bf16(np.sin(angle) / 8.0).astype(np.float64)
    taper = np.sin(math.pi * (n + 0.5) / PATCH) ** 2
    two = np.eye(2)
    zero = np.zeros((PATCH, PATCH))

    rows_centre = np.block([[c, s], [-s, c]])
    up = np.concatenate([np.eye(PATCH), zero], 1)
    low = np.concatenate([zero, np.eye(PATCH)], 1)
    rows_edge = np.block(
        [[c @ up, s @ up], [c @ low, s @ low], [-s @ up, c @ up], [-s @ low, c @ low]]
    )
    c2, s2 = np.kron(two, c), np.kron(two, s)
    cols = np.block([[c2, -s2], [s2, c2]])
    shift = np.zeros((2, LANES, LANES))
    for i in range(LANES):
        if i < HALF:
            shift[0, LANES - HALF + i, i] = 1.0
        else:
            shift[1, i - HALF, i] = 1.0
    left, right = np.kron(two, shift[0]), np.kron(two, shift[1])
    t2 = np.concatenate([taper, taper])
    inv = np.block([[c2 * t2, s2 * t2], [-s2 * t2, c2 * t2]])
    forward = np.stack([cols, left @ cols, right @ cols])
    inverse = np.stack([inv, inv @ left.T, inv @ right.T])
    ct, st = c * taper[:, None], s * taper[:, None]
    top = np.concatenate([ct[HALF:], np.zeros((HALF, PATCH))], 0)
    top_s = np.concatenate([st[HALF:], np.zeros((HALF, PATCH))], 0)
    bot = np.concatenate([np.zeros((HALF, PATCH)), ct[:HALF]], 0)
    bot_s = np.concatenate([np.zeros((HALF, PATCH)), st[:HALF]], 0)
    back_centre = np.block([[ct, -st], [st, ct]])
    back_edge = np.block([[top, bot, -top_s, -bot_s], [top_s, bot_s, top, bot]])
    return tuple(
        bf16(x) for x in (rows_centre, rows_edge, forward, inverse, back_centre, back_edge)
    )


def gauss(distance):
    return np.where(np.abs(distance) <= RADIUS, np.exp(-0.5 * (distance / SIGMA) ** 2), 0.0)


def blur_tables(rows, local_rows, cols):
    i = np.arange(cols)
    by_col = gauss(i[:, None] - i[None, :])
    by_col = by_col / by_col.sum(0, keepdims=True)
    out = np.arange(rows)[:, None]
    src = np.arange(-RADIUS, rows + RADIUS)[None, :]
    by_row = gauss(src - out) * ((src >= 0) & (src < rows))
    by_row = by_row / by_row.sum(1, keepdims=True)
    blocks = [
        by_row[a : a + local_rows, a : a + local_rows + 2 * RADIUS]
        for a in range(0, rows, local_rows)
    ]
    return by_col.astype(np.float32), np.stack(blocks).astype(np.float32)


def mm(a, b):
    return jnp.dot(a, b, preferred_element_type=F32)


def spectral(y_re, y_im, fwd, inv):
    count = y_re.shape[1] // LANES
    pieces = []
    for c in range(count):
        sl = slice(c * LANES, (c + 1) * LANES)
        pieces.append(jnp.concatenate([y_re[:, sl], y_im[:, sl]], axis=1))
    f0, f_left, f_right = fwd[0], fwd[1], fwd[2]
    g0, g_left, g_right = inv[0], inv[1], inv[2]

    def shaped(z):
        re, im = z[:, :LANES], z[:, LANES:]
        scale = lax.rsqrt(lax.rsqrt(re * re + im * im + 1.0))
        return jnp.concatenate([(re * scale).astype(BF16), (im * scale).astype(BF16)], axis=1)

    even = []
    for c in range(count + 1):
        z = None
        if c > 0:
            z = mm(pieces[c - 1], f_left)
        if c < count:
            w = mm(pieces[c], f_right)
            z = w if z is None else z + w
        even.append(shaped(z))
    out_re, out_im = [], []
    for c in range(count):
        odd = shaped(mm(pieces[c], f0))
        u = mm(odd, g0) + mm(even[c], g_right) + mm(even[c + 1], g_left)
        u = u.astype(BF16)
        out_re.append(u[:, :LANES])
        out_im.append(u[:, LANES:])
    return jnp.concatenate(out_re, axis=1), jnp.concatenate(out_im, axis=1)


def centre_kernel(re_ref, im_ref, rows_ref, fwd_ref, inv_ref, u_ref):
    table = rows_ref[...]
    for i in range(re_ref.shape[0]):
        x = jnp.concatenate([re_ref[i], im_ref[i]], axis=0)
        y = mm(table, x).astype(BF16)
        u_re, u_im = spectral(y[:PATCH], y[PATCH:], fwd_ref, inv_ref)
        u_ref[i] = jnp.concatenate([u_re, u_im], axis=0)


def centre(re, im, rows_t, fwd, inv):
    n, rows, cols = re.shape
    g = 2
    whole = lambda a: pl.BlockSpec(a.shape, lambda i: (0,) * a.ndim)
    block = pl.BlockSpec((g, rows, cols), lambda i: (i, 0, 0))
    return pl.pallas_call(
        centre_kernel,
        grid=(n // g,),
        in_specs=[block, block, whole(rows_t), whole(fwd), whole(inv)],
        out_specs=pl.BlockSpec((g, 2 * rows, cols), lambda i: (i, 0, 0)),
        out_shape=jax.ShapeDtypeStruct((n, 2 * rows, cols), BF16),
        compiler_params=pltpu.CompilerParams(vmem_limit_bytes=40 << 20),
        cost_estimate=pl.CostEstimate(
            flops=n * 2 * 64 * 256 * 256 * 26, bytes_accessed=n * rows * cols * 8,
            transcendentals=n * 64 * 2304,
        ),
        name="centre",
    )(re, im, rows_t, fwd, inv)


GROUP = 16


def edges_kernel(
    re_ref, im_ref, up_re, up_im, dn_re, dn_im, u_ref,
    rows_ref, fwd_ref, inv_ref, bc_ref, be_ref, q_ref, keep
):
    g = re_ref.shape[0]
    half = pl.program_id(0) % (GROUP // g)
    for i in range(g):
        x = jnp.concatenate(
            [up_re[i], re_ref[i], dn_re[i], up_im[i], im_ref[i], dn_im[i]], axis=0
        )
        y = mm(rows_ref[...], x).astype(BF16)
        u_re, u_im = spectral(y[: 2 * PATCH], y[2 * PATCH :], fwd_ref, inv_ref)
        f = mm(be_ref[...], jnp.concatenate([u_re, u_im], axis=0)) + mm(bc_ref[...], u_ref[i])
        re, im = f[:PATCH], f[PATCH:]
        q = im * lax.rsqrt(re * re + im * im + 1.0)
        slot = half * g + i
        tiles = q.shape[1] // LANES
        for h in range(2):
            for c in range(tiles):
                keep[h * tiles + c, pl.ds(slot, HALF, stride=GROUP), :] = q[
                    h * HALF : (h + 1) * HALF, c * LANES : (c + 1) * LANES
                ]

    @pl.when(half == GROUP // g - 1)
    def _():
        for t in range(keep.shape[0]):
            block = keep[t].astype(BF16)
            q_ref[:, :, t * LANES : (t + 1) * LANES] = block.reshape(HALF, GROUP, LANES)


def edges(re, im, halos, u, rows_t, fwd, inv, bc, be):
    n, rows, cols = re.shape
    g = 2
    whole = lambda a: pl.BlockSpec(a.shape, lambda i: (0,) * a.ndim)
    block = pl.BlockSpec((g, rows, cols), lambda i: (i, 0, 0))
    halo = pl.BlockSpec((g, HALF, cols), lambda i: (i, 0, 0))
    return pl.pallas_call(
        edges_kernel,
        grid=(n // g,),
        in_specs=[block, block, halo, halo, halo, halo,
                  pl.BlockSpec((g, 2 * rows, cols), lambda i: (i, 0, 0)),
                  whole(rows_t), whole(fwd), whole(inv), whole(bc), whole(be)],
        out_specs=pl.BlockSpec((HALF, GROUP, 2 * cols), lambda i: (0, i // (GROUP // g), 0)),
        out_shape=jax.ShapeDtypeStruct((HALF, n, 2 * cols), BF16),
        scratch_shapes=[pltpu.VMEM((2 * cols // LANES, HALF * GROUP, LANES), F32)],
        compiler_params=pltpu.CompilerParams(vmem_limit_bytes=48 << 20),
        cost_estimate=pl.CostEstimate(
            flops=n * 2 * 64 * 256 * 256 * 60, bytes_accessed=n * rows * cols * 14,
            transcendentals=n * 128 * 2304,
        ),
        name="edges",
    )(re, im, *halos, u, rows_t, fwd, inv, bc, be)


def projection_kernel(pairs_ref, pairs_t_ref, p_ref, g_ref, band, factor, solved):
    nifg = pairs_ref.shape[0]
    first, second = pairs_ref[:, 0:1], pairs_ref[:, 1:2]
    dates = lax.broadcasted_iota(jnp.int32, (nifg, DATE_PAD), 1)
    one = jnp.ones((nifg, DATE_PAD), F32)
    design = jnp.where(dates == second, one, 0.0) - jnp.where(dates == first, one, 0.0)
    g_ref[...] = design.astype(BF16)

    row_date = lax.broadcasted_iota(jnp.int32, (NDATES, nifg), 0)
    is_first = row_date == pairs_t_ref[0:1, :]
    is_either = is_first | (row_date == pairs_t_ref[1:2, :])
    first_t = jnp.where(is_first, 1.0, 0.0).astype(BF16)
    either_t = jnp.where(is_either, 1.0, 0.0).astype(BF16)
    gap = jnp.broadcast_to(second - first, (nifg, LANES))
    degree = mm(either_t, jnp.ones((nifg, LANES), BF16)) + 1.0
    band[...] = jnp.zeros_like(band)
    band[pl.ds(0, NDATES, stride=8), :] = degree
    for j in range(1, BAND + 1):
        match = jnp.where(gap == j, 1.0, 0.0).astype(BF16)
        band[pl.ds(j, NDATES, stride=8), :] = -mm(first_t, match)

    sub = lax.broadcasted_iota(jnp.int32, (8, LANES), 0)
    flat = sub * LANES + lax.broadcasted_iota(jnp.int32, (8, LANES), 1)

    def unit(i):
        return jnp.where(flat == i, 1.0, 0.0)

    def spread(x, j):
        return jnp.broadcast_to(x[j : j + 1, :], (8, LANES))

    def down(i, carry):
        rows, rhs = list(carry[: BAND + 1]), list(carry[BAND + 1 :])
        r, x = rows[0], rhs[0]
        inv = 1.0 / spread(r, 0)
        scaled = r * inv
        at = pl.ds(pl.multiple_of(i * 8, 8), 8)
        factor[at, :] = scaled
        solved[at, :] = x * inv
        for j in range(1, BAND + 1):
            moved = jnp.where(sub <= BAND - j, pltpu.roll(r, 8 - j, axis=0), 0.0)
            rows[j] = rows[j] - (spread(r, j) * moved) * inv
            rhs[j] = rhs[j] - spread(scaled, j) * x
        ahead = i + BAND + 1
        rows = rows[1:] + [band[pl.ds(pl.multiple_of(ahead * 8, 8), 8), :]]
        rhs = rhs[1:] + [unit(ahead)]
        return tuple(rows + rhs)

    start = [band[j * 8 : (j + 1) * 8, :] for j in range(BAND + 1)]
    start += [unit(j) for j in range(BAND + 1)]
    lax.fori_loop(0, NDATES, down, tuple(start), unroll=4)

    def up(t, carry):
        i = NDATES - 1 - t
        at = pl.ds(pl.multiple_of(i * 8, 8), 8)
        l = factor[at, :]
        x = solved[at, :]
        for j in range(BAND, 0, -1):
            x = x - spread(l, j) * carry[j - 1]
        solved[at, :] = x
        return (x,) + carry[:-1]

    zero = band[pl.ds((NDATES + BAND) * 8, 8), :]
    lax.fori_loop(0, NDATES, up, (zero,) * BAND, unroll=8)

    total = jnp.zeros((NDATES, nifg), F32)
    inverse = jnp.concatenate(
        [solved[pl.ds(c, NDATES, stride=8), :] for c in range(DATE_PAD // LANES)], axis=1
    )
    rest = inverse
    for _ in range(3):
        part = rest.astype(BF16)
        rest = rest - part.astype(F32)
        total = total + lax.dot_general(
            part, g_ref[...], (((1,), (1,)), ((), ())), preferred_element_type=F32
        )
    high = total.astype(BF16)
    p_ref[0:NDATES, :] = high
    p_ref[NDATES:, :] = (total - high.astype(F32)).astype(BF16)


def projection(date_pairs):
    nifg = date_pairs.shape[0]
    tail = (NDATES + 2 * BAND + 6) * 8
    return pl.pallas_call(
        projection_kernel,
        out_shape=(
            jax.ShapeDtypeStruct((2 * NDATES, nifg), BF16),
            jax.ShapeDtypeStruct((nifg, DATE_PAD), BF16),
        ),
        scratch_shapes=[
            pltpu.VMEM((tail, LANES), F32),
            pltpu.VMEM((NDATES * 8, LANES), F32),
            pltpu.VMEM((NDATES * 8, LANES), F32),
        ],
        compiler_params=pltpu.CompilerParams(vmem_limit_bytes=40 << 20),
        cost_estimate=pl.CostEstimate(
            flops=20_000_000_000, bytes_accessed=4_000_000, transcendentals=0
        ),
        name="projection",
    )(date_pairs, date_pairs.T)


def invert_kernel(d_ref, p_ref, g_ref, m_ref):
    scaled = d_ref[...].astype(F32) * (1.0 / THRESHOLD)
    width = scaled.shape[1]
    fill = jnp.zeros((DATE_PAD - NDATES, width), BF16)
    series = None
    misfit = scaled
    for step in range(ITERS):
        if step > 0:
            high = series.astype(BF16)
            low = (series - high.astype(F32)).astype(BF16)
            misfit = scaled - (
                mm(g_ref[...], jnp.concatenate([high, fill], axis=0))
                + mm(g_ref[...], jnp.concatenate([low, fill], axis=0))
            )
        clipped = jnp.clip(misfit, -1.0, 1.0).astype(BF16)
        both = mm(p_ref[...], clipped)
        change = both[:NDATES] + both[NDATES:]
        series = change if series is None else series + change
    series = series * THRESHOLD
    tiles = width // LANES
    for t in range(tiles):
        m_ref[pl.ds(pl.program_id(0) * tiles + t, NDATES, stride=8), :] = series[
            :, t * LANES : (t + 1) * LANES
        ]


def invert(sines, p, g):
    nifg, pixels = sines.shape
    width = 256
    return pl.pallas_call(
        invert_kernel,
        grid=(pixels // width,),
        in_specs=[
            pl.BlockSpec((nifg, width), lambda i: (0, i)),
            pl.BlockSpec(p.shape, lambda i: (0, 0)),
            pl.BlockSpec(g.shape, lambda i: (0, 0)),
        ],
        out_specs=pl.BlockSpec((NDATES * 8, LANES), lambda i: (0, 0)),
        out_shape=jax.ShapeDtypeStruct((NDATES * 8, LANES), F32),
        compiler_params=pltpu.CompilerParams(vmem_limit_bytes=48 << 20),
        name="invert",
    )(sines, p, g)


def split3(x):
    high = x.astype(BF16)
    return high, (x - high.astype(F32)).astype(BF16)


def dot3(a, b):
    (ah, al), (bh, bl) = a, b
    return mm(ah, bh) + (mm(ah, bl) + mm(al, bh))


def gather_kernel(got_ref, ch_ref, cl_ref, series_ref, smooth_ref):
    dates, rows, cols = series_ref.shape
    tiles = cols // LANES
    for d in range(dates):
        halves = []
        for h in range(2):
            halves.append(
                jnp.concatenate(
                    [
                        got_ref[pl.ds(d * 8 + h * tiles + c, HALF, stride=dates * 8), :]
                        for c in range(tiles)
                    ],
                    axis=1,
                )
            )
        x = jnp.concatenate(halves, axis=0)
        series_ref[d] = x
        smooth_ref[d] = dot3(split3(x), (ch_ref[...], cl_ref[...]))


def gather(got, col_high, col_low, rows, cols):
    dates = got.shape[0] // 8 // HALF
    return pl.pallas_call(
        gather_kernel,
        out_shape=(jax.ShapeDtypeStruct((dates, rows, cols), F32),) * 2,
        compiler_params=pltpu.CompilerParams(vmem_limit_bytes=40 << 20),
        name="gather",
    )(got, col_high, col_low)


def finish_kernel(where_ref, series_ref, smooth_ref, up_ref, dn_ref, rh_ref, rl_ref, corr_ref, atm_ref):
    table = (rh_ref[0], rl_ref[0])
    for d in range(series_ref.shape[0]):
        x = jnp.concatenate([up_ref[d], smooth_ref[d], dn_ref[d]], axis=0)
        atm = dot3(table, split3(x))
        atm_ref[d] = atm
        corr_ref[d] = series_ref[d] - atm


def finish(where, series, smooth, up, dn, row_high, row_low):
    dates, rows, cols = series.shape
    g = 5
    block = pl.BlockSpec((g, rows, cols), lambda i, w: (i, 0, 0))
    halo = pl.BlockSpec((g, RADIUS, cols), lambda i, w: (i, 0, 0))
    table = pl.BlockSpec((1,) + row_high.shape[1:], lambda i, w: (w[0], 0, 0))
    return pl.pallas_call(
        finish_kernel,
        grid_spec=pltpu.PrefetchScalarGridSpec(
            num_scalar_prefetch=1,
            grid=(dates // g,),
            in_specs=[block, block, halo, halo, table, table],
            out_specs=[block, block],
        ),
        out_shape=(jax.ShapeDtypeStruct((dates, rows, cols), F32),) * 2,
        compiler_params=pltpu.CompilerParams(vmem_limit_bytes=40 << 20),
        name="finish",
    )(where, series, smooth, up, dn, row_high, row_low)


def neighbours(low_part, high_part, axis):
    count = lax.axis_size(axis)
    forward = [(i, i + 1) for i in range(count - 1)]
    backward = [(b, a) for a, b in forward]
    return lax.ppermute(high_part, axis, forward), lax.ppermute(low_part, axis, backward)


def on_device(ifg_real, ifg_imag, date_pairs):
    n, rows, cols = ifg_real.shape
    rows_c, rows_e, fwd, inv, back_c, back_e = (jnp.asarray(t) for t in tables())
    col_t, row_t = blur_tables(rows * lax.axis_size("row"), rows, cols)
    col_high, col_low = bf16(col_t), bf16(col_t - bf16(col_t).astype(np.float32))
    row_high, row_low = bf16(row_t), bf16(row_t - bf16(row_t).astype(np.float32))

    up_re, dn_re = neighbours(ifg_real[:, :HALF], ifg_real[:, rows - HALF :], "row")
    up_im, dn_im = neighbours(ifg_imag[:, :HALF], ifg_imag[:, rows - HALF :], "row")
    u = centre(ifg_real, ifg_imag, rows_c, fwd, inv)
    p, g = projection(date_pairs)
    q = edges(ifg_real, ifg_imag, (up_re, up_im, dn_re, dn_im), u, rows_e, fwd, inv, back_c, back_e)
    sines = lax.all_to_all(q, "ifg", split_axis=0, concat_axis=0, tiled=True)
    series = invert(sines.reshape(-1, 2 * cols), p, g)
    devices = lax.axis_size("ifg")
    series = lax.all_to_all(
        series.reshape(devices, -1, LANES), "ifg", split_axis=0, concat_axis=0, tiled=True
    )
    series, smooth = gather(
        series.reshape(-1, LANES), jnp.asarray(col_high), jnp.asarray(col_low), rows, cols
    )
    up, dn = neighbours(smooth[:, :RADIUS], smooth[:, rows - RADIUS :], "row")
    where = lax.axis_index("row").astype(jnp.int32).reshape(1)
    return finish(where, series, smooth, up, dn, jnp.asarray(row_high), jnp.asarray(row_low))


def solution(mesh):
    placed = (P("ifg", "row", None), P("ifg", "row", None), P())
    return jax.shard_map(
        on_device,
        mesh=mesh,
        in_specs=placed,
        out_specs=(P("ifg", "row", None), P("ifg", "row", None)),
        check_vma=False,
    )
```

time: 1250 us -> 184 us (0.15); the launches traced: 1240 us -> 184 us
  local copies, waits for them, and re-layouts: 539 us -> 9.17 us
  matrix products: 266 us -> 0 us
  other arithmetic: 262 us -> 0 us
  Pallas kernels: 0 us -> 93.5 us
  waiting for transfers between devices: 119 us -> 28.1 us
  blocking collectives: 0 us -> 25.3 us
    dot_general x360 -> x0, matrix products: 252 us -> none  [the longest x64 71.1 us: filter_block(): jnp.einsum('anbcl,lm->anbcm', stacked, forward, preferred_element_type=jn...]
    another operation x139 -> x0, local copies, waits for them, and re-layouts: 163 us -> none  [the longest x128 159 us: filter_block(): pieces = jnp.stack([weighted[..., :PATCH], weighted[..., PATCH:]], axis=1)]
    slice x244 -> x3, local copies, waits for them, and re-layouts: 125 us -> 3.06 us  [the longest x1 1.94 us: on_device(): ifg_real[:, :HALF]]
    another operation x36 -> x0, other arithmetic: 96.6 us -> none  [the longest x10 50.7 us: projection(): cholesky_factor = jnp.linalg.cholesky(gram)]
    pallas_call x0 -> x6, Pallas kernels: none -> 93.5 us  [the longest x1 35.1 us: edges(): pl.pallas_call(edges_kernel, grid=(n // g,), in_specs=[block, block, halo...]
    ppermute x6, waiting for transfers between devices: 72 us -> 5.6 us  [the longest x3 4.3 us: neighbours(): lax.ppermute(low_part, axis, backward)]
    while x256 -> x0, local copies, waits for them, and re-layouts: 59.7 us -> none
    broadcast_in_dim x17 -> x0, other arithmetic: 44.3 us -> none  [on_device(): lax.map(run_block, block_list)]
  transfers between devices with their start and end apart: 9 -> 7, of which waited for: 6 -> 3; matrix products, arithmetic and copies ran while one was open for 11% -> 1% of each run, Pallas kernels for 0% -> 20%
where the time goes in v1:
time: 184 us
  Pallas kernels  93.5 us (51%)
  waiting for transfers between devices  28.1 us (15%)
  starting transfers between devices  26.7 us (15%)
  blocking collectives  25.3 us (14%)
  local copies, waits for them, and re-layouts  9.17 us (5%)
    pallas_call x1, Pallas kernels, edges(): pl.pallas_call(edges_kernel, grid=(n // g,), in_specs=[block, block, halo...  35.1 us
    pallas_call x1, Pallas kernels, centre(): pl.pallas_call(centre_kernel, grid=(n // g,), in_specs=[block, block, who...  27.9 us
    all_to_all x1, blocking collectives, on_device(): lax.all_to_all(series.reshape(devices, -1, LANES), 'ifg', split_axis=0, c...  25.3 us
    all_to_all x1, waiting for transfers between devices, on_device(): sines = lax.all_to_all(q, 'ifg', split_axis=0, concat_axis=0, tiled=True)  22.5 us
    pallas_call x1, Pallas kernels, invert(): pl.pallas_call(invert_kernel, grid=(pixels // width,), in_specs=[pl.Block...  17.6 us
    all_to_all x1, starting transfers between devices, on_device(): sines = lax.all_to_all(q, 'ifg', split_axis=0, concat_axis=0, tiled=True)  10.2 us
    ppermute x3, starting transfers between devices, neighbours(): lax.ppermute(high_part, axis, forward)  9.03 us
    pallas_call x1, Pallas kernels, projection(): pl.pallas_call(projection_kernel, out_shape=(jax.ShapeDtypeStruct((2 * ND...  8.25 us
  transfers between devices with their start and end apart: 7, of which 3 were waited for; matrix products, arithmetic and copies ran while one was open for 1% of the time, Pallas kernels for 20%

profile of v1, /device:TPU:1, one launch (start us, length us, event | category | flops | bytes accessed | tf_op | source)
XLA Modules:
  0.0 183.7 jit_solution(7791994126018262099)
XLA Ops:
  0.6 1.9 %fusion.1 = (bf16[32,32,512]{2,1,0:T(8,128)(2,1)S(1)}, bf16[32,32,512]{2,1,0:T(8,128)(2,1)S(1)}) fusion(bf16[32,64,512]{2,1,0:T(8,128)(2,1)} %re_ref.3), kind=kLoop, calls=%fused_computation.1 | loop fusion | bytes 4194304 | tf_op jit(solution)/shard_map/slice | solution.py:441
  2.6 5.2 %collective-permute-start = (bf16[32,32,512]{2,1,0:T(8,128)(2,1)S(1)}, bf16[32,32,512]{2,1,0:T(8,128)(2,1)S(1)}, u32[]{:S(2)}, u32[]{:S(2)}) collective-permute-start(bf16[32,32,512]{2,1,0:T(8,128)(2,1)S(1)} %get-tuple-element.13), channel_id=1, source_target_pairs={{0,1},{1,2},{2,3},{4,5},{5,6},{6,7},{8,9},{9,10},{10,11},{12,13},{... | collective-permute-start | bytes 3145736 | tf_op jit(solution)/shard_map/ppermute | solution.py:431
  8.1 1.9 %collective-permute-start.1 = (bf16[32,32,512]{2,1,0:T(8,128)(2,1)S(1)}, bf16[32,32,512]{2,1,0:T(8,128)(2,1)S(1)}, u32[]{:S(2)}, u32[]{:S(2)}) collective-permute-start(bf16[32,32,512]{2,1,0:T(8,128)(2,1)S(1)} %get-tuple-element.11), channel_id=1, source_target_pairs={{0,1},{1,2},{2,3},{4,5},{5,6},{6,7},{8,9},{9,10},{10,11},{12,13},{... | collective-permute-start | bytes 3145736 | tf_op jit(solution)/shard_map/ppermute | solution.py:431
  10.0 2.5 %collective-permute-start.2 = (bf16[32,32,512]{2,1,0:T(8,128)(2,1)S(1)}, bf16[32,32,512]{2,1,0:T(8,128)(2,1)S(1)}, u32[]{:S(2)}, u32[]{:S(2)}) collective-permute-start(bf16[32,32,512]{2,1,0:T(8,128)(2,1)S(1)} %get-tuple-element.12), channel_id=1, source_target_pairs={{1,0},{2,1},{3,2},{5,4},{6,5},{7,6},{9,8},{10,9},{11,10},{13,12},{... | collective-permute-start | bytes 3145736 | tf_op jit(solution)/shard_map/ppermute | solution.py:431
  12.5 2.1 %collective-permute-start.3 = (bf16[32,32,512]{2,1,0:T(8,128)(2,1)S(1)}, bf16[32,32,512]{2,1,0:T(8,128)(2,1)S(1)}, u32[]{:S(2)}, u32[]{:S(2)}) collective-permute-start(bf16[32,32,512]{2,1,0:T(8,128)(2,1)S(1)} %get-tuple-element.10), channel_id=1, source_target_pairs={{1,0},{2,1},{3,2},{5,4},{6,5},{7,6},{9,8},{10,9},{11,10},{13,12},{... | collective-permute-start | bytes 3145736 | tf_op jit(solution)/shard_map/ppermute | solution.py:431
  14.6 27.9 %centre.1.u_ref = bf16[32,128,512]{2,1,0:T(8,128)(2,1)S(1)} custom-call(bf16[32,64,512]{2,1,0:T(8,128)(2,1)S(1)} %copy-done, bf16[32,64,512]{2,1,0:T(8,128)(2,1)S(1)} %copy-done.1, bf16[128,128]{1,0:T(8,128)(2,1)S(1)} %copy-done.15, bf16[3,256,256]{2,1,0:T(8,128)(2,1)S(1)} %copy-done.10, bf16[3,256,256]{2,1,0:T(8,128)(2,1)S(1)} %copy-done.11), custom_call_target="tpu_custom_call" | custom-call | flops 6979321856 | bytes 8388608 | tf_op jit(solution)/shard_map/centre/pallas_call | solution.py:140
  42.5 1.9 %copy-done.16 = bf16[32,128,512]{2,1,0:T(8,128)(2,1)} copy-done((bf16[32,128,512]{2,1,0:T(8,128)(2,1)}, bf16[32,128,512]{2,1,0:T(8,128)(2,1)S(1)}, u32[]{:S(2)}) %copy-start.16) | copy-done | bytes 4194328
  44.5 35.1 %edges.1 = bf16[32,32,1024]{2,1,0:T(8,128)(2,1)} custom-call(bf16[32,64,512]{2,1,0:T(8,128)(2,1)} %re_ref.3, bf16[32,64,512]{2,1,0:T(8,128)(2,1)} %im_ref.3, bf16[32,32,512]{2,1,0:T(8,128)(2,1)S(1)} %collective-permute-done.up_re, bf16[32,32,512]{2,1,0:T(8,128)(2,1)S(1)} %collective-permute-done.1.up_im, ...), custom_call_target="tpu_custom_call" | custom-call | flops 16106127360 | bytes 14680064 | tf_op jit(solution)/shard_map/edges/pallas_call | solution.py:194
  79.6 10.2 %all-to-all-start = ((bf16[32,32,1024]{2,1,0:T(8,128)(2,1)}), bf16[32,32,1024]{2,1,0:T(8,128)(2,1)S(1)}, u32[]{:S(2)}, u32[]{:S(2)}) async-start(bf16[32,32,1024]{2,1,0:T(8,128)(2,1)} %edges.1), calls=%async_computation | async-start | bytes 4194304 | tf_op jit(solution)/shard_map/all_to_all | solution.py:446
  89.8 1.0 copy.15.pairs_ref
  90.8 1.0 copy-done.4
  91.9 8.3 %projection.1 = (bf16[640,1024]{1,0:T(8,128)(2,1)S(1)}, bf16[1024,384]{1,0:T(8,128)(2,1)S(1)}) custom-call(s32[1024,2]{1,0:T(8,128)S(1)} %copy-done.4, s32[2,1024]{1,0:T(2,128)S(1)} %bitcast.8), custom_call_target="tpu_custom_call" | custom-call | flops 20000000000 | bytes 4000000 | tf_op jit(solution)/shard_map/projection/pallas_call | solution.py:295
  100.1 0.9 copy-done.2
  101.0 22.5 %all-to-all-done = bf16[32,32,1024]{2,1,0:T(8,128)(2,1)S(1)} async-done(((bf16[32,32,1024]{2,1,0:T(8,128)(2,1)}), bf16[32,32,1024]{2,1,0:T(8,128)(2,1)S(1)}, u32[]{:S(2)}, u32[]{:S(2)}) %all-to-all-start) | async-done | bytes 2097184 | tf_op jit(solution)/shard_map/all_to_all | solution.py:446
  123.5 1.1 copy-done.3
  124.6 17.6 %invert.1 = f32[2560,128]{1,0:T(8,128)S(1)} custom-call(bf16[1024,1024]{1,0:T(8,128)(2,1)S(1)} %bitcast.5, bf16[640,1024]{1,0:T(8,128)(2,1)S(1)} %get-tuple-element.6.p_ref, bf16[1024,384]{1,0:T(8,128)(2,1)S(1)} %copy-done.3), custom_call_target="tpu_custom_call" | custom-call | tf_op jit(solution)/shard_map/invert/pallas_call | solution.py:343
  142.3 25.3 %all_to_all.10 = f32[32,80,128]{2,1,0:T(8,128)S(1)} all-to-all(f32[32,80,128]{2,1,0:T(8,128)S(1)} %bitcast.7), channel_id=1, replica_groups=mesh['ifg'=32,'row'=4] {'ifg'}, dimensions={0} | all-to-all | bytes 2621440 | tf_op jit(solution)/shard_map/all_to_all | solution.py:449
  167.5 2.8 %gather.1 = (f32[10,64,512]{2,1,0:T(8,128)S(1)}, f32[10,64,512]{2,1,0:T(8,128)S(1)}) custom-call(f32[2560,128]{1,0:T(8,128)S(1)} %bitcast.6, bf16[512,512]{1,0:T(8,128)(2,1)S(1)} %copy-done.5, bf16[512,512]{1,0:T(8,128)(2,1)S(1)} %copy-done.6), custom_call_target="tpu_custom_call" | custom-call | tf_op jit(solution)/shard_map/gather/pallas_call | solution.py:390
  170.3 0.9 fusion.2
  171.2 1.9 %collective-permute-start.4 = (f32[10,16,512]{2,1,0:T(8,128)}, f32[10,16,512]{2,1,0:T(8,128)S(1)}, u32[]{:S(2)}, u32[]{:S(2)}) collective-permute-start(f32[10,16,512]{2,1,0:T(8,128)} %get-tuple-element.15), channel_id=1, source_target_pairs={{0,1},{1,2},{2,3},{4,5},{5,6},{6,7},{8,9},{9,10},{10,11},{12,13},{... | collective-permute-start | bytes 983048 | tf_op jit(solution)/shard_map/ppermute | solution.py:431
  173.1 3.0 %collective-permute-start.5 = (f32[10,16,512]{2,1,0:T(8,128)}, f32[10,16,512]{2,1,0:T(8,128)S(1)}, u32[]{:S(2)}, u32[]{:S(2)}) collective-permute-start(f32[10,16,512]{2,1,0:T(8,128)} %get-tuple-element.14), channel_id=1, source_target_pairs={{1,0},{2,1},{3,2},{5,4},{6,5},{7,6},{9,8},{10,9},{11,10},{13,12},{... | collective-permute-start | bytes 983048 | tf_op jit(solution)/shard_map/ppermute | solution.py:431
  176.2 1.3 collective-permute-done.4.up_ref
  177.4 4.3 %collective-permute-done.5.dn_ref = f32[10,16,512]{2,1,0:T(8,128)S(1)} collective-permute-done((f32[10,16,512]{2,1,0:T(8,128)}, f32[10,16,512]{2,1,0:T(8,128)S(1)}, u32[]{:S(2)}, u32[]{:S(2)}) %collective-permute-start.5) | collective-permute-done | bytes 327712 | tf_op jit(solution)/shard_map/ppermute | solution.py:431
  181.7 1.9 %finish.1 = (f32[10,64,512]{2,1,0:T(8,128)}, f32[10,64,512]{2,1,0:T(8,128)}) custom-call(s32[1]{0:T(128)} %bitcast.where_ref, f32[10,64,512]{2,1,0:T(8,128)S(1)} %get-tuple-element.8.series_ref, f32[10,64,512]{2,1,0:T(8,128)S(1)} %get-tuple-element.9.smooth_ref, f32[10,16,512]{2,1,0:T(8,128)S(1)} %collective-permute-done.4.up_ref, ...), custom_call_target="tpu_custom_call" | custom-call | tf_op jit(solution)/shard_map/finish/pallas_call | solution.py:413
  (35 shorter events, 0.3 us)
Async XLA Ops:
  0.6 7.2 %copy-start.1 = (bf16[32,64,512]{2,1,0:T(8,128)(2,1)S(1)}, bf16[32,64,512]{2,1,0:T(8,128)(2,1)}, u32[]{:S(2)}) copy-start(bf16[32,64,512]{2,1,0:T(8,128)(2,1)} %im_ref.3) | copy-start | bytes 6291460
  2.6 12.0 %copy-start = (bf16[32,64,512]{2,1,0:T(8,128)(2,1)S(1)}, bf16[32,64,512]{2,1,0:T(8,128)(2,1)}, u32[]{:S(2)}) copy-start(bf16[32,64,512]{2,1,0:T(8,128)(2,1)} %re_ref.3) | copy-start | bytes 6291460
  2.6 12.0 %copy-start.10 = (bf16[3,256,256]{2,1,0:T(8,128)(2,1)S(1)}, bf16[3,256,256]{2,1,0:T(8,128)(2,1)}, u32[]{:S(2)}) copy-start(bf16[3,256,256]{2,1,0:T(8,128)(2,1)} %constant.26.clone.fwd_ref) | copy-start | bytes 1179652
  2.6 12.0 %copy-start.11 = (bf16[3,256,256]{2,1,0:T(8,128)(2,1)S(1)}, bf16[3,256,256]{2,1,0:T(8,128)(2,1)}, u32[]{:S(2)}) copy-start(bf16[3,256,256]{2,1,0:T(8,128)(2,1)} %constant.27.clone.inv_ref) | copy-start | bytes 1179652
  2.6 12.0 %copy-start.15 = (bf16[128,128]{1,0:T(8,128)(2,1)S(1)}, bf16[128,128]{1,0:T(8,128)(2,1)}, u32[]{:S(2)}) copy-start(bf16[128,128]{1,0:T(8,128)(2,1)} %constant.24.clone.rows_ref) | copy-start | bytes 98308
  2.6 41.8 %collective-permute-start = (bf16[32,32,512]{2,1,0:T(8,128)(2,1)S(1)}, bf16[32,32,512]{2,1,0:T(8,128)(2,1)S(1)}, u32[]{:S(2)}, u32[]{:S(2)}) collective-permute-start(bf16[32,32,512]{2,1,0:T(8,128)(2,1)S(1)} %get-tuple-element.13), channel_id=1, source_target_pairs={{0,1},{1,2},{2,3},{4,5},{5,6},{6,7},{8,9},{9,10},{10,11},{12,13},{... | collective-permute-start | bytes 3145736 | tf_op jit(solution)/shard_map/ppermute | solution.py:431
  8.1 36.4 %collective-permute-start.1 = (bf16[32,32,512]{2,1,0:T(8,128)(2,1)S(1)}, bf16[32,32,512]{2,1,0:T(8,128)(2,1)S(1)}, u32[]{:S(2)}, u32[]{:S(2)}) collective-permute-start(bf16[32,32,512]{2,1,0:T(8,128)(2,1)S(1)} %get-tuple-element.11), channel_id=1, source_target_pairs={{0,1},{1,2},{2,3},{4,5},{5,6},{6,7},{8,9},{9,10},{10,11},{12,13},{... | collective-permute-start | bytes 3145736 | tf_op jit(solution)/shard_map/ppermute | solution.py:431
  10.0 34.5 %collective-permute-start.2 = (bf16[32,32,512]{2,1,0:T(8,128)(2,1)S(1)}, bf16[32,32,512]{2,1,0:T(8,128)(2,1)S(1)}, u32[]{:S(2)}, u32[]{:S(2)}) collective-permute-start(bf16[32,32,512]{2,1,0:T(8,128)(2,1)S(1)} %get-tuple-element.12), channel_id=1, source_target_pairs={{1,0},{2,1},{3,2},{5,4},{6,5},{7,6},{9,8},{10,9},{11,10},{13,12},{... | collective-permute-start | bytes 3145736 | tf_op jit(solution)/shard_map/ppermute | solution.py:431
  12.5 32.0 %copy-start.12 = (bf16[256,256]{1,0:T(8,128)(2,1)S(1)}, bf16[256,256]{1,0:T(8,128)(2,1)}, u32[]{:S(2)}) copy-start(bf16[256,256]{1,0:T(8,128)(2,1)} %constant.25.clone.rows_ref) | copy-start | bytes 393220
  12.5 32.0 %copy-start.13 = (bf16[128,256]{1,0:T(8,128)(2,1)S(1)}, bf16[128,256]{1,0:T(8,128)(2,1)}, u32[]{:S(2)}) copy-start(bf16[128,256]{1,0:T(8,128)(2,1)} %constant.29.clone.be_ref) | copy-start | bytes 196612
  12.5 32.0 %copy-start.14 = (bf16[128,128]{1,0:T(8,128)(2,1)S(1)}, bf16[128,128]{1,0:T(8,128)(2,1)}, u32[]{:S(2)}) copy-start(bf16[128,128]{1,0:T(8,128)(2,1)} %constant.28.clone.bc_ref) | copy-start | bytes 98308
  12.5 31.9 %collective-permute-start.3 = (bf16[32,32,512]{2,1,0:T(8,128)(2,1)S(1)}, bf16[32,32,512]{2,1,0:T(8,128)(2,1)S(1)}, u32[]{:S(2)}, u32[]{:S(2)}) collective-permute-start(bf16[32,32,512]{2,1,0:T(8,128)(2,1)S(1)} %get-tuple-element.10), channel_id=1, source_target_pairs={{1,0},{2,1},{3,2},{5,4},{6,5},{7,6},{9,8},{10,9},{11,10},{13,12},{... | collective-permute-start | bytes 3145736 | tf_op jit(solution)/shard_map/ppermute | solution.py:431
  42.5 2.0 %copy-start.16 = (bf16[32,128,512]{2,1,0:T(8,128)(2,1)}, bf16[32,128,512]{2,1,0:T(8,128)(2,1)S(1)}, u32[]{:S(2)}) copy-start(bf16[32,128,512]{2,1,0:T(8,128)(2,1)S(1)} %centre.1.u_ref) | copy-start | bytes 12582916
  79.6 10.2 %copy-start.9 = (s32[1024,2]{0,1:T(2,128)S(1)}, s32[1024,2]{0,1:T(2,128)}, u32[]{:S(2)}) copy-start(s32[1024,2]{0,1:T(2,128)} %param.15) | copy-start | bytes 24580
  79.6 43.9 %all-to-all-start = ((bf16[32,32,1024]{2,1,0:T(8,128)(2,1)}), bf16[32,32,1024]{2,1,0:T(8,128)(2,1)S(1)}, u32[]{:S(2)}, u32[]{:S(2)}) async-start(bf16[32,32,1024]{2,1,0:T(8,128)(2,1)} %edges.1), calls=%async_computation | async-start | bytes 4194304 | tf_op jit(solution)/shard_map/all_to_all | solution.py:446
  90.8 1.0 copy-start.4
  100.1 0.9 copy-start.2
  123.5 1.1 copy-start.3
  142.2 25.3 %copy-start.5 = (bf16[512,512]{1,0:T(8,128)(2,1)S(1)}, bf16[512,512]{1,0:T(8,128)(2,1)}, u32[]{:S(2)}) copy-start(bf16[512,512]{1,0:T(8,128)(2,1)} %constant.30.clone.ch_ref) | copy-start | bytes 1572868
  142.2 25.3 %copy-start.6 = (bf16[512,512]{1,0:T(8,128)(2,1)S(1)}, bf16[512,512]{1,0:T(8,128)(2,1)}, u32[]{:S(2)}) copy-start(bf16[512,512]{1,0:T(8,128)(2,1)} %constant.31.clone.cl_ref) | copy-start | bytes 1572868
  167.5 14.2 %copy-start.7 = (bf16[4,64,96]{2,1,0:T(8,128)(2,1)S(1)}, bf16[4,64,96]{2,1,0:T(8,128)(2,1)}, u32[]{:S(2)}) copy-start(bf16[4,64,96]{2,1,0:T(8,128)(2,1)} %constant.32.clone.rh_ref) | copy-start | bytes 147460
  167.5 14.2 %copy-start.8 = (bf16[4,64,96]{2,1,0:T(8,128)(2,1)S(1)}, bf16[4,64,96]{2,1,0:T(8,128)(2,1)}, u32[]{:S(2)}) copy-start(bf16[4,64,96]{2,1,0:T(8,128)(2,1)} %constant.33.clone.rl_ref) | copy-start | bytes 147460
  171.2 6.2 %collective-permute-start.4 = (f32[10,16,512]{2,1,0:T(8,128)}, f32[10,16,512]{2,1,0:T(8,128)S(1)}, u32[]{:S(2)}, u32[]{:S(2)}) collective-permute-start(f32[10,16,512]{2,1,0:T(8,128)} %get-tuple-element.15), channel_id=1, source_target_pairs={{0,1},{1,2},{2,3},{4,5},{5,6},{6,7},{8,9},{9,10},{10,11},{12,13},{... | collective-permute-start | bytes 983048 | tf_op jit(solution)/shard_map/ppermute | solution.py:431
  173.1 8.6 %collective-permute-start.5 = (f32[10,16,512]{2,1,0:T(8,128)}, f32[10,16,512]{2,1,0:T(8,128)S(1)}, u32[]{:S(2)}, u32[]{:S(2)}) collective-permute-start(f32[10,16,512]{2,1,0:T(8,128)} %get-tuple-element.14), channel_id=1, source_target_pairs={{1,0},{2,1},{3,2},{5,4},{6,5},{7,6},{9,8},{10,9},{11,10},{13,12},{... | collective-permute-start | bytes 983048 | tf_op jit(solution)/shard_map/ppermute | solution.py:431

commit v2 on v1

--- a/solution.py
+++ b/solution.py
@@ -36,12 +36,7 @@
     two = np.eye(2)
     zero = np.zeros((PATCH, PATCH))
 
-    rows_centre = np.block([[c, s], [-s, c]])
-    up = np.concatenate([np.eye(PATCH), zero], 1)
-    low = np.concatenate([zero, np.eye(PATCH)], 1)
-    rows_edge = np.block(
-        [[c @ up, s @ up], [c @ low, s @ low], [-s @ up, c @ up], [-s @ low, c @ low]]
-    )
+    rows_strip = np.block([[c, s], [-s, c]])
     c2, s2 = np.kron(two, c), np.kron(two, s)
     cols = np.block([[c2, -s2], [s2, c2]])
     shift = np.zeros((2, LANES, LANES))
@@ -56,15 +51,11 @@
     forward = np.stack([cols, left @ cols, right @ cols])
     inverse = np.stack([inv, inv @ left.T, inv @ right.T])
     ct, st = c * taper[:, None], s * taper[:, None]
-    top = np.concatenate([ct[HALF:], np.zeros((HALF, PATCH))], 0)
-    top_s = np.concatenate([st[HALF:], np.zeros((HALF, PATCH))], 0)
-    bot = np.concatenate([np.zeros((HALF, PATCH)), ct[:HALF]], 0)
-    bot_s = np.concatenate([np.zeros((HALF, PATCH)), st[:HALF]], 0)
-    back_centre = np.block([[ct, -st], [st, ct]])
-    back_edge = np.block([[top, bot, -top_s, -bot_s], [top_s, bot_s, top, bot]])
-    return tuple(
-        bf16(x) for x in (rows_centre, rows_edge, forward, inverse, back_centre, back_edge)
-    )
+    back = []
+    for centre_rows, edge_rows in ((slice(0, HALF), slice(HALF, PATCH)), (slice(HALF, PATCH), slice(0, HALF))):
+        c1, s1, c2, s2 = ct[centre_rows], st[centre_rows], ct[edge_rows], st[edge_rows]
+        back.append(np.block([[c1, -s1, c2, -s2], [s1, c1, s2, c2]]))
+    return tuple(bf16(x) for x in (rows_strip, forward, inverse, *back))
 
 
 def gauss(distance):
@@ -123,99 +114,118 @@
     return jnp.concatenate(out_re, axis=1), jnp.concatenate(out_im, axis=1)
 
 
+def stacked_rows(table, strips):
+    y = [mm(table, x).astype(BF16) for x in strips]
+    y_re = jnp.concatenate([t[:PATCH] for t in y], axis=0)
+    y_im = jnp.concatenate([t[PATCH:] for t in y], axis=0)
+    return y_re, y_im
+
+
 def centre_kernel(re_ref, im_ref, rows_ref, fwd_ref, inv_ref, u_ref):
-    table = rows_ref[...]
-    for i in range(re_ref.shape[0]):
-        x = jnp.concatenate([re_ref[i], im_ref[i]], axis=0)
-        y = mm(table, x).astype(BF16)
-        u_re, u_im = spectral(y[:PATCH], y[PATCH:], fwd_ref, inv_ref)
-        u_ref[i] = jnp.concatenate([u_re, u_im], axis=0)
+    n = re_ref.shape[0]
+    strips = [jnp.concatenate([re_ref[i], im_ref[i]], axis=0) for i in range(n)]
+    y_re, y_im = stacked_rows(rows_ref[...], strips)
+    u_re, u_im = spectral(y_re, y_im, fwd_ref, inv_ref)
+    for i in range(n):
+        sl = slice(i * PATCH, (i + 1) * PATCH)
+        u_ref[i, :PATCH] = u_re[sl]
+        u_ref[i, PATCH:] = u_im[sl]
+
+
+BATCH = 4
+
+
+def in_hbm(x):
+    return pltpu.with_memory_space_constraint(x, pltpu.HBM)
+
+
+def whole(a):
+    return pl.BlockSpec(a.shape, lambda i: (0,) * a.ndim)
 
 
 def centre(re, im, rows_t, fwd, inv):
     n, rows, cols = re.shape
-    g = 2
-    whole = lambda a: pl.BlockSpec(a.shape, lambda i: (0,) * a.ndim)
+    g = BATCH
     block = pl.BlockSpec((g, rows, cols), lambda i: (i, 0, 0))
     return pl.pallas_call(
         centre_kernel,
         grid=(n // g,),
         in_specs=[block, block, whole(rows_t), whole(fwd), whole(inv)],
         out_specs=pl.BlockSpec((g, 2 * rows, cols), lambda i: (i, 0, 0)),
-        out_shape=jax.ShapeDtypeStruct((n, 2 * rows, cols), BF16),
-        compiler_params=pltpu.CompilerParams(vmem_limit_bytes=40 << 20),
+        out_shape=pltpu.HBM((n, 2 * rows, cols), BF16),
+        compiler_params=pltpu.CompilerParams(vmem_limit_bytes=24 << 20),
         cost_estimate=pl.CostEstimate(
             flops=n * 2 * 64 * 256 * 256 * 26, bytes_accessed=n * rows * cols * 8,
             transcendentals=n * 64 * 2304,
         ),
         name="centre",
-    )(re, im, rows_t, fwd, inv)
+    )(in_hbm(re), in_hbm(im), rows_t, fwd, inv)
 
 
 GROUP = 16
 
 
-def edges_kernel(
-    re_ref, im_ref, up_re, up_im, dn_re, dn_im, u_ref,
-    rows_ref, fwd_ref, inv_ref, bc_ref, be_ref, q_ref, keep
-):
+def edge_kernel(upper, re_ref, im_ref, halo_ref, u_ref, rows_ref, fwd_ref, inv_ref, back_ref, q_ref, keep):
     g = re_ref.shape[0]
-    half = pl.program_id(0) % (GROUP // g)
+    part = pl.program_id(0) % (GROUP // g)
+    strips = []
     for i in range(g):
-        x = jnp.concatenate(
-            [up_re[i], re_ref[i], dn_re[i], up_im[i], im_ref[i], dn_im[i]], axis=0
-        )
-        y = mm(rows_ref[...], x).astype(BF16)
-        u_re, u_im = spectral(y[: 2 * PATCH], y[2 * PATCH :], fwd_ref, inv_ref)
-        f = mm(be_ref[...], jnp.concatenate([u_re, u_im], axis=0)) + mm(bc_ref[...], u_ref[i])
-        re, im = f[:PATCH], f[PATCH:]
+        own = [re_ref[i], im_ref[i]]
+        other = [halo_ref[0, i], halo_ref[1, i]]
+        first, second = (other, own) if upper else (own, other)
+        strips.append(jnp.concatenate([first[0], second[0], first[1], second[1]], axis=0))
+    y_re, y_im = stacked_rows(rows_ref[...], strips)
+    u_re, u_im = spectral(y_re, y_im, fwd_ref, inv_ref)
+    for i in range(g):
+        sl = slice(i * PATCH, (i + 1) * PATCH)
+        f = mm(back_ref[...], jnp.concatenate([u_ref[i], u_re[sl], u_im[sl]], axis=0))
+        re, im = f[:HALF], f[HALF:]
         q = im * lax.rsqrt(re * re + im * im + 1.0)
-        slot = half * g + i
-        tiles = q.shape[1] // LANES
-        for h in range(2):
-            for c in range(tiles):
-                keep[h * tiles + c, pl.ds(slot, HALF, stride=GROUP), :] = q[
-                    h * HALF : (h + 1) * HALF, c * LANES : (c + 1) * LANES
-                ]
-
-    @pl.when(half == GROUP // g - 1)
+        for c in range(keep.shape[0]):
+            keep[c, pl.ds(part * g + i, HALF, stride=GROUP), :] = q[:, c * LANES : (c + 1) * LANES]
+
+    @pl.when(part == GROUP // g - 1)
     def _():
         for t in range(keep.shape[0]):
             block = keep[t].astype(BF16)
             q_ref[:, :, t * LANES : (t + 1) * LANES] = block.reshape(HALF, GROUP, LANES)
 
 
-def edges(re, im, halos, u, rows_t, fwd, inv, bc, be):
+def edge(upper, re, im, halo, u, rows_t, fwd, inv, back):
     n, rows, cols = re.shape
-    g = 2
-    whole = lambda a: pl.BlockSpec(a.shape, lambda i: (0,) * a.ndim)
-    block = pl.BlockSpec((g, rows, cols), lambda i: (i, 0, 0))
-    halo = pl.BlockSpec((g, HALF, cols), lambda i: (i, 0, 0))
+    g = BATCH
+    side = 0 if upper else 1
+    block = pl.BlockSpec((g, HALF, cols), lambda i: (i, side, 0))
     return pl.pallas_call(
-        edges_kernel,
+        lambda *refs: edge_kernel(upper, *refs),
         grid=(n // g,),
-        in_specs=[block, block, halo, halo, halo, halo,
+        in_specs=[block, block,
+                  pl.BlockSpec((2, g, HALF, cols), lambda i: (0, i, 0, 0)),
                   pl.BlockSpec((g, 2 * rows, cols), lambda i: (i, 0, 0)),
-                  whole(rows_t), whole(fwd), whole(inv), whole(bc), whole(be)],
-        out_specs=pl.BlockSpec((HALF, GROUP, 2 * cols), lambda i: (0, i // (GROUP // g), 0)),
-        out_shape=jax.ShapeDtypeStruct((HALF, n, 2 * cols), BF16),
-        scratch_shapes=[pltpu.VMEM((2 * cols // LANES, HALF * GROUP, LANES), F32)],
-        compiler_params=pltpu.CompilerParams(vmem_limit_bytes=48 << 20),
+                  whole(rows_t), whole(fwd), whole(inv), whole(back)],
+        out_specs=pl.BlockSpec((HALF, GROUP, cols), lambda i: (0, i // (GROUP // g), 0)),
+        out_shape=pltpu.HBM((HALF, n, cols), BF16),
+        scratch_shapes=[pltpu.VMEM((cols // LANES, HALF * GROUP, LANES), F32)],
+        compiler_params=pltpu.CompilerParams(vmem_limit_bytes=24 << 20),
         cost_estimate=pl.CostEstimate(
-            flops=n * 2 * 64 * 256 * 256 * 60, bytes_accessed=n * rows * cols * 14,
-            transcendentals=n * 128 * 2304,
+            flops=n * 2 * 64 * 256 * 256 * 30, bytes_accessed=n * rows * cols * 7,
+            transcendentals=n * 64 * 2304,
         ),
-        name="edges",
-    )(re, im, *halos, u, rows_t, fwd, inv, bc, be)
+        name="upper" if upper else "lower",
+    )(in_hbm(re), in_hbm(im), halo, in_hbm(u), rows_t, fwd, inv, back)
 
 
 def projection_kernel(pairs_ref, pairs_t_ref, p_ref, g_ref, band, factor, solved):
     nifg = pairs_ref.shape[0]
     first, second = pairs_ref[:, 0:1], pairs_ref[:, 1:2]
-    dates = lax.broadcasted_iota(jnp.int32, (nifg, DATE_PAD), 1)
-    one = jnp.ones((nifg, DATE_PAD), F32)
-    design = jnp.where(dates == second, one, 0.0) - jnp.where(dates == first, one, 0.0)
-    g_ref[...] = design.astype(BF16)
+    def design(width, wrap):
+        dates = lax.broadcasted_iota(jnp.int32, (nifg, width), 1)
+        if wrap:
+            dates = jnp.where(dates >= NDATES, dates - NDATES, dates)
+        return (jnp.where(dates == second, 1.0, 0.0) - jnp.where(dates == first, 1.0, 0.0)).astype(BF16)
+
+    g_ref[...] = design(2 * NDATES, True)
+    single = design(DATE_PAD, False)
 
     row_date = lax.broadcasted_iota(jnp.int32, (NDATES, nifg), 0)
     is_first = row_date == pairs_t_ref[0:1, :]
@@ -282,11 +292,10 @@
         part = rest.astype(BF16)
         rest = rest - part.astype(F32)
         total = total + lax.dot_general(
-            part, g_ref[...], (((1,), (1,)), ((), ())), preferred_element_type=F32
+            part, single, (((1,), (1,)), ((), ())), preferred_element_type=F32
         )
     high = total.astype(BF16)
-    p_ref[0:NDATES, :] = high
-    p_ref[NDATES:, :] = (total - high.astype(F32)).astype(BF16)
+    p_ref[...] = high
 
 
 def projection(date_pairs):
@@ -295,8 +304,8 @@
     return pl.pallas_call(
         projection_kernel,
         out_shape=(
-            jax.ShapeDtypeStruct((2 * NDATES, nifg), BF16),
-            jax.ShapeDtypeStruct((nifg, DATE_PAD), BF16),
+            pltpu.HBM((NDATES, nifg), BF16),
+            pltpu.HBM((nifg, 2 * NDATES), BF16),
         ),
         scratch_shapes=[
             pltpu.VMEM((tail, LANES), F32),
@@ -311,48 +320,60 @@
     )(date_pairs, date_pairs.T)
 
 
-def invert_kernel(d_ref, p_ref, g_ref, m_ref):
+def invert_kernel(d_ref, p_ref, g_ref, *refs):
     scaled = d_ref[...].astype(F32) * (1.0 / THRESHOLD)
-    width = scaled.shape[1]
-    fill = jnp.zeros((DATE_PAD - NDATES, width), BF16)
     series = None
     misfit = scaled
     for step in range(ITERS):
         if step > 0:
             high = series.astype(BF16)
             low = (series - high.astype(F32)).astype(BF16)
-            misfit = scaled - (
-                mm(g_ref[...], jnp.concatenate([high, fill], axis=0))
-                + mm(g_ref[...], jnp.concatenate([low, fill], axis=0))
-            )
+            misfit = scaled - mm(g_ref[...], jnp.concatenate([high, low], axis=0))
         clipped = jnp.clip(misfit, -1.0, 1.0).astype(BF16)
-        both = mm(p_ref[...], clipped)
-        change = both[:NDATES] + both[NDATES:]
+        change = mm(p_ref[...], clipped)
         series = change if series is None else series + change
     series = series * THRESHOLD
-    tiles = width // LANES
+    tiles = series.shape[1] // LANES
+    place = pl.program_id(0) * tiles
+    if len(refs) == 1:
+        (m_ref,) = refs
+        for t in range(tiles):
+            m_ref[pl.ds(place + t, NDATES, stride=4), :] = series[:, t * LANES : (t + 1) * LANES]
+        return
+    other_ref, m_ref, keep = refs
     for t in range(tiles):
-        m_ref[pl.ds(pl.program_id(0) * tiles + t, NDATES, stride=8), :] = series[
-            :, t * LANES : (t + 1) * LANES
-        ]
-
-
-def invert(sines, p, g):
+        keep[pl.ds(4 + place + t, NDATES, stride=8), :] = series[:, t * LANES : (t + 1) * LANES]
+
+    @pl.when(pl.program_id(0) == pl.num_programs(0) - 1)
+    def _():
+        for t in range(4):
+            keep[pl.ds(t, NDATES, stride=8), :] = other_ref[pl.ds(t, NDATES, stride=4), :]
+        m_ref[...] = keep[...].astype(BF16)
+
+
+WIDTH = 256
+
+
+def invert(sines, p, g, *other):
     nifg, pixels = sines.shape
-    width = 256
+    width = WIDTH
+    rows = NDATES * (8 if other else 4)
     return pl.pallas_call(
         invert_kernel,
         grid=(pixels // width,),
         in_specs=[
             pl.BlockSpec((nifg, width), lambda i: (0, i)),
-            pl.BlockSpec(p.shape, lambda i: (0, 0)),
-            pl.BlockSpec(g.shape, lambda i: (0, 0)),
+            whole(p), whole(g), *(whole(x) for x in other)
         ],
-        out_specs=pl.BlockSpec((NDATES * 8, LANES), lambda i: (0, 0)),
-        out_shape=jax.ShapeDtypeStruct((NDATES * 8, LANES), F32),
-        compiler_params=pltpu.CompilerParams(vmem_limit_bytes=48 << 20),
-        name="invert",
-    )(sines, p, g)
+        out_specs=pl.BlockSpec((rows, LANES), lambda i: (0, 0)),
+        out_shape=jax.ShapeDtypeStruct((rows, LANES), BF16) if other else pltpu.HBM((rows, LANES), F32),
+        scratch_shapes=[pltpu.VMEM((rows, LANES), F32)] if other else [],
+        compiler_params=pltpu.CompilerParams(vmem_limit_bytes=32 << 20),
+        cost_estimate=pl.CostEstimate(
+            flops=pixels * nifg * NDATES * 14, bytes_accessed=6_000_000, transcendentals=0
+        ),
+        name="invert_rest" if other else "invert",
+    )(sines, in_hbm(p), in_hbm(g), *(in_hbm(x) for x in other))
 
 
 def split3(x):
@@ -365,16 +386,17 @@
     return mm(ah, bh) + (mm(ah, bl) + mm(al, bh))
 
 
-def gather_kernel(got_ref, ch_ref, cl_ref, series_ref, smooth_ref):
+def gather_kernel(got_ref, ch_ref, cl_ref, series_ref, smooth_ref, low_ref, high_ref, wide):
     dates, rows, cols = series_ref.shape
     tiles = cols // LANES
+    wide[...] = got_ref[...].astype(F32)
     for d in range(dates):
         halves = []
         for h in range(2):
             halves.append(
                 jnp.concatenate(
                     [
-                        got_ref[pl.ds(d * 8 + h * tiles + c, HALF, stride=dates * 8), :]
+                        wide[pl.ds(d * 8 + h * tiles + c, HALF, stride=dates * 8), :]
                         for c in range(tiles)
                     ],
                     axis=1,
@@ -382,15 +404,22 @@
             )
         x = jnp.concatenate(halves, axis=0)
         series_ref[d] = x
-        smooth_ref[d] = dot3(split3(x), (ch_ref[...], cl_ref[...]))
+        x = x.astype(BF16)
+        smooth = mm(x, ch_ref[...]) + mm(x, cl_ref[...])
+        smooth_ref[d] = smooth
+        low_ref[d] = smooth[:RADIUS]
+        high_ref[d] = smooth[rows - RADIUS :]
 
 
 def gather(got, col_high, col_low, rows, cols):
     dates = got.shape[0] // 8 // HALF
+    block = jax.ShapeDtypeStruct((dates, rows, cols), F32)
+    border = jax.ShapeDtypeStruct((dates, RADIUS, cols), F32)
     return pl.pallas_call(
         gather_kernel,
-        out_shape=(jax.ShapeDtypeStruct((dates, rows, cols), F32),) * 2,
-        compiler_params=pltpu.CompilerParams(vmem_limit_bytes=40 << 20),
+        out_shape=(block, block, border, border),
+        scratch_shapes=[pltpu.VMEM(got.shape, F32)],
+        compiler_params=pltpu.CompilerParams(vmem_limit_bytes=24 << 20),
         name="gather",
     )(got, col_high, col_low)
 
@@ -433,26 +462,30 @@
 
 def on_device(ifg_real, ifg_imag, date_pairs):
     n, rows, cols = ifg_real.shape
-    rows_c, rows_e, fwd, inv, back_c, back_e = (jnp.asarray(t) for t in tables())
+    rows_t, fwd, inv, back_up, back_dn = (jnp.asarray(t) for t in tables())
     col_t, row_t = blur_tables(rows * lax.axis_size("row"), rows, cols)
     col_high, col_low = bf16(col_t), bf16(col_t - bf16(col_t).astype(np.float32))
     row_high, row_low = bf16(row_t), bf16(row_t - bf16(row_t).astype(np.float32))
 
-    up_re, dn_re = neighbours(ifg_real[:, :HALF], ifg_real[:, rows - HALF :], "row")
-    up_im, dn_im = neighbours(ifg_imag[:, :HALF], ifg_imag[:, rows - HALF :], "row")
-    u = centre(ifg_real, ifg_imag, rows_c, fwd, inv)
+    low = jnp.stack([ifg_real[:, :HALF], ifg_imag[:, :HALF]])
+    high = jnp.stack([ifg_real[:, rows - HALF :], ifg_imag[:, rows - HALF :]])
+    above, below = neighbours(low, high, "row")
+    u = centre(ifg_real, ifg_imag, rows_t, fwd, inv)
     p, g = projection(date_pairs)
-    q = edges(ifg_real, ifg_imag, (up_re, up_im, dn_re, dn_im), u, rows_e, fwd, inv, back_c, back_e)
-    sines = lax.all_to_all(q, "ifg", split_axis=0, concat_axis=0, tiled=True)
-    series = invert(sines.reshape(-1, 2 * cols), p, g)
+    u, p, g = lax.optimization_barrier((u, p, g))
+    series = ()
+    for upper, halo, back in ((True, above, back_up), (False, below, back_dn)):
+        q = edge(upper, ifg_real, ifg_imag, halo, u, rows_t, fwd, inv, back)
+        sines = lax.all_to_all(q, "ifg", split_axis=0, concat_axis=0, tiled=True)
+        series = (invert(sines.reshape(-1, cols), p, g, *series),)
     devices = lax.axis_size("ifg")
     series = lax.all_to_all(
-        series.reshape(devices, -1, LANES), "ifg", split_axis=0, concat_axis=0, tiled=True
+        series[0].reshape(devices, -1, LANES), "ifg", split_axis=0, concat_axis=0, tiled=True
     )
-    series, smooth = gather(
+    series, smooth, low, high = gather(
         series.reshape(-1, LANES), jnp.asarray(col_high), jnp.asarray(col_low), rows, cols
     )
-    up, dn = neighbours(smooth[:, :RADIUS], smooth[:, rows - RADIUS :], "row")
+    up, dn = neighbours(low, high, "row")
     where = lax.axis_index("row").astype(jnp.int32).reshape(1)
     return finish(where, series, smooth, up, dn, jnp.asarray(row_high), jnp.asarray(row_low))
 

time: 184 us -> 147 us (0.80)
  Pallas kernels: 93.5 us -> 71.2 us
  waiting for transfers between devices: 28.1 us -> 18.7 us
  blocking collectives: 25.3 us -> 17.1 us
  local copies, waits for them, and re-layouts: 9.17 us -> 5.55 us
  other arithmetic: 0 us -> 3.11 us
  starting transfers between devices: 26.7 us -> 29.8 us
    pallas_call x1, Pallas kernels: 27.9 us -> 11.7 us  [centre(): pl.pallas_call(centre_kernel, grid=(n // g,), in_specs=[block, block, who...]
    all_to_all x1 -> x2, waiting for transfers between devices: 22.5 us -> 13.3 us  [on_device(): sines = lax.all_to_all(q, 'ifg', split_axis=0, concat_axis=0, tiled=True)]
    all_to_all x1, blocking collectives: 25.3 us -> 17.1 us  [on_device(): lax.all_to_all(series[0].reshape(devices, -1, LANES), 'ifg', split_axis=0...]
    all_to_all x1 -> x2, starting transfers between devices: 10.2 us -> 17.1 us  [on_device(): sines = lax.all_to_all(q, 'ifg', split_axis=0, concat_axis=0, tiled=True)]
    pallas_call x3 -> x4, Pallas kernels: 46.1 us -> 42.3 us  [the longest x2 30.1 us: edge(): pl.pallas_call(lambda *refs: edge_kernel(upper, *refs), grid=(n // g,), i...]
    unnamed x35 -> x25, local copies, waits for them, and re-layouts: 6.1 us -> 2.78 us
    another operation x0 -> x2, other arithmetic: none -> 3.11 us  [the longest x1 1.58 us: on_device(): high = jnp.stack([ifg_real[:, rows - HALF:], ifg_imag[:, rows - HALF:]])]
    slice x3 -> x0, local copies, waits for them, and re-layouts: 3.06 us -> none  [the longest x1 1.94 us: on_device(): ifg_real[:, :HALF]]
  transfers between devices with their start and end apart: 7 -> 6, of which waited for: 3 -> 4; matrix products, arithmetic and copies ran while one was open for 1% -> 1% of each run, Pallas kernels for 20% -> 40%
where the time goes in v2:
time: 147 us; the launch traced here: 146 us
  Pallas kernels  71.2 us (48%)
  starting transfers between devices  29.8 us (20%)
  waiting for transfers between devices  18.7 us (13%)
  blocking collectives  17.1 us (12%)
  local copies, waits for them, and re-layouts  5.55 us (4%)
  other arithmetic  3.11 us (2%)
    pallas_call x2, Pallas kernels, edge(): pl.pallas_call(lambda *refs: edge_kernel(upper, *refs), grid=(n // g,), i...  30.1 us
    all_to_all x2, starting transfers between devices, on_device(): sines = lax.all_to_all(q, 'ifg', split_axis=0, concat_axis=0, tiled=True)  17.1 us
    all_to_all x1, blocking collectives, on_device(): lax.all_to_all(series[0].reshape(devices, -1, LANES), 'ifg', split_axis=0...  17.1 us
    pallas_call x2, Pallas kernels, invert(): pl.pallas_call(invert_kernel, grid=(pixels // width,), in_specs=[pl.Block...  15.3 us
    all_to_all x2, waiting for transfers between devices, on_device(): sines = lax.all_to_all(q, 'ifg', split_axis=0, concat_axis=0, tiled=True)  13.3 us
    pallas_call x1, Pallas kernels, centre(): pl.pallas_call(centre_kernel, grid=(n // g,), in_specs=[block, block, who...  11.7 us
    pallas_call x1, Pallas kernels, projection(): pl.pallas_call(projection_kernel, out_shape=(pltpu.HBM((NDATES, nifg), BF...  9.4 us
    ppermute x2, starting transfers between devices, neighbours(): lax.ppermute(high_part, axis, forward)  7.45 us
  transfers between devices with their start and end apart: 6, of which 4 were waited for; matrix products, arithmetic and copies ran while one was open for 1% of the time, Pallas kernels for 40%

profile of v2, /device:TPU:1, one launch (start us, length us, event | category | flops | bytes accessed | tf_op | source)
XLA Modules:
  0.0 146.2 jit_solution(11522970771860414024)
XLA Ops:
  0.6 2.8 %slice_bitcast_fusion = (bf16[1,32,32,512]{3,2,1,0:T(8,128)(2,1)S(1)}, bf16[1,32,32,512]{3,2,1,0:T(8,128)(2,1)S(1)}, bf16[1,32,32,512]{3,2,1,0:T(8,128)(2,1)S(1)}, bf16[1,32,32,512]{3,2,1,0:T(8,128)(2,1)S(1)}) fusion(bf16[32,64,512]{2,1,0:T(8,128)(2,1)} %refs_1_.3, bf16[32,64,512]{2,1,0:T(8,128)(2,1)} %refs_0_.3), kind=kLoop, calls=%fused_computation.2 | loop fusion | bytes 8388608 | tf_op jit(solution)/shard_map/stack | solution.py:471
  3.4 1.6 %pad_maximum_fusion.1 = bf16[2,32,32,512]{3,2,1,0:T(8,128)(2,1)} fusion(bf16[1,32,32,512]{3,2,1,0:T(8,128)(2,1)S(1)} %get-tuple-element.22, bf16[1,32,32,512]{3,2,1,0:T(8,128)(2,1)S(1)} %get-tuple-element.25), kind=kLoop, calls=%fused_computation.1 | loop fusion | flops 1048576 | bytes 4194304 | tf_op jit(solution)/shard_map/stack | solution.py:471
  5.0 4.9 %collective-permute-start.1 = (bf16[2,32,32,512]{3,2,1,0:T(8,128)(2,1)}, bf16[2,32,32,512]{3,2,1,0:T(8,128)(2,1)}, u32[]{:S(2)}, u32[]{:S(2)}) collective-permute-start(bf16[2,32,32,512]{3,2,1,0:T(8,128)(2,1)} %pad_maximum_fusion.1), channel_id=1, source_target_pairs={{0,1},{1,2},{2,3},{4,5},{5,6},{6,7},{8,9},{9,10},{10,11},{12,13},{... | collective-permute-start | bytes 6291464 | tf_op jit(solution)/shard_map/ppermute | solution.py:460
  9.9 1.5 %pad_maximum_fusion = bf16[2,32,32,512]{3,2,1,0:T(8,128)(2,1)} fusion(bf16[1,32,32,512]{3,2,1,0:T(8,128)(2,1)S(1)} %get-tuple-element.23, bf16[1,32,32,512]{3,2,1,0:T(8,128)(2,1)S(1)} %get-tuple-element.24), kind=kLoop, calls=%fused_computation | loop fusion | flops 1048576 | bytes 4194304 | tf_op jit(solution)/shard_map/stack | solution.py:470
  11.5 1.9 %collective-permute-start = (bf16[2,32,32,512]{3,2,1,0:T(8,128)(2,1)}, bf16[2,32,32,512]{3,2,1,0:T(8,128)(2,1)S(1)}, u32[]{:S(2)}, u32[]{:S(2)}) collective-permute-start(bf16[2,32,32,512]{3,2,1,0:T(8,128)(2,1)} %pad_maximum_fusion), channel_id=1, source_target_pairs={{1,0},{2,1},{3,2},{5,4},{6,5},{7,6},{9,8},{10,9},{11,10},{13,12},{... | collective-permute-start | bytes 6291464 | tf_op jit(solution)/shard_map/ppermute | solution.py:460
  13.7 9.4 %projection.1 = (bf16[320,1024]{1,0:T(8,128)(2,1)}, bf16[1024,640]{1,0:T(8,128)(2,1)}) custom-call(s32[1024,2]{1,0:T(8,128)S(1)} %copy.14.pairs_ref, s32[2,1024]{1,0:T(2,128)S(1)} %bitcast.18), custom_call_target="tpu_custom_call" | custom-call | flops 20000000000 | bytes 4000000 | tf_op jit(solution)/shard_map/projection/pallas_call | solution.py:304
  23.1 11.7 %centre.1.refs_3_ = bf16[32,128,512]{2,1,0:T(8,128)(2,1)} custom-call(bf16[32,64,512]{2,1,0:T(8,128)(2,1)} %refs_0_.3, bf16[32,64,512]{2,1,0:T(8,128)(2,1)} %refs_1_.3, bf16[128,128]{1,0:T(8,128)(2,1)S(1)} %copy-done.8, bf16[3,256,256]{2,1,0:T(8,128)(2,1)S(1)} %copy-done.5, bf16[3,256,256]{2,1,0:T(8,128)(2,1)S(1)} %copy-done.6), custom_call_target="tpu_custom_call" | custom-call | flops 6979321856 | bytes 8388608 | tf_op jit(solution)/shard_map/centre/pallas_call | solution.py:150
  34.8 15.1 %upper.1 = bf16[32,32,512]{2,1,0:T(8,128)(2,1)} custom-call(bf16[32,64,512]{2,1,0:T(8,128)(2,1)} %refs_0_.3, bf16[32,64,512]{2,1,0:T(8,128)(2,1)} %refs_1_.3, bf16[2,32,32,512]{3,2,1,0:T(8,128)(2,1)} %collective-permute-done.1.refs_2_, bf16[32,128,512]{2,1,0:T(8,128)(2,1)} %centre.1.refs_3_, bf16[128,128]{1,0:T(8,128)(2,1)S(1)} %copy-done.8, ...), custom_call_target="tpu_custom_call" | custom-call | flops 8053063680 | bytes 7340032 | tf_op jit(solution)/shard_map/upper/pallas_call | solution.py:199
  49.9 10.1 %all-to-all-start.1 = ((bf16[32,32,512]{2,1,0:T(8,128)(2,1)}), bf16[32,32,512]{2,1,0:T(8,128)(2,1)S(1)}, u32[]{:S(2)}, u32[]{:S(2)}) async-start(bf16[32,32,512]{2,1,0:T(8,128)(2,1)} %upper.1), calls=%async_computation.1 | async-start | bytes 2097152 | tf_op jit(solution)/shard_map/all_to_all | solution.py:479
  60.0 1.0 copy-done.7
  61.0 0.8 copy-done.9
  62.5 15.0 %lower.1 = bf16[32,32,512]{2,1,0:T(8,128)(2,1)} custom-call(bf16[32,64,512]{2,1,0:T(8,128)(2,1)} %refs_0_.3, bf16[32,64,512]{2,1,0:T(8,128)(2,1)} %refs_1_.3, bf16[2,32,32,512]{3,2,1,0:T(8,128)(2,1)S(1)} %collective-permute-done.refs_2_, bf16[32,128,512]{2,1,0:T(8,128)(2,1)} %centre.1.refs_3_, bf16[128,128]{1,0:T(8,128)(2,1)S(1)} %copy-done.9, ...), custom_call_target="tpu_custom_call" | custom-call | flops 8053063680 | bytes 7340032 | tf_op jit(solution)/shard_map/lower/pallas_call | solution.py:199
  77.5 2.3 %all-to-all-done.1 = bf16[32,32,512]{2,1,0:T(8,128)(2,1)S(1)} async-done(((bf16[32,32,512]{2,1,0:T(8,128)(2,1)}), bf16[32,32,512]{2,1,0:T(8,128)(2,1)S(1)}, u32[]{:S(2)}, u32[]{:S(2)}) %all-to-all-start.1) | async-done | bytes 1048608 | tf_op jit(solution)/shard_map/all_to_all | solution.py:479
  79.8 7.1 %all-to-all-start = ((bf16[32,32,512]{2,1,0:T(8,128)(2,1)}), bf16[32,32,512]{2,1,0:T(8,128)(2,1)S(1)}, u32[]{:S(2)}, u32[]{:S(2)}) async-start(bf16[32,32,512]{2,1,0:T(8,128)(2,1)} %lower.1), calls=%async_computation | async-start | bytes 2097152 | tf_op jit(solution)/shard_map/all_to_all | solution.py:479
  86.9 7.8 %invert.1.refs_0_ = f32[1280,128]{1,0:T(8,128)} custom-call(bf16[1024,512]{1,0:T(8,128)(2,1)S(1)} %bitcast.15, bf16[320,1024]{1,0:T(8,128)(2,1)} %get-tuple-element.14.p_ref, bf16[1024,640]{1,0:T(8,128)(2,1)} %get-tuple-element.15.g_ref), custom_call_target="tpu_custom_call" | custom-call | flops 2348810240 | bytes 6000000 | tf_op jit(solution)/shard_map/invert/pallas_call | solution.py:361
  94.8 11.0 %all-to-all-done = bf16[32,32,512]{2,1,0:T(8,128)(2,1)S(1)} async-done(((bf16[32,32,512]{2,1,0:T(8,128)(2,1)}), bf16[32,32,512]{2,1,0:T(8,128)(2,1)S(1)}, u32[]{:S(2)}, u32[]{:S(2)}) %all-to-all-start) | async-done | bytes 1048608 | tf_op jit(solution)/shard_map/all_to_all | solution.py:479
  105.8 7.5 %invert_rest.1 = bf16[2560,128]{1,0:T(8,128)(2,1)S(1)} custom-call(bf16[1024,512]{1,0:T(8,128)(2,1)S(1)} %bitcast.16, bf16[320,1024]{1,0:T(8,128)(2,1)} %get-tuple-element.14.p_ref, bf16[1024,640]{1,0:T(8,128)(2,1)} %get-tuple-element.15.g_ref, f32[1280,128]{1,0:T(8,128)} %invert.1.refs_0_), custom_call_target="tpu_custom_call" | custom-call | flops 2348810240 | bytes 6000000 | tf_op jit(solution)/shard_map/invert_rest/pallas_call | solution.py:361
  113.3 17.1 %all_to_all.15 = bf16[32,80,128]{2,1,0:T(8,128)(2,1)S(1)} all-to-all(bf16[32,80,128]{2,1,0:T(8,128)(2,1)S(1)} %bitcast.17), channel_id=1, replica_groups=mesh['ifg'=32,'row'=4] {'ifg'}, dimensions={0} | all-to-all | bytes 1310720 | tf_op jit(solution)/shard_map/all_to_all | solution.py:482
  130.4 2.8 %gather.1 = (f32[10,64,512]{2,1,0:T(8,128)S(1)}, f32[10,64,512]{2,1,0:T(8,128)S(1)}, f32[10,16,512]{2,1,0:T(8,128)}, f32[10,16,512]{2,1,0:T(8,128)}) custom-call(bf16[2560,128]{1,0:T(8,128)(2,1)S(1)} %bitcast.14, bf16[512,512]{1,0:T(8,128)(2,1)S(1)} %copy-done, bf16[512,512]{1,0:T(8,128)(2,1)S(1)} %copy-done.1), custom_call_target="tpu_custom_call" | custom-call | tf_op jit(solution)/shard_map/gather/pallas_call | solution.py:418
  133.2 2.5 %collective-permute-start.2 = (f32[10,16,512]{2,1,0:T(8,128)}, f32[10,16,512]{2,1,0:T(8,128)S(1)}, u32[]{:S(2)}, u32[]{:S(2)}) collective-permute-start(f32[10,16,512]{2,1,0:T(8,128)} %get-tuple-element.18), channel_id=1, source_target_pairs={{0,1},{1,2},{2,3},{4,5},{5,6},{6,7},{8,9},{9,10},{10,11},{12,13},{... | collective-permute-start | bytes 983048 | tf_op jit(solution)/shard_map/ppermute | solution.py:460
  135.7 3.3 %collective-permute-start.3 = (f32[10,16,512]{2,1,0:T(8,128)}, f32[10,16,512]{2,1,0:T(8,128)S(1)}, u32[]{:S(2)}, u32[]{:S(2)}) collective-permute-start(f32[10,16,512]{2,1,0:T(8,128)} %get-tuple-element.19), channel_id=1, source_target_pairs={{1,0},{2,1},{3,2},{5,4},{6,5},{7,6},{9,8},{10,9},{11,10},{13,12},{... | collective-permute-start | bytes 983048 | tf_op jit(solution)/shard_map/ppermute | solution.py:460
  139.0 1.0 collective-permute-done.2.up_ref
  140.0 4.3 %collective-permute-done.3.dn_ref = f32[10,16,512]{2,1,0:T(8,128)S(1)} collective-permute-done((f32[10,16,512]{2,1,0:T(8,128)}, f32[10,16,512]{2,1,0:T(8,128)S(1)}, u32[]{:S(2)}, u32[]{:S(2)}) %collective-permute-start.3) | collective-permute-done | bytes 327712 | tf_op jit(solution)/shard_map/ppermute | solution.py:460
  144.3 1.9 %finish.1 = (f32[10,64,512]{2,1,0:T(8,128)}, f32[10,64,512]{2,1,0:T(8,128)}) custom-call(s32[1]{0:T(128)} %bitcast.where_ref, f32[10,64,512]{2,1,0:T(8,128)S(1)} %get-tuple-element.16.series_ref, f32[10,64,512]{2,1,0:T(8,128)S(1)} %get-tuple-element.17.smooth_ref, f32[10,16,512]{2,1,0:T(8,128)S(1)} %collective-permute-done.2.up_ref, ...), custom_call_target="tpu_custom_call" | custom-call | tf_op jit(solution)/shard_map/finish/pallas_call | solution.py:442
  (25 shorter events, 1.0 us)
Async XLA Ops:
  5.0 29.8 %collective-permute-start.1 = (bf16[2,32,32,512]{3,2,1,0:T(8,128)(2,1)}, bf16[2,32,32,512]{3,2,1,0:T(8,128)(2,1)}, u32[]{:S(2)}, u32[]{:S(2)}) collective-permute-start(bf16[2,32,32,512]{3,2,1,0:T(8,128)(2,1)} %pad_maximum_fusion.1), channel_id=1, source_target_pairs={{0,1},{1,2},{2,3},{4,5},{5,6},{6,7},{8,9},{9,10},{10,11},{12,13},{... | collective-permute-start | bytes 6291464 | tf_op jit(solution)/shard_map/ppermute | solution.py:460
  9.9 3.5 %copy-start.4 = (s32[1024,2]{0,1:T(2,128)S(1)}, s32[1024,2]{0,1:T(2,128)}, u32[]{:S(2)}) copy-start(s32[1024,2]{0,1:T(2,128)} %param.14) | copy-start | bytes 24580
  11.5 48.5 %collective-permute-start = (bf16[2,32,32,512]{3,2,1,0:T(8,128)(2,1)}, bf16[2,32,32,512]{3,2,1,0:T(8,128)(2,1)S(1)}, u32[]{:S(2)}, u32[]{:S(2)}) collective-permute-start(bf16[2,32,32,512]{3,2,1,0:T(8,128)(2,1)} %pad_maximum_fusion), channel_id=1, source_target_pairs={{1,0},{2,1},{3,2},{5,4},{6,5},{7,6},{9,8},{10,9},{11,10},{13,12},{... | collective-permute-start | bytes 6291464 | tf_op jit(solution)/shard_map/ppermute | solution.py:460
  13.6 9.4 %copy-start.5 = (bf16[3,256,256]{2,1,0:T(8,128)(2,1)S(1)}, bf16[3,256,256]{2,1,0:T(8,128)(2,1)}, u32[]{:S(2)}) copy-start(bf16[3,256,256]{2,1,0:T(8,128)(2,1)} %constant.23.clone.fwd_ref.refs_5_) | copy-start | bytes 1179652
  13.6 9.4 %copy-start.6 = (bf16[3,256,256]{2,1,0:T(8,128)(2,1)S(1)}, bf16[3,256,256]{2,1,0:T(8,128)(2,1)}, u32[]{:S(2)}) copy-start(bf16[3,256,256]{2,1,0:T(8,128)(2,1)} %constant.24.clone.inv_ref.refs_6_) | copy-start | bytes 1179652
  13.6 9.4 %copy-start.8 = (bf16[128,128]{1,0:T(8,128)(2,1)S(1)}, bf16[128,128]{1,0:T(8,128)(2,1)}, u32[]{:S(2)}) copy-start(bf16[128,128]{1,0:T(8,128)(2,1)} %constant.22.clone.rows_ref.refs_4_) | copy-start | bytes 98308
  23.1 11.7 %copy-start.11 = (bf16[64,256]{1,0:T(8,128)(2,1)S(1)}, bf16[64,256]{1,0:T(8,128)(2,1)}, u32[]{:S(2)}) copy-start(bf16[64,256]{1,0:T(8,128)(2,1)} %constant.25.clone.refs_7_) | copy-start | bytes 98308
  49.9 29.9 %all-to-all-start.1 = ((bf16[32,32,512]{2,1,0:T(8,128)(2,1)}), bf16[32,32,512]{2,1,0:T(8,128)(2,1)S(1)}, u32[]{:S(2)}, u32[]{:S(2)}) async-start(bf16[32,32,512]{2,1,0:T(8,128)(2,1)} %upper.1), calls=%async_computation.1 | async-start | bytes 2097152 | tf_op jit(solution)/shard_map/all_to_all | solution.py:479
  60.0 1.0 copy-start.7
  61.0 0.8 copy-start.9
  61.7 0.8 copy-start.10
  79.8 25.9 %all-to-all-start = ((bf16[32,32,512]{2,1,0:T(8,128)(2,1)}), bf16[32,32,512]{2,1,0:T(8,128)(2,1)S(1)}, u32[]{:S(2)}, u32[]{:S(2)}) async-start(bf16[32,32,512]{2,1,0:T(8,128)(2,1)} %lower.1), calls=%async_computation | async-start | bytes 2097152 | tf_op jit(solution)/shard_map/all_to_all | solution.py:479
  105.8 24.6 %copy-start = (bf16[512,512]{1,0:T(8,128)(2,1)S(1)}, bf16[512,512]{1,0:T(8,128)(2,1)}, u32[]{:S(2)}) copy-start(bf16[512,512]{1,0:T(8,128)(2,1)} %constant.27.clone.ch_ref) | copy-start | bytes 1572868
  105.8 24.6 %copy-start.1 = (bf16[512,512]{1,0:T(8,128)(2,1)S(1)}, bf16[512,512]{1,0:T(8,128)(2,1)}, u32[]{:S(2)}) copy-start(bf16[512,512]{1,0:T(8,128)(2,1)} %constant.28.clone.cl_ref) | copy-start | bytes 1572868
  113.2 31.0 %copy-start.2 = (bf16[4,64,96]{2,1,0:T(8,128)(2,1)S(1)}, bf16[4,64,96]{2,1,0:T(8,128)(2,1)}, u32[]{:S(2)}) copy-start(bf16[4,64,96]{2,1,0:T(8,128)(2,1)} %constant.29.clone.rh_ref) | copy-start | bytes 147460
  113.3 31.0 %copy-start.3 = (bf16[4,64,96]{2,1,0:T(8,128)(2,1)S(1)}, bf16[4,64,96]{2,1,0:T(8,128)(2,1)}, u32[]{:S(2)}) copy-start(bf16[4,64,96]{2,1,0:T(8,128)(2,1)} %constant.30.clone.rl_ref) | copy-start | bytes 147460
  133.2 6.8 %collective-permute-start.2 = (f32[10,16,512]{2,1,0:T(8,128)}, f32[10,16,512]{2,1,0:T(8,128)S(1)}, u32[]{:S(2)}, u32[]{:S(2)}) collective-permute-start(f32[10,16,512]{2,1,0:T(8,128)} %get-tuple-element.18), channel_id=1, source_target_pairs={{0,1},{1,2},{2,3},{4,5},{5,6},{6,7},{8,9},{9,10},{10,11},{12,13},{... | collective-permute-start | bytes 983048 | tf_op jit(solution)/shard_map/ppermute | solution.py:460
  135.7 8.6 %collective-permute-start.3 = (f32[10,16,512]{2,1,0:T(8,128)}, f32[10,16,512]{2,1,0:T(8,128)S(1)}, u32[]{:S(2)}, u32[]{:S(2)}) collective-permute-start(f32[10,16,512]{2,1,0:T(8,128)} %get-tuple-element.19), channel_id=1, source_target_pairs={{1,0},{2,1},{3,2},{5,4},{6,5},{7,6},{9,8},{10,9},{11,10},{13,12},{... | collective-permute-start | bytes 983048 | tf_op jit(solution)/shard_map/ppermute | solution.py:460

commit v3 on v2

--- a/solution.py
+++ b/solution.py
@@ -38,18 +38,9 @@
 
     rows_strip = np.block([[c, s], [-s, c]])
     c2, s2 = np.kron(two, c), np.kron(two, s)
-    cols = np.block([[c2, -s2], [s2, c2]])
-    shift = np.zeros((2, LANES, LANES))
-    for i in range(LANES):
-        if i < HALF:
-            shift[0, LANES - HALF + i, i] = 1.0
-        else:
-            shift[1, i - HALF, i] = 1.0
-    left, right = np.kron(two, shift[0]), np.kron(two, shift[1])
+    forward = np.block([[c2, -s2], [s2, c2]])
     t2 = np.concatenate([taper, taper])
-    inv = np.block([[c2 * t2, s2 * t2], [-s2 * t2, c2 * t2]])
-    forward = np.stack([cols, left @ cols, right @ cols])
-    inverse = np.stack([inv, inv @ left.T, inv @ right.T])
+    inverse = np.block([[c2 * t2, s2 * t2], [-s2 * t2, c2 * t2]])
     ct, st = c * taper[:, None], s * taper[:, None]
     back = []
     for centre_rows, edge_rows in ((slice(0, HALF), slice(HALF, PATCH)), (slice(HALF, PATCH), slice(0, HALF))):
@@ -87,30 +78,35 @@
     for c in range(count):
         sl = slice(c * LANES, (c + 1) * LANES)
         pieces.append(jnp.concatenate([y_re[:, sl], y_im[:, sl]], axis=1))
-    f0, f_left, f_right = fwd[0], fwd[1], fwd[2]
-    g0, g_left, g_right = inv[0], inv[1], inv[2]
+    f0, g0 = fwd[...], inv[...]
 
     def shaped(z):
         re, im = z[:, :LANES], z[:, LANES:]
         scale = lax.rsqrt(lax.rsqrt(re * re + im * im + 1.0))
         return jnp.concatenate([(re * scale).astype(BF16), (im * scale).astype(BF16)], axis=1)
 
-    even = []
-    for c in range(count + 1):
-        z = None
-        if c > 0:
-            z = mm(pieces[c - 1], f_left)
-        if c < count:
-            w = mm(pieces[c], f_right)
-            z = w if z is None else z + w
-        even.append(shaped(z))
+    lane = lax.broadcasted_iota(jnp.int32, (y_re.shape[0], LANES), 1)
+
+    def moved(y):
+        rolled = [pltpu.roll(y[:, c * LANES : (c + 1) * LANES], HALF, axis=1) for c in range(count)]
+        zero = jnp.zeros_like(rolled[0])
+        before, after = [zero] + rolled, rolled + [zero]
+        return [jnp.where(lane < HALF, a, b) for a, b in zip(before, after)]
+
+    even = [
+        shaped(mm(jnp.concatenate([a, b], axis=1), f0)) for a, b in zip(moved(y_re), moved(y_im))
+    ]
+    def back(z):
+        u = mm(z, g0)
+        return [pltpu.roll(u[:, :LANES], LANES - HALF, axis=1), pltpu.roll(u[:, LANES:], LANES - HALF, axis=1)]
+
+    turned = [back(z) for z in even]
     out_re, out_im = [], []
     for c in range(count):
-        odd = shaped(mm(pieces[c], f0))
-        u = mm(odd, g0) + mm(even[c], g_right) + mm(even[c + 1], g_left)
-        u = u.astype(BF16)
-        out_re.append(u[:, :LANES])
-        out_im.append(u[:, LANES:])
+        u = mm(shaped(mm(pieces[c], f0)), g0)
+        for out, k in ((out_re, 0), (out_im, 1)):
+            other = jnp.where(lane < LANES - HALF, turned[c][k], turned[c + 1][k])
+            out.append((u[:, k * LANES : (k + 1) * LANES] + other).astype(BF16))
     return jnp.concatenate(out_re, axis=1), jnp.concatenate(out_im, axis=1)
 
 
@@ -132,7 +128,7 @@
         u_ref[i, PATCH:] = u_im[sl]
 
 
-BATCH = 4
+BATCH = 8
 
 
 def in_hbm(x):
@@ -159,7 +155,7 @@
             transcendentals=n * 64 * 2304,
         ),
         name="centre",
-    )(in_hbm(re), in_hbm(im), rows_t, fwd, inv)
+    )(*(in_hbm(x) for x in (re, im, rows_t, fwd, inv)))
 
 
 GROUP = 16
@@ -212,7 +208,7 @@
             transcendentals=n * 64 * 2304,
         ),
         name="upper" if upper else "lower",
-    )(in_hbm(re), in_hbm(im), halo, in_hbm(u), rows_t, fwd, inv, back)
+    )(in_hbm(re), in_hbm(im), halo, *(in_hbm(x) for x in (u, rows_t, fwd, inv, back)))
 
 
 def projection_kernel(pairs_ref, pairs_t_ref, p_ref, g_ref, band, factor, solved):
@@ -321,18 +317,21 @@
 
 
 def invert_kernel(d_ref, p_ref, g_ref, *refs):
-    scaled = d_ref[...].astype(F32) * (1.0 / THRESHOLD)
-    series = None
+    chains = range(d_ref.shape[1] // CHAIN)
+    scaled = [d_ref[:, k * CHAIN : (k + 1) * CHAIN].astype(F32) * (1.0 / THRESHOLD) for k in chains]
+    series = [None for k in chains]
     misfit = scaled
     for step in range(ITERS):
         if step > 0:
-            high = series.astype(BF16)
-            low = (series - high.astype(F32)).astype(BF16)
-            misfit = scaled - mm(g_ref[...], jnp.concatenate([high, low], axis=0))
-        clipped = jnp.clip(misfit, -1.0, 1.0).astype(BF16)
-        change = mm(p_ref[...], clipped)
-        series = change if series is None else series + change
-    series = series * THRESHOLD
+            parts = []
+            for k in chains:
+                high = series[k].astype(BF16)
+                low = (series[k] - high.astype(F32)).astype(BF16)
+                parts.append(jnp.concatenate([high, low], axis=0))
+            misfit = [scaled[k] - mm(g_ref[...], parts[k]) for k in chains]
+        change = [mm(p_ref[...], jnp.clip(misfit[k], -1.0, 1.0).astype(BF16)) for k in chains]
+        series = [change[k] if step == 0 else series[k] + change[k] for k in chains]
+    series = jnp.concatenate(series, axis=1) * THRESHOLD
     tiles = series.shape[1] // LANES
     place = pl.program_id(0) * tiles
     if len(refs) == 1:
@@ -351,7 +350,8 @@
         m_ref[...] = keep[...].astype(BF16)
 
 
-WIDTH = 256
+WIDTH = 512
+CHAIN = 512
 
 
 def invert(sines, p, g, *other):
@@ -376,7 +376,12 @@
     )(sines, in_hbm(p), in_hbm(g), *(in_hbm(x) for x in other))
 
 
-def split3(x):
+def halves(table):
+    high = bf16(table)
+    return jnp.asarray(high), jnp.asarray(bf16(table - high.astype(np.float32)))
+
+
+def split2(x):
     high = x.astype(BF16)
     return high, (x - high.astype(F32)).astype(BF16)
 
@@ -407,14 +412,14 @@
         x = x.astype(BF16)
         smooth = mm(x, ch_ref[...]) + mm(x, cl_ref[...])
         smooth_ref[d] = smooth
-        low_ref[d] = smooth[:RADIUS]
-        high_ref[d] = smooth[rows - RADIUS :]
+        low_ref[d] = smooth[:RADIUS].astype(BF16)
+        high_ref[d] = smooth[rows - RADIUS :].astype(BF16)
 
 
 def gather(got, col_high, col_low, rows, cols):
     dates = got.shape[0] // 8 // HALF
     block = jax.ShapeDtypeStruct((dates, rows, cols), F32)
-    border = jax.ShapeDtypeStruct((dates, RADIUS, cols), F32)
+    border = jax.ShapeDtypeStruct((dates, RADIUS, cols), BF16)
     return pl.pallas_call(
         gather_kernel,
         out_shape=(block, block, border, border),
@@ -424,33 +429,72 @@
     )(got, col_high, col_low)
 
 
-def finish_kernel(where_ref, series_ref, smooth_ref, up_ref, dn_ref, rh_ref, rl_ref, corr_ref, atm_ref):
-    table = (rh_ref[0], rl_ref[0])
+def inner_kernel(where_ref, series_ref, smooth_ref, high_ref, low_ref, corr_ref, atm_ref):
+    table = (high_ref[0], low_ref[0])
     for d in range(series_ref.shape[0]):
-        x = jnp.concatenate([up_ref[d], smooth_ref[d], dn_ref[d]], axis=0)
-        atm = dot3(table, split3(x))
+        atm = dot3(table, split2(smooth_ref[d]))
         atm_ref[d] = atm
         corr_ref[d] = series_ref[d] - atm
 
 
-def finish(where, series, smooth, up, dn, row_high, row_low):
+def inner(where, series, smooth, high, low):
     dates, rows, cols = series.shape
     g = 5
     block = pl.BlockSpec((g, rows, cols), lambda i, w: (i, 0, 0))
-    halo = pl.BlockSpec((g, RADIUS, cols), lambda i, w: (i, 0, 0))
-    table = pl.BlockSpec((1,) + row_high.shape[1:], lambda i, w: (w[0], 0, 0))
-    return pl.pallas_call(
-        finish_kernel,
+    table = pl.BlockSpec((1,) + high.shape[1:], lambda i, w: (w[0], 0, 0))
+    return pl.pallas_call(
+        inner_kernel,
         grid_spec=pltpu.PrefetchScalarGridSpec(
             num_scalar_prefetch=1,
             grid=(dates // g,),
+            in_specs=[block, block, table, table],
+            out_specs=[block, block],
+        ),
+        out_shape=(pltpu.HBM((dates, rows, cols), F32),) * 2,
+        compiler_params=pltpu.CompilerParams(vmem_limit_bytes=24 << 20),
+        cost_estimate=pl.CostEstimate(
+            flops=dates * rows * cols * 1024, bytes_accessed=dates * rows * cols * 16, transcendentals=0
+        ),
+        name="inner",
+    )(where, series, smooth, high, low)
+
+
+def border_kernel(where_ref, corr_in, atm_in, up_ref, dn_ref, high_ref, low_ref, corr_ref, atm_ref):
+    def add(halo_ref):
+        for d in range(corr_in.shape[0]):
+            x = halo_ref[d]
+            more = mm(high_ref[0, 0], x) + mm(low_ref[0, 0], x)
+            atm_ref[d] = atm_in[d] + more
+            corr_ref[d] = corr_in[d] - more
+
+    @pl.when(pl.program_id(0) == 0)
+    def _():
+        add(up_ref)
+
+    @pl.when(pl.program_id(0) == 1)
+    def _():
+        add(dn_ref)
+
+
+def border(where, corrected, atmosphere, up, dn, high, low):
+    dates, rows, cols = corrected.shape
+    last = rows // RADIUS - 1
+    block = pl.BlockSpec((dates, RADIUS, cols), lambda i, w: (0, i * last, 0))
+    halo = pl.BlockSpec(up.shape, lambda i, w: (0, 0, 0))
+    table = pl.BlockSpec((1, 1) + high.shape[2:], lambda i, w: (w[0], i, 0, 0))
+    return pl.pallas_call(
+        border_kernel,
+        grid_spec=pltpu.PrefetchScalarGridSpec(
+            num_scalar_prefetch=1,
+            grid=(2,),
             in_specs=[block, block, halo, halo, table, table],
             out_specs=[block, block],
         ),
-        out_shape=(jax.ShapeDtypeStruct((dates, rows, cols), F32),) * 2,
-        compiler_params=pltpu.CompilerParams(vmem_limit_bytes=40 << 20),
-        name="finish",
-    )(where, series, smooth, up, dn, row_high, row_low)
+        out_shape=(pltpu.HBM((dates, rows, cols), F32),) * 2,
+        input_output_aliases={1: 0, 2: 1},
+        compiler_params=pltpu.CompilerParams(vmem_limit_bytes=24 << 20),
+        name="border",
+    )(where, in_hbm(corrected), in_hbm(atmosphere), up, dn, high, low)
 
 
 def neighbours(low_part, high_part, axis):
@@ -464,15 +508,15 @@
     n, rows, cols = ifg_real.shape
     rows_t, fwd, inv, back_up, back_dn = (jnp.asarray(t) for t in tables())
     col_t, row_t = blur_tables(rows * lax.axis_size("row"), rows, cols)
-    col_high, col_low = bf16(col_t), bf16(col_t - bf16(col_t).astype(np.float32))
-    row_high, row_low = bf16(row_t), bf16(row_t - bf16(row_t).astype(np.float32))
+    own = row_t[:, :, RADIUS : RADIUS + rows]
+    edges = np.stack([row_t[:, :RADIUS, :RADIUS], row_t[:, rows - RADIUS :, rows + RADIUS :]], axis=1)
+    where = lax.axis_index("row").astype(jnp.int32).reshape(1)
 
     low = jnp.stack([ifg_real[:, :HALF], ifg_imag[:, :HALF]])
     high = jnp.stack([ifg_real[:, rows - HALF :], ifg_imag[:, rows - HALF :]])
     above, below = neighbours(low, high, "row")
     u = centre(ifg_real, ifg_imag, rows_t, fwd, inv)
     p, g = projection(date_pairs)
-    u, p, g = lax.optimization_barrier((u, p, g))
     series = ()
     for upper, halo, back in ((True, above, back_up), (False, below, back_dn)):
         q = edge(upper, ifg_real, ifg_imag, halo, u, rows_t, fwd, inv, back)
@@ -482,12 +526,10 @@
     series = lax.all_to_all(
         series[0].reshape(devices, -1, LANES), "ifg", split_axis=0, concat_axis=0, tiled=True
     )
-    series, smooth, low, high = gather(
-        series.reshape(-1, LANES), jnp.asarray(col_high), jnp.asarray(col_low), rows, cols
-    )
+    series, smooth, low, high = gather(series.reshape(-1, LANES), *halves(col_t), rows, cols)
     up, dn = neighbours(low, high, "row")
-    where = lax.axis_index("row").astype(jnp.int32).reshape(1)
-    return finish(where, series, smooth, up, dn, jnp.asarray(row_high), jnp.asarray(row_low))
+    corrected, atmosphere = inner(where, series, smooth, *halves(own))
+    return tuple(border(where, corrected, atmosphere, up, dn, *halves(edges)))
 
 
 def solution(mesh):

time: 147 us -> 134 us (0.912)
  Pallas kernels: 71.2 us -> 60.4 us
  waiting for transfers between devices: 18.7 us -> 13.7 us
  blocking collectives: 17.1 us -> 20.9 us
  starting transfers between devices: 29.8 us -> 33 us
  local copies, waits for them, and re-layouts: 5.55 us -> 3.02 us
    all_to_all x2, waiting for transfers between devices: 13.3 us -> 1.68 us  [on_device(): sines = lax.all_to_all(q, 'ifg', split_axis=0, concat_axis=0, tiled=True)]
    ppermute x2, waiting for transfers between devices: 1.03 us -> 9.25 us  [neighbours(): lax.ppermute(high_part, axis, forward)]
    pallas_call x2, Pallas kernels: 30.1 us -> 24 us  [edge(): pl.pallas_call(lambda *refs: edge_kernel(upper, *refs), grid=(n // g,), i...]
    pallas_call x2, Pallas kernels: 15.3 us -> 10.4 us  [invert(): pl.pallas_call(invert_kernel, grid=(pixels // width,), in_specs=[pl.Block...]
    ppermute x2, starting transfers between devices: 7.45 us -> 11.3 us  [neighbours(): lax.ppermute(high_part, axis, forward)]
    all_to_all x1, blocking collectives: 17.1 us -> 20.9 us  [on_device(): lax.all_to_all(series[0].reshape(devices, -1, LANES), 'ifg', split_axis=0...]
    unnamed x25 -> x15, local copies, waits for them, and re-layouts: 2.78 us -> 0.25 us
    pallas_call x1 -> x2, Pallas kernels: 1.92 us -> 4.35 us  [the longest x1 2.43 us: border(): pl.pallas_call(border_kernel, grid_spec=pltpu.PrefetchScalarGridSpec(num_...]
  transfers between devices with their start and end apart: 6 -> 6, of which waited for: 4 -> 3; matrix products, arithmetic and copies ran while one was open for 1% -> 1% of each run, Pallas kernels for 40% -> 38%
where the time goes in v3:
time: 134 us
  Pallas kernels  60.4 us (45%)
  starting transfers between devices  33 us (25%)
  blocking collectives  20.9 us (16%)
  waiting for transfers between devices  13.7 us (10%)
  local copies, waits for them, and re-layouts  3.02 us (2%)
  other arithmetic  1.74 us (1%)
    pallas_call x2, Pallas kernels, edge(): pl.pallas_call(lambda *refs: edge_kernel(upper, *refs), grid=(n // g,), i...  24 us
    all_to_all x1, blocking collectives, on_device(): lax.all_to_all(series[0].reshape(devices, -1, LANES), 'ifg', split_axis=0...  20.9 us
    all_to_all x2, starting transfers between devices, on_device(): sines = lax.all_to_all(q, 'ifg', split_axis=0, concat_axis=0, tiled=True)  17.9 us
    ppermute x2, starting transfers between devices, neighbours(): lax.ppermute(high_part, axis, forward)  11.3 us
    pallas_call x2, Pallas kernels, invert(): pl.pallas_call(invert_kernel, grid=(pixels // width,), in_specs=[pl.Block...  10.4 us
    pallas_call x1, Pallas kernels, centre(): pl.pallas_call(centre_kernel, grid=(n // g,), in_specs=[block, block, who...  10.2 us
    pallas_call x1, Pallas kernels, projection(): pl.pallas_call(projection_kernel, out_shape=(pltpu.HBM((NDATES, nifg), BF...  9.38 us
    ppermute x2, waiting for transfers between devices, neighbours(): lax.ppermute(high_part, axis, forward)  9.25 us
  transfers between devices with their start and end apart: 6, of which 3 were waited for; matrix products, arithmetic and copies ran while one was open for 1% of the time, Pallas kernels for 38%

profile of v3, /device:TPU:1, one launch (start us, length us, event | category | flops | bytes accessed | tf_op | source)
XLA Modules:
  0.0 133.5 jit_solution(18086442661421181799)
XLA Ops:
  0.6 2.8 %slice_bitcast_fusion = (bf16[1,32,32,512]{3,2,1,0:T(8,128)(2,1)S(1)}, bf16[1,32,32,512]{3,2,1,0:T(8,128)(2,1)S(1)}, bf16[1,32,32,512]{3,2,1,0:T(8,128)(2,1)S(1)}, bf16[1,32,32,512]{3,2,1,0:T(8,128)(2,1)S(1)}) fusion(bf16[32,64,512]{2,1,0:T(8,128)(2,1)} %refs_1_.3, bf16[32,64,512]{2,1,0:T(8,128)(2,1)} %refs_0_.3), kind=kLoop, calls=%fused_computation.2 | loop fusion | bytes 8388608 | tf_op jit(solution)/shard_map/stack | solution.py:516
  3.4 0.2 pad_maximum_fusion.1
  3.6 4.9 %collective-permute-start.1 = (bf16[2,32,32,512]{3,2,1,0:T(8,128)(2,1)S(1)}, bf16[2,32,32,512]{3,2,1,0:T(8,128)(2,1)S(1)}, u32[]{:S(2)}, u32[]{:S(2)}) collective-permute-start(bf16[2,32,32,512]{3,2,1,0:T(8,128)(2,1)S(1)} %pad_maximum_fusion.1), channel_id=1, source_target_pairs={{0,1},{1,2},{2,3},{4,5},{5,6},{6,7},{8,9},{9,10},{10,11},{12,13},{... | collective-permute-start | bytes 6291464 | tf_op jit(solution)/shard_map/ppermute | solution.py:504
  8.6 1.5 %pad_maximum_fusion = bf16[2,32,32,512]{3,2,1,0:T(8,128)(2,1)} fusion(bf16[1,32,32,512]{3,2,1,0:T(8,128)(2,1)S(1)} %get-tuple-element.21, bf16[1,32,32,512]{3,2,1,0:T(8,128)(2,1)S(1)} %get-tuple-element.22), kind=kLoop, calls=%fused_computation | loop fusion | flops 1048576 | bytes 4194304 | tf_op jit(solution)/shard_map/stack | solution.py:515
  10.1 1.9 %collective-permute-start = (bf16[2,32,32,512]{3,2,1,0:T(8,128)(2,1)}, bf16[2,32,32,512]{3,2,1,0:T(8,128)(2,1)}, u32[]{:S(2)}, u32[]{:S(2)}) collective-permute-start(bf16[2,32,32,512]{3,2,1,0:T(8,128)(2,1)} %pad_maximum_fusion), channel_id=1, source_target_pairs={{1,0},{2,1},{3,2},{5,4},{6,5},{7,6},{9,8},{10,9},{11,10},{13,12},{... | collective-permute-start | bytes 6291464 | tf_op jit(solution)/shard_map/ppermute | solution.py:504
  12.0 10.2 %centre.1.refs_3_ = bf16[32,128,512]{2,1,0:T(8,128)(2,1)} custom-call(bf16[32,64,512]{2,1,0:T(8,128)(2,1)} %refs_0_.3, bf16[32,64,512]{2,1,0:T(8,128)(2,1)} %refs_1_.3, bf16[128,128]{1,0:T(8,128)(2,1)} %constant.26.clone.rows_ref.refs_4_, bf16[256,256]{1,0:T(8,128)(2,1)} %constant.27.clone.fwd_ref.refs_5_, bf16[256,256]{1,0:T(8,128)(2,1)} %constant.28.clone.inv_ref.refs_6_), custom_call_target="tpu_custom_call" | custom-call | flops 6979321856 | bytes 8388608 | tf_op jit(solution)/shard_map/centre/pallas_call | solution.py:146
  22.3 9.2 %collective-permute-done.1.refs_2_ = bf16[2,32,32,512]{3,2,1,0:T(8,128)(2,1)S(1)} collective-permute-done((bf16[2,32,32,512]{3,2,1,0:T(8,128)(2,1)S(1)}, bf16[2,32,32,512]{3,2,1,0:T(8,128)(2,1)S(1)}, u32[]{:S(2)}, u32[]{:S(2)}) %collective-permute-start.1) | collective-permute-done | bytes 2097184 | tf_op jit(solution)/shard_map/ppermute | solution.py:504
  31.5 11.9 %upper.1 = bf16[32,32,512]{2,1,0:T(8,128)(2,1)} custom-call(bf16[32,64,512]{2,1,0:T(8,128)(2,1)} %refs_0_.3, bf16[32,64,512]{2,1,0:T(8,128)(2,1)} %refs_1_.3, bf16[2,32,32,512]{3,2,1,0:T(8,128)(2,1)S(1)} %collective-permute-done.1.refs_2_, bf16[32,128,512]{2,1,0:T(8,128)(2,1)} %centre.1.refs_3_, bf16[128,128]{1,0:T(8,128)(2,1)} %constant.26.clone.rows_ref.refs_4_, ...), custom_call_target="tpu_custom_call" | custom-call | flops 8053063680 | bytes 7340032 | tf_op jit(solution)/shard_map/upper/pallas_call | solution.py:195
  43.4 10.2 %all-to-all-start.1 = ((bf16[32,32,512]{2,1,0:T(8,128)(2,1)}), bf16[32,32,512]{2,1,0:T(8,128)(2,1)S(1)}, u32[]{:S(2)}, u32[]{:S(2)}) async-start(bf16[32,32,512]{2,1,0:T(8,128)(2,1)} %upper.1), calls=%async_computation.1 | async-start | bytes 2097152 | tf_op jit(solution)/shard_map/all_to_all | solution.py:523
  53.6 0.2 copy.18.pairs_ref
  53.9 12.1 %lower.1 = bf16[32,32,512]{2,1,0:T(8,128)(2,1)} custom-call(bf16[32,64,512]{2,1,0:T(8,128)(2,1)} %refs_0_.3, bf16[32,64,512]{2,1,0:T(8,128)(2,1)} %refs_1_.3, bf16[2,32,32,512]{3,2,1,0:T(8,128)(2,1)} %collective-permute-done.refs_2_, bf16[32,128,512]{2,1,0:T(8,128)(2,1)} %centre.1.refs_3_, bf16[128,128]{1,0:T(8,128)(2,1)} %constant.26.clone.rows_ref.refs_4_, ...), custom_call_target="tpu_custom_call" | custom-call | flops 8053063680 | bytes 7340032 | tf_op jit(solution)/shard_map/lower/pallas_call | solution.py:195
  65.9 1.7 %all-to-all-done.1 = bf16[32,32,512]{2,1,0:T(8,128)(2,1)S(1)} async-done(((bf16[32,32,512]{2,1,0:T(8,128)(2,1)}), bf16[32,32,512]{2,1,0:T(8,128)(2,1)S(1)}, u32[]{:S(2)}, u32[]{:S(2)}) %all-to-all-start.1) | async-done | bytes 1048608 | tf_op jit(solution)/shard_map/all_to_all | solution.py:523
  67.6 7.8 %all-to-all-start = ((bf16[32,32,512]{2,1,0:T(8,128)(2,1)}), bf16[32,32,512]{2,1,0:T(8,128)(2,1)S(1)}, u32[]{:S(2)}, u32[]{:S(2)}) async-start(bf16[32,32,512]{2,1,0:T(8,128)(2,1)} %lower.1), calls=%async_computation | async-start | bytes 2097152 | tf_op jit(solution)/shard_map/all_to_all | solution.py:523
  75.4 9.4 %projection.1 = (bf16[320,1024]{1,0:T(8,128)(2,1)}, bf16[1024,640]{1,0:T(8,128)(2,1)}) custom-call(s32[1024,2]{1,0:T(8,128)S(1)} %copy.18.pairs_ref, s32[2,1024]{1,0:T(2,128)S(1)} %bitcast.18), custom_call_target="tpu_custom_call" | custom-call | flops 20000000000 | bytes 4000000 | tf_op jit(solution)/shard_map/projection/pallas_call | solution.py:300
  84.8 5.5 %invert.1.refs_0_ = f32[1280,128]{1,0:T(8,128)} custom-call(bf16[1024,512]{1,0:T(8,128)(2,1)S(1)} %bitcast.15, bf16[320,1024]{1,0:T(8,128)(2,1)} %get-tuple-element.10.p_ref, bf16[1024,640]{1,0:T(8,128)(2,1)} %get-tuple-element.11.g_ref), custom_call_target="tpu_custom_call" | custom-call | flops 2348810240 | bytes 6000000 | tf_op jit(solution)/shard_map/invert/pallas_call | solution.py:361
  90.2 5.0 %invert_rest.1 = bf16[2560,128]{1,0:T(8,128)(2,1)S(1)} custom-call(bf16[1024,512]{1,0:T(8,128)(2,1)S(1)} %bitcast.16, bf16[320,1024]{1,0:T(8,128)(2,1)} %get-tuple-element.10.p_ref, bf16[1024,640]{1,0:T(8,128)(2,1)} %get-tuple-element.11.g_ref, f32[1280,128]{1,0:T(8,128)} %invert.1.refs_0_), custom_call_target="tpu_custom_call" | custom-call | flops 2348810240 | bytes 6000000 | tf_op jit(solution)/shard_map/invert_rest/pallas_call | solution.py:361
  95.2 0.0 copy-start.2
  95.2 20.9 %all_to_all.15 = bf16[32,80,128]{2,1,0:T(8,128)(2,1)S(1)} all-to-all(bf16[32,80,128]{2,1,0:T(8,128)(2,1)S(1)} %bitcast.17), channel_id=1, replica_groups=mesh['ifg'=32,'row'=4] {'ifg'}, dimensions={0} | all-to-all | bytes 1310720 | tf_op jit(solution)/shard_map/all_to_all | solution.py:526
  116.1 2.0 %gather.1 = (f32[10,64,512]{2,1,0:T(8,128)S(1)}, f32[10,64,512]{2,1,0:T(8,128)S(1)}, bf16[10,16,512]{2,1,0:T(8,128)(2,1)S(1)}, bf16[10,16,512]{2,1,0:T(8,128)(2,1)S(1)}) custom-call(bf16[2560,128]{1,0:T(8,128)(2,1)S(1)} %bitcast.14, bf16[512,512]{1,0:T(8,128)(2,1)S(1)} %copy-done, bf16[512,512]{1,0:T(8,128)(2,1)S(1)} %copy-done.1), custom_call_target="tpu_custom_call" | custom-call | tf_op jit(solution)/shard_map/gather/pallas_call | solution.py:423
  118.1 6.3 %collective-permute-start.2 = (bf16[10,16,512]{2,1,0:T(8,128)(2,1)S(1)}, bf16[10,16,512]{2,1,0:T(8,128)(2,1)S(1)}, u32[]{:S(2)}, u32[]{:S(2)}) collective-permute-start(bf16[10,16,512]{2,1,0:T(8,128)(2,1)S(1)} %get-tuple-element.16), channel_id=1, source_target_pairs={{0,1},{1,2},{2,3},{4,5},{5,6},{6,7},{8,9},{9,10},{10,11},{12,13},{... | collective-permute-start | bytes 491528 | tf_op jit(solution)/shard_map/ppermute | solution.py:504
  124.4 1.9 %collective-permute-start.3 = (bf16[10,16,512]{2,1,0:T(8,128)(2,1)S(1)}, bf16[10,16,512]{2,1,0:T(8,128)(2,1)S(1)}, u32[]{:S(2)}, u32[]{:S(2)}) collective-permute-start(bf16[10,16,512]{2,1,0:T(8,128)(2,1)S(1)} %get-tuple-element.17), channel_id=1, source_target_pairs={{1,0},{2,1},{3,2},{5,4},{6,5},{7,6},{9,8},{10,9},{11,10},{13,12},{... | collective-permute-start | bytes 491528 | tf_op jit(solution)/shard_map/ppermute | solution.py:504
  126.4 1.9 %inner.1 = (f32[10,64,512]{2,1,0:T(8,128)}, f32[10,64,512]{2,1,0:T(8,128)}) custom-call(s32[1]{0:T(128)} %bitcast.where_ref, f32[10,64,512]{2,1,0:T(8,128)S(1)} %get-tuple-element.12.series_ref, f32[10,64,512]{2,1,0:T(8,128)S(1)} %get-tuple-element.13.smooth_ref, bf16[4,64,64]{2,1,0:T(8,128)(2,1)S(1)} %copy-done.2, bf16[4,64,64]{2,1,0:T(8,128)(2,1)S(1)} %copy-done.3), custom_call_target="tpu_custom_call" | custom-call | flops 335544320 | bytes 5242880 | tf_op jit(solution)/shard_map/inner/pallas_call | solution.py:445
  128.3 2.8 %collective-permute-done.3.dn_ref = bf16[10,16,512]{2,1,0:T(8,128)(2,1)S(1)} collective-permute-done((bf16[10,16,512]{2,1,0:T(8,128)(2,1)S(1)}, bf16[10,16,512]{2,1,0:T(8,128)(2,1)S(1)}, u32[]{:S(2)}, u32[]{:S(2)}) %collective-permute-start.3) | collective-permute-done | bytes 163872 | tf_op jit(solution)/shard_map/ppermute | solution.py:504
  131.1 2.4 %border.1 = (f32[10,64,512]{2,1,0:T(8,128)}, f32[10,64,512]{2,1,0:T(8,128)}) custom-call(s32[1]{0:T(128)} %bitcast.where_ref, f32[10,64,512]{2,1,0:T(8,128)} %get-tuple-element.14.corr_in, f32[10,64,512]{2,1,0:T(8,128)} %get-tuple-element.15.atm_in, ...), custom_call_target="tpu_custom_call", output_to_operand_aliasing={{0}: (1, {}), {1}: (2, {})} | custom-call | tf_op jit(solution)/shard_map/border/pallas_call | solution.py:485
  (16 shorter events, 0.0 us)
Async XLA Ops:
  3.6 27.9 %collective-permute-start.1 = (bf16[2,32,32,512]{3,2,1,0:T(8,128)(2,1)S(1)}, bf16[2,32,32,512]{3,2,1,0:T(8,128)(2,1)S(1)}, u32[]{:S(2)}, u32[]{:S(2)}) collective-permute-start(bf16[2,32,32,512]{3,2,1,0:T(8,128)(2,1)S(1)} %pad_maximum_fusion.1), channel_id=1, source_target_pairs={{0,1},{1,2},{2,3},{4,5},{5,6},{6,7},{8,9},{9,10},{10,11},{12,13},{... | collective-permute-start | bytes 6291464 | tf_op jit(solution)/shard_map/ppermute | solution.py:504
  10.1 43.8 %collective-permute-start = (bf16[2,32,32,512]{3,2,1,0:T(8,128)(2,1)}, bf16[2,32,32,512]{3,2,1,0:T(8,128)(2,1)}, u32[]{:S(2)}, u32[]{:S(2)}) collective-permute-start(bf16[2,32,32,512]{3,2,1,0:T(8,128)(2,1)} %pad_maximum_fusion), channel_id=1, source_target_pairs={{1,0},{2,1},{3,2},{5,4},{6,5},{7,6},{9,8},{10,9},{11,10},{13,12},{... | collective-permute-start | bytes 6291464 | tf_op jit(solution)/shard_map/ppermute | solution.py:504
  43.4 10.2 %copy-start.6 = (s32[1024,2]{0,1:T(2,128)S(1)}, s32[1024,2]{0,1:T(2,128)}, u32[]{:S(2)}) copy-start(s32[1024,2]{0,1:T(2,128)} %param.16) | copy-start | bytes 24580
  43.4 24.2 %all-to-all-start.1 = ((bf16[32,32,512]{2,1,0:T(8,128)(2,1)}), bf16[32,32,512]{2,1,0:T(8,128)(2,1)S(1)}, u32[]{:S(2)}, u32[]{:S(2)}) async-start(bf16[32,32,512]{2,1,0:T(8,128)(2,1)} %upper.1), calls=%async_computation.1 | async-start | bytes 2097152 | tf_op jit(solution)/shard_map/all_to_all | solution.py:523
  67.6 22.6 %all-to-all-start = ((bf16[32,32,512]{2,1,0:T(8,128)(2,1)}), bf16[32,32,512]{2,1,0:T(8,128)(2,1)S(1)}, u32[]{:S(2)}, u32[]{:S(2)}) async-start(bf16[32,32,512]{2,1,0:T(8,128)(2,1)} %lower.1), calls=%async_computation | async-start | bytes 2097152 | tf_op jit(solution)/shard_map/all_to_all | solution.py:523
  90.2 25.9 %copy-start = (bf16[512,512]{1,0:T(8,128)(2,1)S(1)}, bf16[512,512]{1,0:T(8,128)(2,1)}, u32[]{:S(2)}) copy-start(bf16[512,512]{1,0:T(8,128)(2,1)} %constant.31.clone.ch_ref) | copy-start | bytes 1572868
  90.2 25.9 %copy-start.1 = (bf16[512,512]{1,0:T(8,128)(2,1)S(1)}, bf16[512,512]{1,0:T(8,128)(2,1)}, u32[]{:S(2)}) copy-start(bf16[512,512]{1,0:T(8,128)(2,1)} %constant.32.clone.cl_ref) | copy-start | bytes 1572868
  95.2 31.2 %copy-start.2 = (bf16[4,64,64]{2,1,0:T(8,128)(2,1)S(1)}, bf16[4,64,64]{2,1,0:T(8,128)(2,1)}, u32[]{:S(2)}) copy-start(bf16[4,64,64]{2,1,0:T(8,128)(2,1)} %constant.33.clone.high_ref) | copy-start | bytes 98308
  95.2 31.1 %copy-start.3 = (bf16[4,64,64]{2,1,0:T(8,128)(2,1)S(1)}, bf16[4,64,64]{2,1,0:T(8,128)(2,1)}, u32[]{:S(2)}) copy-start(bf16[4,64,64]{2,1,0:T(8,128)(2,1)} %constant.34.clone.low_ref) | copy-start | bytes 98308
  116.1 15.0 %copy-start.4 = (bf16[4,2,16,16]{3,2,1,0:T(8,128)(2,1)S(1)}, bf16[4,2,16,16]{3,2,1,0:T(8,128)(2,1)}, u32[]{:S(2)}) copy-start(bf16[4,2,16,16]{3,2,1,0:T(8,128)(2,1)} %constant.35.clone.high_ref) | copy-start | bytes 12292
  116.1 15.0 %copy-start.5 = (bf16[4,2,16,16]{3,2,1,0:T(8,128)(2,1)S(1)}, bf16[4,2,16,16]{3,2,1,0:T(8,128)(2,1)}, u32[]{:S(2)}) copy-start(bf16[4,2,16,16]{3,2,1,0:T(8,128)(2,1)} %constant.36.clone.low_ref) | copy-start | bytes 12292
  118.1 10.2 %collective-permute-start.2 = (bf16[10,16,512]{2,1,0:T(8,128)(2,1)S(1)}, bf16[10,16,512]{2,1,0:T(8,128)(2,1)S(1)}, u32[]{:S(2)}, u32[]{:S(2)}) collective-permute-start(bf16[10,16,512]{2,1,0:T(8,128)(2,1)S(1)} %get-tuple-element.16), channel_id=1, source_target_pairs={{0,1},{1,2},{2,3},{4,5},{5,6},{6,7},{8,9},{9,10},{10,11},{12,13},{... | collective-permute-start | bytes 491528 | tf_op jit(solution)/shard_map/ppermute | solution.py:504
  124.4 6.6 %collective-permute-start.3 = (bf16[10,16,512]{2,1,0:T(8,128)(2,1)S(1)}, bf16[10,16,512]{2,1,0:T(8,128)(2,1)S(1)}, u32[]{:S(2)}, u32[]{:S(2)}) collective-permute-start(bf16[10,16,512]{2,1,0:T(8,128)(2,1)S(1)} %get-tuple-element.17), channel_id=1, source_target_pairs={{1,0},{2,1},{3,2},{5,4},{6,5},{7,6},{9,8},{10,9},{11,10},{13,12},{... | collective-permute-start | bytes 491528 | tf_op jit(solution)/shard_map/ppermute | solution.py:504

commit v4 on v3

--- a/solution.py
+++ b/solution.py
@@ -117,7 +117,8 @@
     return y_re, y_im
 
 
-def centre_kernel(re_ref, im_ref, rows_ref, fwd_ref, inv_ref, u_ref):
+def centre_kernel(re_ref, im_ref, rows_ref, fwd_ref, inv_ref, *refs):
+    u_ref = refs[-1]
     n = re_ref.shape[0]
     strips = [jnp.concatenate([re_ref[i], im_ref[i]], axis=0) for i in range(n)]
     y_re, y_im = stacked_rows(rows_ref[...], strips)
@@ -139,14 +140,15 @@
     return pl.BlockSpec(a.shape, lambda i: (0,) * a.ndim)
 
 
-def centre(re, im, rows_t, fwd, inv):
+def centre(re, im, rows_t, fwd, inv, *after):
     n, rows, cols = re.shape
     g = BATCH
     block = pl.BlockSpec((g, rows, cols), lambda i: (i, 0, 0))
     return pl.pallas_call(
         centre_kernel,
         grid=(n // g,),
-        in_specs=[block, block, whole(rows_t), whole(fwd), whole(inv)],
+        in_specs=[block, block, whole(rows_t), whole(fwd), whole(inv),
+                  *(pl.BlockSpec(memory_space=pl.ANY) for _ in after)],
         out_specs=pl.BlockSpec((g, 2 * rows, cols), lambda i: (i, 0, 0)),
         out_shape=pltpu.HBM((n, 2 * rows, cols), BF16),
         compiler_params=pltpu.CompilerParams(vmem_limit_bytes=24 << 20),
@@ -155,13 +157,35 @@
             transcendentals=n * 64 * 2304,
         ),
         name="centre",
-    )(*(in_hbm(x) for x in (re, im, rows_t, fwd, inv)))
+    )(*(in_hbm(x) for x in (re, im, rows_t, fwd, inv)), *after)
+
+
+def pack_kernel(re_ref, im_ref, *refs):
+    out_ref = refs[-1]
+    out_ref[0] = re_ref[...]
+    out_ref[1] = im_ref[...]
+
+
+def pack(re, im, side, first, count, *after):
+    n, rows, cols = re.shape
+    g = BATCH
+    block = pl.BlockSpec((g, HALF, cols), lambda i: (first // g + i, side, 0))
+    return pl.pallas_call(
+        pack_kernel,
+        grid=(count // g,),
+        in_specs=[block, block, *(pl.BlockSpec(memory_space=pl.ANY) for _ in after)],
+        out_specs=pl.BlockSpec((2, g, HALF, cols), lambda i: (0, i, 0, 0)),
+        out_shape=jax.ShapeDtypeStruct((2, count, HALF, cols), BF16),
+        compiler_params=pltpu.CompilerParams(vmem_limit_bytes=16 << 20),
+        name="pack",
+    )(in_hbm(re), in_hbm(im), *after)
 
 
 GROUP = 16
 
 
-def edge_kernel(upper, re_ref, im_ref, halo_ref, u_ref, rows_ref, fwd_ref, inv_ref, back_ref, q_ref, keep):
+def edge_kernel(upper, re_ref, im_ref, halo_ref, u_ref, rows_ref, fwd_ref, inv_ref, back_ref, *refs):
+    q_ref, keep = refs[-2:]
     g = re_ref.shape[0]
     part = pl.program_id(0) % (GROUP // g)
     strips = []
@@ -187,28 +211,33 @@
             q_ref[:, :, t * LANES : (t + 1) * LANES] = block.reshape(HALF, GROUP, LANES)
 
 
-def edge(upper, re, im, halo, u, rows_t, fwd, inv, back):
+def edge(upper, first, re, im, halo, u, rows_t, fwd, inv, back, *done):
     n, rows, cols = re.shape
     g = BATCH
     side = 0 if upper else 1
-    block = pl.BlockSpec((g, HALF, cols), lambda i: (i, side, 0))
+    at = first // g
+    block = pl.BlockSpec((g, HALF, cols), lambda i: (at + i, side, 0))
+    operands = [re, im, halo, u, rows_t, fwd, inv, back]
     return pl.pallas_call(
         lambda *refs: edge_kernel(upper, *refs),
-        grid=(n // g,),
+        grid=(halo.shape[1] // g,),
         in_specs=[block, block,
                   pl.BlockSpec((2, g, HALF, cols), lambda i: (0, i, 0, 0)),
-                  pl.BlockSpec((g, 2 * rows, cols), lambda i: (i, 0, 0)),
-                  whole(rows_t), whole(fwd), whole(inv), whole(back)],
-        out_specs=pl.BlockSpec((HALF, GROUP, cols), lambda i: (0, i // (GROUP // g), 0)),
+                  pl.BlockSpec((g, 2 * rows, cols), lambda i: (at + i, 0, 0)),
+                  *(whole(x) for x in operands[4:]),
+                  *(pl.BlockSpec(memory_space=pl.ANY) for _ in done)],
+        out_specs=pl.BlockSpec((HALF, GROUP, cols), lambda i: (0, (first + i * g) // GROUP, 0)),
         out_shape=pltpu.HBM((HALF, n, cols), BF16),
         scratch_shapes=[pltpu.VMEM((cols // LANES, HALF * GROUP, LANES), F32)],
+        input_output_aliases={len(operands): 0} if done else {},
         compiler_params=pltpu.CompilerParams(vmem_limit_bytes=24 << 20),
         cost_estimate=pl.CostEstimate(
-            flops=n * 2 * 64 * 256 * 256 * 30, bytes_accessed=n * rows * cols * 7,
-            transcendentals=n * 64 * 2304,
+            flops=halo.shape[1] * 2 * 64 * 256 * 256 * 30,
+            bytes_accessed=halo.shape[1] * rows * cols * 7,
+            transcendentals=halo.shape[1] * 64 * 2304,
         ),
         name="upper" if upper else "lower",
-    )(in_hbm(re), in_hbm(im), halo, *(in_hbm(x) for x in (u, rows_t, fwd, inv, back)))
+    )(*(x if x is halo else in_hbm(x) for x in operands), *(in_hbm(x) for x in done))
 
 
 def projection_kernel(pairs_ref, pairs_t_ref, p_ref, g_ref, band, factor, solved):
@@ -512,15 +541,24 @@
     edges = np.stack([row_t[:, :RADIUS, :RADIUS], row_t[:, rows - RADIUS :, rows + RADIUS :]], axis=1)
     where = lax.axis_index("row").astype(jnp.int32).reshape(1)
 
-    low = jnp.stack([ifg_real[:, :HALF], ifg_imag[:, :HALF]])
-    high = jnp.stack([ifg_real[:, rows - HALF :], ifg_imag[:, rows - HALF :]])
-    above, below = neighbours(low, high, "row")
-    u = centre(ifg_real, ifg_imag, rows_t, fwd, inv)
+    count = lax.axis_size("row")
+    onward = [(i, i + 1) for i in range(count - 1)]
+    back = [(b, a) for a, b in onward]
+    packed = pack(ifg_real, ifg_imag, 1, 0, n // 2)
+    above = [lax.ppermute(packed, "row", onward)]
+    packed = pack(ifg_real, ifg_imag, 1, n // 2, n // 2, packed)
+    above += [lax.ppermute(packed, "row", onward)]
+    packed = pack(ifg_real, ifg_imag, 0, 0, n, packed)
+    below = lax.ppermute(packed, "row", back)
+    u = centre(ifg_real, ifg_imag, rows_t, fwd, inv, packed)
     p, g = projection(date_pairs)
+    q = ()
+    for k, halo in enumerate(above):
+        q = (edge(True, k * (n // 2), ifg_real, ifg_imag, halo, u, rows_t, fwd, inv, back_up, *q),)
+    lower = edge(False, 0, ifg_real, ifg_imag, below, u, rows_t, fwd, inv, back_dn)
     series = ()
-    for upper, halo, back in ((True, above, back_up), (False, below, back_dn)):
-        q = edge(upper, ifg_real, ifg_imag, halo, u, rows_t, fwd, inv, back)
-        sines = lax.all_to_all(q, "ifg", split_axis=0, concat_axis=0, tiled=True)
+    for part in (*q, lower):
+        sines = lax.all_to_all(part, "ifg", split_axis=0, concat_axis=0, tiled=True)
         series = (invert(sines.reshape(-1, cols), p, g, *series),)
     devices = lax.axis_size("ifg")
     series = lax.all_to_all(

time: 134 us -> 134 us (level)
  Pallas kernels: 60.4 us -> 67.4 us
  waiting for transfers between devices: 13.7 us -> 11.6 us
  local copies, waits for them, and re-layouts: 3.02 us -> 1.08 us
  other arithmetic: 1.74 us -> 0 us
    ppermute x0 -> x3, starting transfers between devices: none -> 10.6 us  [the longest x1 3.75 us: on_device(): above += [lax.ppermute(packed, 'row', onward)]]
    ppermute x2 -> x1, waiting for transfers between devices: 9.25 us -> 0.01 us  [neighbours(): lax.ppermute(high_part, axis, forward)]
    pallas_call x2 -> x6, Pallas kernels: 24 us -> 31.2 us  [the longest x3 26.1 us: edge(): pl.pallas_call(lambda *refs: edge_kernel(upper, *refs), grid=(halo.shape[...]
    ppermute x2 -> x1, starting transfers between devices: 11.3 us -> 4.1 us  [neighbours(): lax.ppermute(high_part, axis, forward)]
    all_to_all x2, waiting for transfers between devices: 1.68 us -> 6.97 us  [on_device(): sines = lax.all_to_all(part, 'ifg', split_axis=0, concat_axis=0, tiled=True)]
    another operation x1 -> x0, local copies, waits for them, and re-layouts: 2.77 us -> none  [on_device(): high = jnp.stack([ifg_real[:, rows - HALF:], ifg_imag[:, rows - HALF:]])]
    all_to_all x2, starting transfers between devices: 17.9 us -> 15.7 us  [on_device(): sines = lax.all_to_all(part, 'ifg', split_axis=0, concat_axis=0, tiled=True)]
    ppermute x0 -> x3, waiting for transfers between devices: none -> 1.93 us  [the longest x1 1.92 us: on_device(): above += [lax.ppermute(packed, 'row', onward)]]
  transfers between devices with their start and end apart: 6 -> 7, of which waited for: 3 -> 4; matrix products, arithmetic and copies ran while one was open for 1% -> 1% of each run, Pallas kernels for 38% -> 40%
where the time goes in v4:
time: 134 us
  Pallas kernels  67.4 us (50%)
  starting transfers between devices  32.3 us (24%)
  blocking collectives  20.2 us (15%)
  waiting for transfers between devices  11.6 us (9%)
    pallas_call x3, Pallas kernels, edge(): pl.pallas_call(lambda *refs: edge_kernel(upper, *refs), grid=(halo.shape[...  26.1 us
    all_to_all x1, blocking collectives, on_device(): lax.all_to_all(series[0].reshape(devices, -1, LANES), 'ifg', split_axis=0...  20.2 us
    all_to_all x2, starting transfers between devices, on_device(): sines = lax.all_to_all(part, 'ifg', split_axis=0, concat_axis=0, tiled=True)  15.7 us
    pallas_call x2, Pallas kernels, invert(): pl.pallas_call(invert_kernel, grid=(pixels // width,), in_specs=[pl.Block...  10.3 us
    pallas_call x1, Pallas kernels, centre(): pl.pallas_call(centre_kernel, grid=(n // g,), in_specs=[block, block, who...  10.2 us
    pallas_call x1, Pallas kernels, projection(): pl.pallas_call(projection_kernel, out_shape=(pltpu.HBM((NDATES, nifg), BF...  9.37 us
    all_to_all x2, waiting for transfers between devices, on_device(): sines = lax.all_to_all(part, 'ifg', split_axis=0, concat_axis=0, tiled=True)  6.97 us
    pallas_call x3, Pallas kernels, pack(): pl.pallas_call(pack_kernel, grid=(count // g,), in_specs=[block, block, *...  5.06 us
  transfers between devices with their start and end apart: 7, of which 4 were waited for; matrix products, arithmetic and copies ran while one was open for 1% of the time, Pallas kernels for 40%

profile of v4, /device:TPU:1, one launch (start us, length us, event | category | flops | bytes accessed | tf_op | source)
XLA Modules:
  0.0 133.5 jit_solution(13900459992642039420)
XLA Ops:
  1.9 1.3 pack.4.refs_0_
  3.3 2.4 %pack.5.refs_0_ = bf16[2,32,32,512]{3,2,1,0:T(8,128)(2,1)S(1)} custom-call(bf16[32,64,512]{2,1,0:T(8,128)(2,1)} %refs_0_.5, bf16[32,64,512]{2,1,0:T(8,128)(2,1)} %refs_1_.5, bf16[2,16,32,512]{3,2,1,0:T(8,128)(2,1)S(1)} %pack.4.refs_0_), custom_call_target="tpu_custom_call" | custom-call | tf_op jit(solution)/shard_map/pack/pallas_call | solution.py:173
  5.7 3.3 %collective-permute-start = (bf16[2,32,32,512]{3,2,1,0:T(8,128)(2,1)S(1)}, bf16[2,32,32,512]{3,2,1,0:T(8,128)(2,1)}, u32[]{:S(2)}, u32[]{:S(2)}) collective-permute-start(bf16[2,32,32,512]{3,2,1,0:T(8,128)(2,1)S(1)} %pack.5.refs_0_), channel_id=1, source_target_pairs={{1,0},{2,1},{3,2},{5,4},{6,5},{7,6},{9,8},{10,9},{11,10},{13,12},{... | collective-permute-start | bytes 6291464 | tf_op jit(solution)/shard_map/ppermute | solution.py:552
  9.0 3.5 %collective-permute-start.2 = (bf16[2,16,32,512]{3,2,1,0:T(8,128)(2,1)S(1)}, bf16[2,16,32,512]{3,2,1,0:T(8,128)(2,1)S(1)}, u32[]{:S(2)}, u32[]{:S(2)}) collective-permute-start(bf16[2,16,32,512]{3,2,1,0:T(8,128)(2,1)S(1)} %pack.3.refs_0_), channel_id=1, source_target_pairs={{0,1},{1,2},{2,3},{4,5},{5,6},{6,7},{8,9},{9,10},{10,11},{12,13},{... | collective-permute-start | bytes 3145736 | tf_op jit(solution)/shard_map/ppermute | solution.py:548
  12.6 3.7 %collective-permute-start.1 = (bf16[2,16,32,512]{3,2,1,0:T(8,128)(2,1)S(1)}, bf16[2,16,32,512]{3,2,1,0:T(8,128)(2,1)S(1)}, u32[]{:S(2)}, u32[]{:S(2)}) collective-permute-start(bf16[2,16,32,512]{3,2,1,0:T(8,128)(2,1)S(1)} %pack.4.refs_0_), channel_id=1, source_target_pairs={{0,1},{1,2},{2,3},{4,5},{5,6},{6,7},{8,9},{9,10},{10,11},{12,13},{... | collective-permute-start | bytes 3145736 | tf_op jit(solution)/shard_map/ppermute | solution.py:550
  16.3 10.2 %centre.1.refs_3_ = bf16[32,128,512]{2,1,0:T(8,128)(2,1)} custom-call(bf16[32,64,512]{2,1,0:T(8,128)(2,1)} %refs_0_.5, bf16[32,64,512]{2,1,0:T(8,128)(2,1)} %refs_1_.5, bf16[128,128]{1,0:T(8,128)(2,1)} %constant.26.clone.rows_ref.refs_4_, bf16[256,256]{1,0:T(8,128)(2,1)} %constant.27.clone.fwd_ref.refs_5_, bf16[256,256]{1,0:T(8,128)(2,1)} %constant.28.clone.inv_ref.refs_6_, ...), custom_call_target="tpu_custom_call" | custom-call | flops 6979321856 | bytes 8388608 | tf_op jit(solution)/shard_map/centre/pallas_call | solution.py:147
  26.6 7.0 %upper.2.refs_8_ = bf16[32,32,512]{2,1,0:T(8,128)(2,1)} custom-call(bf16[32,64,512]{2,1,0:T(8,128)(2,1)} %refs_0_.5, bf16[32,64,512]{2,1,0:T(8,128)(2,1)} %refs_1_.5, bf16[2,16,32,512]{3,2,1,0:T(8,128)(2,1)S(1)} %collective-permute-done.2.refs_2_, bf16[32,128,512]{2,1,0:T(8,128)(2,1)} %centre.1.refs_3_, bf16[128,128]{1,0:T(8,128)(2,1)} %constant.26.clone.rows_ref.refs_4_, ...), custom_call_target="tpu_custom_call" | custom-call | flops 4026531840 | bytes 3670016 | tf_op jit(solution)/shard_map/upper/pallas_call | solution.py:221
  33.6 1.9 %collective-permute-done.1.refs_2_ = bf16[2,16,32,512]{3,2,1,0:T(8,128)(2,1)S(1)} collective-permute-done((bf16[2,16,32,512]{3,2,1,0:T(8,128)(2,1)S(1)}, bf16[2,16,32,512]{3,2,1,0:T(8,128)(2,1)S(1)}, u32[]{:S(2)}, u32[]{:S(2)}) %collective-permute-start.1) | collective-permute-done | bytes 1048608 | tf_op jit(solution)/shard_map/ppermute | solution.py:550
  35.5 7.0 %upper.3 = bf16[32,32,512]{2,1,0:T(8,128)(2,1)} custom-call(bf16[32,64,512]{2,1,0:T(8,128)(2,1)} %refs_0_.5, bf16[32,64,512]{2,1,0:T(8,128)(2,1)} %refs_1_.5, bf16[2,16,32,512]{3,2,1,0:T(8,128)(2,1)S(1)} %collective-permute-done.1.refs_2_, bf16[32,128,512]{2,1,0:T(8,128)(2,1)} %centre.1.refs_3_, ...), custom_call_target="tpu_custom_call", output_to_operand_aliasing={{}: (8, {})} | custom-call | flops 4026531840 | bytes 3670016 | tf_op jit(solution)/shard_map/upper/pallas_call | solution.py:221
  42.6 10.2 %all-to-all-start.1 = ((bf16[32,32,512]{2,1,0:T(8,128)(2,1)}), bf16[32,32,512]{2,1,0:T(8,128)(2,1)S(1)}, u32[]{:S(2)}, u32[]{:S(2)}) async-start(bf16[32,32,512]{2,1,0:T(8,128)(2,1)} %upper.3), calls=%async_computation.1 | async-start | bytes 2097152 | tf_op jit(solution)/shard_map/all_to_all | solution.py:561
  53.8 12.1 %lower.1 = bf16[32,32,512]{2,1,0:T(8,128)(2,1)} custom-call(bf16[32,64,512]{2,1,0:T(8,128)(2,1)} %refs_0_.5, bf16[32,64,512]{2,1,0:T(8,128)(2,1)} %refs_1_.5, bf16[2,32,32,512]{3,2,1,0:T(8,128)(2,1)} %collective-permute-done.refs_2_, bf16[32,128,512]{2,1,0:T(8,128)(2,1)} %centre.1.refs_3_, bf16[128,128]{1,0:T(8,128)(2,1)} %constant.26.clone.rows_ref.refs_4_, ...), custom_call_target="tpu_custom_call" | custom-call | flops 8053063680 | bytes 7340032 | tf_op jit(solution)/shard_map/lower/pallas_call | solution.py:221
  65.9 4.1 %all-to-all-done.1 = bf16[32,32,512]{2,1,0:T(8,128)(2,1)S(1)} async-done(((bf16[32,32,512]{2,1,0:T(8,128)(2,1)}), bf16[32,32,512]{2,1,0:T(8,128)(2,1)S(1)}, u32[]{:S(2)}, u32[]{:S(2)}) %all-to-all-start.1) | async-done | bytes 1048608 | tf_op jit(solution)/shard_map/all_to_all | solution.py:561
  70.0 5.5 %all-to-all-start = ((bf16[32,32,512]{2,1,0:T(8,128)(2,1)}), bf16[32,32,512]{2,1,0:T(8,128)(2,1)S(1)}, u32[]{:S(2)}, u32[]{:S(2)}) async-start(bf16[32,32,512]{2,1,0:T(8,128)(2,1)} %lower.1), calls=%async_computation | async-start | bytes 2097152 | tf_op jit(solution)/shard_map/all_to_all | solution.py:561
  75.5 9.4 %projection.1 = (bf16[320,1024]{1,0:T(8,128)(2,1)}, bf16[1024,640]{1,0:T(8,128)(2,1)}) custom-call(s32[1024,2]{1,0:T(8,128)S(1)} %copy-done.2, s32[2,1024]{1,0:T(2,128)S(1)} %bitcast.10), custom_call_target="tpu_custom_call" | custom-call | flops 20000000000 | bytes 4000000 | tf_op jit(solution)/shard_map/projection/pallas_call | solution.py:329
  84.8 5.5 %invert.1.refs_0_ = f32[1280,128]{1,0:T(8,128)} custom-call(bf16[1024,512]{1,0:T(8,128)(2,1)S(1)} %bitcast.7, bf16[320,1024]{1,0:T(8,128)(2,1)} %get-tuple-element.10.p_ref, bf16[1024,640]{1,0:T(8,128)(2,1)} %get-tuple-element.11.g_ref), custom_call_target="tpu_custom_call" | custom-call | flops 2348810240 | bytes 6000000 | tf_op jit(solution)/shard_map/invert/pallas_call | solution.py:390
  90.3 2.9 %all-to-all-done = bf16[32,32,512]{2,1,0:T(8,128)(2,1)S(1)} async-done(((bf16[32,32,512]{2,1,0:T(8,128)(2,1)}), bf16[32,32,512]{2,1,0:T(8,128)(2,1)S(1)}, u32[]{:S(2)}, u32[]{:S(2)}) %all-to-all-start) | async-done | bytes 1048608 | tf_op jit(solution)/shard_map/all_to_all | solution.py:561
  93.2 4.9 %invert_rest.1 = bf16[2560,128]{1,0:T(8,128)(2,1)S(1)} custom-call(bf16[1024,512]{1,0:T(8,128)(2,1)S(1)} %bitcast.8, bf16[320,1024]{1,0:T(8,128)(2,1)} %get-tuple-element.10.p_ref, bf16[1024,640]{1,0:T(8,128)(2,1)} %get-tuple-element.11.g_ref, f32[1280,128]{1,0:T(8,128)} %invert.1.refs_0_), custom_call_target="tpu_custom_call" | custom-call | flops 2348810240 | bytes 6000000 | tf_op jit(solution)/shard_map/invert_rest/pallas_call | solution.py:390
  98.1 20.2 %all_to_all.15 = bf16[32,80,128]{2,1,0:T(8,128)(2,1)S(1)} all-to-all(bf16[32,80,128]{2,1,0:T(8,128)(2,1)S(1)} %bitcast.9), channel_id=1, replica_groups=mesh['ifg'=32,'row'=4] {'ifg'}, dimensions={0} | all-to-all | bytes 1310720 | tf_op jit(solution)/shard_map/all_to_all | solution.py:564
  118.3 2.0 %gather.1 = (f32[10,64,512]{2,1,0:T(8,128)S(1)}, f32[10,64,512]{2,1,0:T(8,128)S(1)}, bf16[10,16,512]{2,1,0:T(8,128)(2,1)S(1)}, bf16[10,16,512]{2,1,0:T(8,128)(2,1)S(1)}) custom-call(bf16[2560,128]{1,0:T(8,128)(2,1)S(1)} %bitcast.6, bf16[512,512]{1,0:T(8,128)(2,1)S(1)} %copy-done, bf16[512,512]{1,0:T(8,128)(2,1)S(1)} %copy-done.1), custom_call_target="tpu_custom_call" | custom-call | tf_op jit(solution)/shard_map/gather/pallas_call | solution.py:452
  120.3 4.1 %collective-permute-start.3 = (bf16[10,16,512]{2,1,0:T(8,128)(2,1)S(1)}, bf16[10,16,512]{2,1,0:T(8,128)(2,1)S(1)}, u32[]{:S(2)}, u32[]{:S(2)}) collective-permute-start(bf16[10,16,512]{2,1,0:T(8,128)(2,1)S(1)} %get-tuple-element.16), channel_id=1, source_target_pairs={{0,1},{1,2},{2,3},{4,5},{5,6},{6,7},{8,9},{9,10},{10,11},{12,13},{... | collective-permute-start | bytes 491528 | tf_op jit(solution)/shard_map/ppermute | solution.py:533
  124.4 1.9 %collective-permute-start.4 = (bf16[10,16,512]{2,1,0:T(8,128)(2,1)S(1)}, bf16[10,16,512]{2,1,0:T(8,128)(2,1)S(1)}, u32[]{:S(2)}, u32[]{:S(2)}) collective-permute-start(bf16[10,16,512]{2,1,0:T(8,128)(2,1)S(1)} %get-tuple-element.17), channel_id=1, source_target_pairs={{1,0},{2,1},{3,2},{5,4},{6,5},{7,6},{9,8},{10,9},{11,10},{13,12},{... | collective-permute-start | bytes 491528 | tf_op jit(solution)/shard_map/ppermute | solution.py:533
  126.4 1.9 %inner.1 = (f32[10,64,512]{2,1,0:T(8,128)}, f32[10,64,512]{2,1,0:T(8,128)}) custom-call(s32[1]{0:T(128)} %bitcast.where_ref, f32[10,64,512]{2,1,0:T(8,128)S(1)} %get-tuple-element.12.series_ref, f32[10,64,512]{2,1,0:T(8,128)S(1)} %get-tuple-element.13.smooth_ref, bf16[4,64,64]{2,1,0:T(8,128)(2,1)S(1)} %copy-done.3, bf16[4,64,64]{2,1,0:T(8,128)(2,1)S(1)} %copy-done.4), custom_call_target="tpu_custom_call" | custom-call | flops 335544320 | bytes 5242880 | tf_op jit(solution)/shard_map/inner/pallas_call | solution.py:474
  128.3 2.7 %collective-permute-done.4.dn_ref = bf16[10,16,512]{2,1,0:T(8,128)(2,1)S(1)} collective-permute-done((bf16[10,16,512]{2,1,0:T(8,128)(2,1)S(1)}, bf16[10,16,512]{2,1,0:T(8,128)(2,1)S(1)}, u32[]{:S(2)}, u32[]{:S(2)}) %collective-permute-start.4) | collective-permute-done | bytes 163872 | tf_op jit(solution)/shard_map/ppermute | solution.py:533
  131.1 2.4 %border.1 = (f32[10,64,512]{2,1,0:T(8,128)}, f32[10,64,512]{2,1,0:T(8,128)}) custom-call(s32[1]{0:T(128)} %bitcast.where_ref, f32[10,64,512]{2,1,0:T(8,128)} %get-tuple-element.14.corr_in, f32[10,64,512]{2,1,0:T(8,128)} %get-tuple-element.15.atm_in, ...), custom_call_target="tpu_custom_call", output_to_operand_aliasing={{0}: (1, {}), {1}: (2, {})} | custom-call | tf_op jit(solution)/shard_map/border/pallas_call | solution.py:514
  (21 shorter events, 2.4 us)
Async XLA Ops:
  5.7 48.1 %collective-permute-start = (bf16[2,32,32,512]{3,2,1,0:T(8,128)(2,1)S(1)}, bf16[2,32,32,512]{3,2,1,0:T(8,128)(2,1)}, u32[]{:S(2)}, u32[]{:S(2)}) collective-permute-start(bf16[2,32,32,512]{3,2,1,0:T(8,128)(2,1)S(1)} %pack.5.refs_0_), channel_id=1, source_target_pairs={{1,0},{2,1},{3,2},{5,4},{6,5},{7,6},{9,8},{10,9},{11,10},{13,12},{... | collective-permute-start | bytes 6291464 | tf_op jit(solution)/shard_map/ppermute | solution.py:552
  9.0 17.5 %collective-permute-start.2 = (bf16[2,16,32,512]{3,2,1,0:T(8,128)(2,1)S(1)}, bf16[2,16,32,512]{3,2,1,0:T(8,128)(2,1)S(1)}, u32[]{:S(2)}, u32[]{:S(2)}) collective-permute-start(bf16[2,16,32,512]{3,2,1,0:T(8,128)(2,1)S(1)} %pack.3.refs_0_), channel_id=1, source_target_pairs={{0,1},{1,2},{2,3},{4,5},{5,6},{6,7},{8,9},{9,10},{10,11},{12,13},{... | collective-permute-start | bytes 3145736 | tf_op jit(solution)/shard_map/ppermute | solution.py:548
  12.6 23.0 %collective-permute-start.1 = (bf16[2,16,32,512]{3,2,1,0:T(8,128)(2,1)S(1)}, bf16[2,16,32,512]{3,2,1,0:T(8,128)(2,1)S(1)}, u32[]{:S(2)}, u32[]{:S(2)}) collective-permute-start(bf16[2,16,32,512]{3,2,1,0:T(8,128)(2,1)S(1)} %pack.4.refs_0_), channel_id=1, source_target_pairs={{0,1},{1,2},{2,3},{4,5},{5,6},{6,7},{8,9},{9,10},{10,11},{12,13},{... | collective-permute-start | bytes 3145736 | tf_op jit(solution)/shard_map/ppermute | solution.py:550
  42.6 10.2 %copy-start.7 = (s32[1024,2]{0,1:T(2,128)S(1)}, s32[1024,2]{0,1:T(2,128)}, u32[]{:S(2)}) copy-start(s32[1024,2]{0,1:T(2,128)} %param.16) | copy-start | bytes 24580
  42.6 27.4 %all-to-all-start.1 = ((bf16[32,32,512]{2,1,0:T(8,128)(2,1)}), bf16[32,32,512]{2,1,0:T(8,128)(2,1)S(1)}, u32[]{:S(2)}, u32[]{:S(2)}) async-start(bf16[32,32,512]{2,1,0:T(8,128)(2,1)} %upper.3), calls=%async_computation.1 | async-start | bytes 2097152 | tf_op jit(solution)/shard_map/all_to_all | solution.py:561
  65.9 9.6 %copy-start.2 = (s32[1024,2]{1,0:T(8,128)S(1)}, s32[1024,2]{1,0:T(8,128)}, u32[]{:S(2)}) copy-start(s32[1024,2]{1,0:T(8,128)} %copy.19.pairs_ref) | copy-start | bytes 24580
  70.0 23.2 %all-to-all-start = ((bf16[32,32,512]{2,1,0:T(8,128)(2,1)}), bf16[32,32,512]{2,1,0:T(8,128)(2,1)S(1)}, u32[]{:S(2)}, u32[]{:S(2)}) async-start(bf16[32,32,512]{2,1,0:T(8,128)(2,1)} %lower.1), calls=%async_computation | async-start | bytes 2097152 | tf_op jit(solution)/shard_map/all_to_all | solution.py:561
  98.1 20.3 %copy-start = (bf16[512,512]{1,0:T(8,128)(2,1)S(1)}, bf16[512,512]{1,0:T(8,128)(2,1)}, u32[]{:S(2)}) copy-start(bf16[512,512]{1,0:T(8,128)(2,1)} %constant.31.clone.ch_ref) | copy-start | bytes 1572868
  98.1 20.3 %copy-start.1 = (bf16[512,512]{1,0:T(8,128)(2,1)S(1)}, bf16[512,512]{1,0:T(8,128)(2,1)}, u32[]{:S(2)}) copy-start(bf16[512,512]{1,0:T(8,128)(2,1)} %constant.32.clone.cl_ref) | copy-start | bytes 1572868
  98.1 28.3 %copy-start.3 = (bf16[4,64,64]{2,1,0:T(8,128)(2,1)S(1)}, bf16[4,64,64]{2,1,0:T(8,128)(2,1)}, u32[]{:S(2)}) copy-start(bf16[4,64,64]{2,1,0:T(8,128)(2,1)} %constant.33.clone.high_ref) | copy-start | bytes 98308
  98.1 28.3 %copy-start.4 = (bf16[4,64,64]{2,1,0:T(8,128)(2,1)S(1)}, bf16[4,64,64]{2,1,0:T(8,128)(2,1)}, u32[]{:S(2)}) copy-start(bf16[4,64,64]{2,1,0:T(8,128)(2,1)} %constant.34.clone.low_ref) | copy-start | bytes 98308
  120.3 8.0 %collective-permute-start.3 = (bf16[10,16,512]{2,1,0:T(8,128)(2,1)S(1)}, bf16[10,16,512]{2,1,0:T(8,128)(2,1)S(1)}, u32[]{:S(2)}, u32[]{:S(2)}) collective-permute-start(bf16[10,16,512]{2,1,0:T(8,128)(2,1)S(1)} %get-tuple-element.16), channel_id=1, source_target_pairs={{0,1},{1,2},{2,3},{4,5},{5,6},{6,7},{8,9},{9,10},{10,11},{12,13},{... | collective-permute-start | bytes 491528 | tf_op jit(solution)/shard_map/ppermute | solution.py:533
  124.4 6.6 %collective-permute-start.4 = (bf16[10,16,512]{2,1,0:T(8,128)(2,1)S(1)}, bf16[10,16,512]{2,1,0:T(8,128)(2,1)S(1)}, u32[]{:S(2)}, u32[]{:S(2)}) collective-permute-start(bf16[10,16,512]{2,1,0:T(8,128)(2,1)S(1)} %get-tuple-element.17), channel_id=1, source_target_pairs={{1,0},{2,1},{3,2},{5,4},{6,5},{7,6},{9,8},{10,9},{11,10},{13,12},{... | collective-permute-start | bytes 491528 | tf_op jit(solution)/shard_map/ppermute | solution.py:533
  126.4 4.7 %copy-start.5 = (bf16[4,2,16,16]{3,2,1,0:T(8,128)(2,1)S(1)}, bf16[4,2,16,16]{3,2,1,0:T(8,128)(2,1)}, u32[]{:S(2)}) copy-start(bf16[4,2,16,16]{3,2,1,0:T(8,128)(2,1)} %constant.35.clone.high_ref) | copy-start | bytes 12292
  126.4 4.7 %copy-start.6 = (bf16[4,2,16,16]{3,2,1,0:T(8,128)(2,1)S(1)}, bf16[4,2,16,16]{3,2,1,0:T(8,128)(2,1)}, u32[]{:S(2)}) copy-start(bf16[4,2,16,16]{3,2,1,0:T(8,128)(2,1)} %constant.36.clone.low_ref) | copy-start | bytes 12292

commit v5 on v4

--- a/solution.py
+++ b/solution.py
@@ -160,25 +160,34 @@
     )(*(in_hbm(x) for x in (re, im, rows_t, fwd, inv)), *after)
 
 
-def pack_kernel(re_ref, im_ref, *refs):
-    out_ref = refs[-1]
-    out_ref[0] = re_ref[...]
-    out_ref[1] = im_ref[...]
-
-
-def pack(re, im, side, first, count, *after):
+def pack_kernel(re_ref, im_ref, *out_refs):
+    step, steps = pl.program_id(0), pl.num_programs(0)
+    for part in range(2):
+
+        @pl.when(step // (steps // 2) == part)
+        def _():
+            for side in range(2):
+                out_ref = out_refs[2 * side + part]
+                out_ref[0] = re_ref[:, side * HALF : (side + 1) * HALF]
+                out_ref[1] = im_ref[:, side * HALF : (side + 1) * HALF]
+
+
+def pack(re, im):
     n, rows, cols = re.shape
     g = BATCH
-    block = pl.BlockSpec((g, HALF, cols), lambda i: (first // g + i, side, 0))
+    steps = n // g
+    block = pl.BlockSpec((g, rows, cols), lambda i: (i, 0, 0))
+    early = pl.BlockSpec((2, g, HALF, cols), lambda i: (0, jnp.minimum(i, steps // 2 - 1), 0, 0))
+    late = pl.BlockSpec((2, g, HALF, cols), lambda i: (0, jnp.maximum(i - steps // 2, 0), 0, 0))
     return pl.pallas_call(
         pack_kernel,
-        grid=(count // g,),
-        in_specs=[block, block, *(pl.BlockSpec(memory_space=pl.ANY) for _ in after)],
-        out_specs=pl.BlockSpec((2, g, HALF, cols), lambda i: (0, i, 0, 0)),
-        out_shape=jax.ShapeDtypeStruct((2, count, HALF, cols), BF16),
+        grid=(steps,),
+        in_specs=[block, block],
+        out_specs=[early, late] * 2,
+        out_shape=[jax.ShapeDtypeStruct((2, n // 2, HALF, cols), BF16)] * 4,
         compiler_params=pltpu.CompilerParams(vmem_limit_bytes=16 << 20),
         name="pack",
-    )(in_hbm(re), in_hbm(im), *after)
+    )(in_hbm(re), in_hbm(im))
 
 
 GROUP = 16
@@ -544,20 +553,19 @@
     count = lax.axis_size("row")
     onward = [(i, i + 1) for i in range(count - 1)]
     back = [(b, a) for a, b in onward]
-    packed = pack(ifg_real, ifg_imag, 1, 0, n // 2)
-    above = [lax.ppermute(packed, "row", onward)]
-    packed = pack(ifg_real, ifg_imag, 1, n // 2, n // 2, packed)
-    above += [lax.ppermute(packed, "row", onward)]
-    packed = pack(ifg_real, ifg_imag, 0, 0, n, packed)
-    below = lax.ppermute(packed, "row", back)
-    u = centre(ifg_real, ifg_imag, rows_t, fwd, inv, packed)
+    packed = pack(ifg_real, ifg_imag)
+    above = [lax.ppermute(part, "row", onward) for part in packed[2:]]
+    below = [lax.ppermute(part, "row", back) for part in packed[:2]]
+    u = centre(ifg_real, ifg_imag, rows_t, fwd, inv, packed[2])
     p, g = projection(date_pairs)
-    q = ()
-    for k, halo in enumerate(above):
-        q = (edge(True, k * (n // 2), ifg_real, ifg_imag, halo, u, rows_t, fwd, inv, back_up, *q),)
-    lower = edge(False, 0, ifg_real, ifg_imag, below, u, rows_t, fwd, inv, back_dn)
+    sides = []
+    for upper, parts, table in ((True, above, back_up), (False, below, back_dn)):
+        q = ()
+        for k, halo in enumerate(parts):
+            q = (edge(upper, k * (n // 2), ifg_real, ifg_imag, halo, u, rows_t, fwd, inv, table, *q),)
+        sides += q
     series = ()
-    for part in (*q, lower):
+    for part in sides:
         sines = lax.all_to_all(part, "ifg", split_axis=0, concat_axis=0, tiled=True)
         series = (invert(sines.reshape(-1, cols), p, g, *series),)
     devices = lax.axis_size("ifg")

time: 134 us -> 135 us (level)
  Pallas kernels: 67.4 us -> 69.1 us
    pallas_call x3 -> x4, Pallas kernels: 26.1 us -> 28.6 us  [edge(): pl.pallas_call(lambda *refs: edge_kernel(upper, *refs), grid=(halo.shape[...]
    all_to_all x2, waiting for transfers between devices: 6.97 us -> 9.08 us  [on_device(): sines = lax.all_to_all(part, 'ifg', split_axis=0, concat_axis=0, tiled=True)]
    ppermute x3 -> x4, waiting for transfers between devices: 1.93 us -> 0.01 us  [the longest x2 0.01 us: on_device(): above = [lax.ppermute(part, 'row', onward) for part in packed[2:]]]
    pallas_call x3 -> x1, Pallas kernels: 5.06 us -> 4.23 us  [pack(): pl.pallas_call(pack_kernel, grid=(steps,), in_specs=[block, block], out_s...]
    ppermute x3 -> x4, starting transfers between devices: 10.6 us -> 11.2 us  [the longest x2 6.84 us: on_device(): above = [lax.ppermute(part, 'row', onward) for part in packed[2:]]]
  transfers between devices with their start and end apart: 7 -> 8, of which waited for: 4 -> 3; matrix products, arithmetic and copies ran while one was open for 1% -> 0% of each run, Pallas kernels for 40% -> 41%
where the time goes in v5:
time: 135 us; the launch traced here: 134 us
  Pallas kernels  69.1 us (51%)
  starting transfers between devices  33.3 us (25%)
  blocking collectives  19 us (14%)
  waiting for transfers between devices  11.8 us (9%)
    pallas_call x4, Pallas kernels, edge(): pl.pallas_call(lambda *refs: edge_kernel(upper, *refs), grid=(halo.shape[...  28.6 us
    all_to_all x1, blocking collectives, on_device(): lax.all_to_all(series[0].reshape(devices, -1, LANES), 'ifg', split_axis=0...  19 us
    all_to_all x2, starting transfers between devices, on_device(): sines = lax.all_to_all(part, 'ifg', split_axis=0, concat_axis=0, tiled=True)  15.4 us
    pallas_call x2, Pallas kernels, invert(): pl.pallas_call(invert_kernel, grid=(pixels // width,), in_specs=[pl.Block...  10.3 us
    pallas_call x1, Pallas kernels, centre(): pl.pallas_call(centre_kernel, grid=(n // g,), in_specs=[block, block, who...  10.2 us
    pallas_call x1, Pallas kernels, projection(): pl.pallas_call(projection_kernel, out_shape=(pltpu.HBM((NDATES, nifg), BF...  9.39 us
    all_to_all x2, waiting for transfers between devices, on_device(): sines = lax.all_to_all(part, 'ifg', split_axis=0, concat_axis=0, tiled=True)  9.08 us
    ppermute x2, starting transfers between devices, on_device(): above = [lax.ppermute(part, 'row', onward) for part in packed[2:]]  6.84 us
  transfers between devices with their start and end apart: 8, of which 3 were waited for; matrix products, arithmetic and copies ran while one was open for 0% of the time, Pallas kernels for 41%

profile of v5, /device:TPU:1, one launch (start us, length us, event | category | flops | bytes accessed | tf_op | source)
XLA Modules:
  0.0 134.2 jit_solution(7567226628966646248)
XLA Ops:
  0.6 4.2 %pack.1 = (bf16[2,16,32,512]{3,2,1,0:T(8,128)(2,1)}, bf16[2,16,32,512]{3,2,1,0:T(8,128)(2,1)S(1)}, bf16[2,16,32,512]{3,2,1,0:T(8,128)(2,1)S(1)}, bf16[2,16,32,512]{3,2,1,0:T(8,128)(2,1)S(1)}) custom-call(bf16[32,64,512]{2,1,0:T(8,128)(2,1)} %refs_0_.7, bf16[32,64,512]{2,1,0:T(8,128)(2,1)} %refs_1_.7), custom_call_target="tpu_custom_call" | custom-call | tf_op jit(solution)/shard_map/pack/pallas_call | solution.py:182
  4.9 4.9 %collective-permute-start.3 = (bf16[2,16,32,512]{3,2,1,0:T(8,128)(2,1)S(1)}, bf16[2,16,32,512]{3,2,1,0:T(8,128)(2,1)S(1)}, u32[]{:S(2)}, u32[]{:S(2)}) collective-permute-start(bf16[2,16,32,512]{3,2,1,0:T(8,128)(2,1)S(1)} %get-tuple-element.15.refs_0_), channel_id=1, source_target_pairs={{0,1},{1,2},{2,3},{4,5},{5,6},{6,7},{8,9},{9,10},{10,11},{12,13},{... | collective-permute-start | bytes 3145736 | tf_op jit(solution)/shard_map/ppermute | solution.py:557
  9.8 1.9 %collective-permute-start.2 = (bf16[2,16,32,512]{3,2,1,0:T(8,128)(2,1)S(1)}, bf16[2,16,32,512]{3,2,1,0:T(8,128)(2,1)S(1)}, u32[]{:S(2)}, u32[]{:S(2)}) collective-permute-start(bf16[2,16,32,512]{3,2,1,0:T(8,128)(2,1)S(1)} %get-tuple-element.19), channel_id=1, source_target_pairs={{0,1},{1,2},{2,3},{4,5},{5,6},{6,7},{8,9},{9,10},{10,11},{12,13},{... | collective-permute-start | bytes 3145736 | tf_op jit(solution)/shard_map/ppermute | solution.py:557
  11.7 2.5 %collective-permute-start.1 = (bf16[2,16,32,512]{3,2,1,0:T(8,128)(2,1)}, bf16[2,16,32,512]{3,2,1,0:T(8,128)(2,1)}, u32[]{:S(2)}, u32[]{:S(2)}) collective-permute-start(bf16[2,16,32,512]{3,2,1,0:T(8,128)(2,1)} %get-tuple-element.16), channel_id=1, source_target_pairs={{1,0},{2,1},{3,2},{5,4},{6,5},{7,6},{9,8},{10,9},{11,10},{13,12},{... | collective-permute-start | bytes 3145736 | tf_op jit(solution)/shard_map/ppermute | solution.py:558
  14.2 1.9 %collective-permute-start = (bf16[2,16,32,512]{3,2,1,0:T(8,128)(2,1)S(1)}, bf16[2,16,32,512]{3,2,1,0:T(8,128)(2,1)}, u32[]{:S(2)}, u32[]{:S(2)}) collective-permute-start(bf16[2,16,32,512]{3,2,1,0:T(8,128)(2,1)S(1)} %get-tuple-element.14), channel_id=1, source_target_pairs={{1,0},{2,1},{3,2},{5,4},{6,5},{7,6},{9,8},{10,9},{11,10},{13,12},{... | collective-permute-start | bytes 3145736 | tf_op jit(solution)/shard_map/ppermute | solution.py:558
  16.1 10.2 %centre.1.refs_3_ = bf16[32,128,512]{2,1,0:T(8,128)(2,1)} custom-call(bf16[32,64,512]{2,1,0:T(8,128)(2,1)} %refs_0_.7, bf16[32,64,512]{2,1,0:T(8,128)(2,1)} %refs_1_.7, bf16[128,128]{1,0:T(8,128)(2,1)} %constant.26.clone.rows_ref.refs_4_, bf16[256,256]{1,0:T(8,128)(2,1)} %constant.27.clone.fwd_ref.refs_5_, bf16[256,256]{1,0:T(8,128)(2,1)} %constant.28.clone.inv_ref.refs_6_, ...), custom_call_target="tpu_custom_call" | custom-call | flops 6979321856 | bytes 8388608 | tf_op jit(solution)/shard_map/centre/pallas_call | solution.py:147
  26.4 7.1 %upper.2.refs_8_ = bf16[32,32,512]{2,1,0:T(8,128)(2,1)} custom-call(bf16[32,64,512]{2,1,0:T(8,128)(2,1)} %refs_0_.7, bf16[32,64,512]{2,1,0:T(8,128)(2,1)} %refs_1_.7, bf16[2,16,32,512]{3,2,1,0:T(8,128)(2,1)S(1)} %collective-permute-done.3.refs_2_, bf16[32,128,512]{2,1,0:T(8,128)(2,1)} %centre.1.refs_3_, bf16[128,128]{1,0:T(8,128)(2,1)} %constant.26.clone.rows_ref.refs_4_, ...), custom_call_target="tpu_custom_call" | custom-call | flops 4026531840 | bytes 3670016 | tf_op jit(solution)/shard_map/upper/pallas_call | solution.py:230
  33.4 7.1 %upper.3 = bf16[32,32,512]{2,1,0:T(8,128)(2,1)} custom-call(bf16[32,64,512]{2,1,0:T(8,128)(2,1)} %refs_0_.7, bf16[32,64,512]{2,1,0:T(8,128)(2,1)} %refs_1_.7, bf16[2,16,32,512]{3,2,1,0:T(8,128)(2,1)S(1)} %collective-permute-done.2.refs_2_, bf16[32,128,512]{2,1,0:T(8,128)(2,1)} %centre.1.refs_3_, ...), custom_call_target="tpu_custom_call", output_to_operand_aliasing={{}: (8, {})} | custom-call | flops 4026531840 | bytes 3670016 | tf_op jit(solution)/shard_map/upper/pallas_call | solution.py:230
  40.5 10.4 %all-to-all-start.1 = ((bf16[32,32,512]{2,1,0:T(8,128)(2,1)}), bf16[32,32,512]{2,1,0:T(8,128)(2,1)S(1)}, u32[]{:S(2)}, u32[]{:S(2)}) async-start(bf16[32,32,512]{2,1,0:T(8,128)(2,1)} %upper.3), calls=%async_computation.1 | async-start | bytes 2097152 | tf_op jit(solution)/shard_map/all_to_all | solution.py:569
  51.2 7.2 %lower.2.refs_8_ = bf16[32,32,512]{2,1,0:T(8,128)(2,1)} custom-call(bf16[32,64,512]{2,1,0:T(8,128)(2,1)} %refs_0_.7, bf16[32,64,512]{2,1,0:T(8,128)(2,1)} %refs_1_.7, bf16[2,16,32,512]{3,2,1,0:T(8,128)(2,1)} %collective-permute-done.1.refs_2_, bf16[32,128,512]{2,1,0:T(8,128)(2,1)} %centre.1.refs_3_, bf16[128,128]{1,0:T(8,128)(2,1)} %constant.26.clone.rows_ref.refs_4_, ...), custom_call_target="tpu_custom_call" | custom-call | flops 4026531840 | bytes 3670016 | tf_op jit(solution)/shard_map/lower/pallas_call | solution.py:230
  58.4 7.2 %lower.3 = bf16[32,32,512]{2,1,0:T(8,128)(2,1)} custom-call(bf16[32,64,512]{2,1,0:T(8,128)(2,1)} %refs_0_.7, bf16[32,64,512]{2,1,0:T(8,128)(2,1)} %refs_1_.7, bf16[2,16,32,512]{3,2,1,0:T(8,128)(2,1)} %collective-permute-done.refs_2_, bf16[32,128,512]{2,1,0:T(8,128)(2,1)} %centre.1.refs_3_, ...), custom_call_target="tpu_custom_call", output_to_operand_aliasing={{}: (8, {})} | custom-call | flops 4026531840 | bytes 3670016 | tf_op jit(solution)/shard_map/lower/pallas_call | solution.py:230
  65.6 4.3 %all-to-all-done.1 = bf16[32,32,512]{2,1,0:T(8,128)(2,1)S(1)} async-done(((bf16[32,32,512]{2,1,0:T(8,128)(2,1)}), bf16[32,32,512]{2,1,0:T(8,128)(2,1)S(1)}, u32[]{:S(2)}, u32[]{:S(2)}) %all-to-all-start.1) | async-done | bytes 1048608 | tf_op jit(solution)/shard_map/all_to_all | solution.py:569
  69.9 5.0 %all-to-all-start = ((bf16[32,32,512]{2,1,0:T(8,128)(2,1)}), bf16[32,32,512]{2,1,0:T(8,128)(2,1)S(1)}, u32[]{:S(2)}, u32[]{:S(2)}) async-start(bf16[32,32,512]{2,1,0:T(8,128)(2,1)} %lower.3), calls=%async_computation | async-start | bytes 2097152 | tf_op jit(solution)/shard_map/all_to_all | solution.py:569
  74.9 9.4 %projection.1 = (bf16[320,1024]{1,0:T(8,128)(2,1)}, bf16[1024,640]{1,0:T(8,128)(2,1)}) custom-call(s32[1024,2]{1,0:T(8,128)S(1)} %copy.20.pairs_ref, s32[2,1024]{1,0:T(2,128)S(1)} %bitcast.10), custom_call_target="tpu_custom_call" | custom-call | flops 20000000000 | bytes 4000000 | tf_op jit(solution)/shard_map/projection/pallas_call | solution.py:338
  84.3 5.5 %invert.1.refs_0_ = f32[1280,128]{1,0:T(8,128)} custom-call(bf16[1024,512]{1,0:T(8,128)(2,1)S(1)} %bitcast.7, bf16[320,1024]{1,0:T(8,128)(2,1)} %get-tuple-element.17.p_ref, bf16[1024,640]{1,0:T(8,128)(2,1)} %get-tuple-element.18.g_ref), custom_call_target="tpu_custom_call" | custom-call | flops 2348810240 | bytes 6000000 | tf_op jit(solution)/shard_map/invert/pallas_call | solution.py:399
  89.8 4.8 %all-to-all-done = bf16[32,32,512]{2,1,0:T(8,128)(2,1)S(1)} async-done(((bf16[32,32,512]{2,1,0:T(8,128)(2,1)}), bf16[32,32,512]{2,1,0:T(8,128)(2,1)S(1)}, u32[]{:S(2)}, u32[]{:S(2)}) %all-to-all-start) | async-done | bytes 1048608 | tf_op jit(solution)/shard_map/all_to_all | solution.py:569
  94.6 4.9 %invert_rest.1 = bf16[2560,128]{1,0:T(8,128)(2,1)S(1)} custom-call(bf16[1024,512]{1,0:T(8,128)(2,1)S(1)} %bitcast.8, bf16[320,1024]{1,0:T(8,128)(2,1)} %get-tuple-element.17.p_ref, bf16[1024,640]{1,0:T(8,128)(2,1)} %get-tuple-element.18.g_ref, f32[1280,128]{1,0:T(8,128)} %invert.1.refs_0_), custom_call_target="tpu_custom_call" | custom-call | flops 2348810240 | bytes 6000000 | tf_op jit(solution)/shard_map/invert_rest/pallas_call | solution.py:399
  99.5 19.0 %all_to_all.15 = bf16[32,80,128]{2,1,0:T(8,128)(2,1)S(1)} all-to-all(bf16[32,80,128]{2,1,0:T(8,128)(2,1)S(1)} %bitcast.9), channel_id=1, replica_groups=mesh['ifg'=32,'row'=4] {'ifg'}, dimensions={0} | all-to-all | bytes 1310720 | tf_op jit(solution)/shard_map/all_to_all | solution.py:572
  118.5 2.0 %gather.1 = (f32[10,64,512]{2,1,0:T(8,128)S(1)}, f32[10,64,512]{2,1,0:T(8,128)S(1)}, bf16[10,16,512]{2,1,0:T(8,128)(2,1)S(1)}, bf16[10,16,512]{2,1,0:T(8,128)(2,1)S(1)}) custom-call(bf16[2560,128]{1,0:T(8,128)(2,1)S(1)} %bitcast.6, bf16[512,512]{1,0:T(8,128)(2,1)S(1)} %copy-done, bf16[512,512]{1,0:T(8,128)(2,1)S(1)} %copy-done.1), custom_call_target="tpu_custom_call" | custom-call | tf_op jit(solution)/shard_map/gather/pallas_call | solution.py:461
  120.5 4.7 %collective-permute-start.4 = (bf16[10,16,512]{2,1,0:T(8,128)(2,1)S(1)}, bf16[10,16,512]{2,1,0:T(8,128)(2,1)S(1)}, u32[]{:S(2)}, u32[]{:S(2)}) collective-permute-start(bf16[10,16,512]{2,1,0:T(8,128)(2,1)S(1)} %get-tuple-element.24), channel_id=1, source_target_pairs={{0,1},{1,2},{2,3},{4,5},{5,6},{6,7},{8,9},{9,10},{10,11},{12,13},{... | collective-permute-start | bytes 491528 | tf_op jit(solution)/shard_map/ppermute | solution.py:542
  125.1 1.9 %collective-permute-start.5 = (bf16[10,16,512]{2,1,0:T(8,128)(2,1)S(1)}, bf16[10,16,512]{2,1,0:T(8,128)(2,1)S(1)}, u32[]{:S(2)}, u32[]{:S(2)}) collective-permute-start(bf16[10,16,512]{2,1,0:T(8,128)(2,1)S(1)} %get-tuple-element.25), channel_id=1, source_target_pairs={{1,0},{2,1},{3,2},{5,4},{6,5},{7,6},{9,8},{10,9},{11,10},{13,12},{... | collective-permute-start | bytes 491528 | tf_op jit(solution)/shard_map/ppermute | solution.py:542
  127.1 1.9 %inner.1 = (f32[10,64,512]{2,1,0:T(8,128)}, f32[10,64,512]{2,1,0:T(8,128)}) custom-call(s32[1]{0:T(128)} %bitcast.where_ref, f32[10,64,512]{2,1,0:T(8,128)S(1)} %get-tuple-element.20.series_ref, f32[10,64,512]{2,1,0:T(8,128)S(1)} %get-tuple-element.21.smooth_ref, bf16[4,64,64]{2,1,0:T(8,128)(2,1)S(1)} %copy-done.2, bf16[4,64,64]{2,1,0:T(8,128)(2,1)S(1)} %copy-done.3), custom_call_target="tpu_custom_call" | custom-call | flops 335544320 | bytes 5242880 | tf_op jit(solution)/shard_map/inner/pallas_call | solution.py:483
  129.0 2.7 %collective-permute-done.5.dn_ref = bf16[10,16,512]{2,1,0:T(8,128)(2,1)S(1)} collective-permute-done((bf16[10,16,512]{2,1,0:T(8,128)(2,1)S(1)}, bf16[10,16,512]{2,1,0:T(8,128)(2,1)S(1)}, u32[]{:S(2)}, u32[]{:S(2)}) %collective-permute-start.5) | collective-permute-done | bytes 163872 | tf_op jit(solution)/shard_map/ppermute | solution.py:542
  131.8 2.4 %border.1 = (f32[10,64,512]{2,1,0:T(8,128)}, f32[10,64,512]{2,1,0:T(8,128)}) custom-call(s32[1]{0:T(128)} %bitcast.where_ref, f32[10,64,512]{2,1,0:T(8,128)} %get-tuple-element.22.corr_in, f32[10,64,512]{2,1,0:T(8,128)} %get-tuple-element.23.atm_in, ...), custom_call_target="tpu_custom_call", output_to_operand_aliasing={{0}: (1, {}), {1}: (2, {})} | custom-call | tf_op jit(solution)/shard_map/border/pallas_call | solution.py:523
  (20 shorter events, 0.3 us)
Async XLA Ops:
  4.9 21.5 %collective-permute-start.3 = (bf16[2,16,32,512]{3,2,1,0:T(8,128)(2,1)S(1)}, bf16[2,16,32,512]{3,2,1,0:T(8,128)(2,1)S(1)}, u32[]{:S(2)}, u32[]{:S(2)}) collective-permute-start(bf16[2,16,32,512]{3,2,1,0:T(8,128)(2,1)S(1)} %get-tuple-element.15.refs_0_), channel_id=1, source_target_pairs={{0,1},{1,2},{2,3},{4,5},{5,6},{6,7},{8,9},{9,10},{10,11},{12,13},{... | collective-permute-start | bytes 3145736 | tf_op jit(solution)/shard_map/ppermute | solution.py:557
  9.8 23.6 %collective-permute-start.2 = (bf16[2,16,32,512]{3,2,1,0:T(8,128)(2,1)S(1)}, bf16[2,16,32,512]{3,2,1,0:T(8,128)(2,1)S(1)}, u32[]{:S(2)}, u32[]{:S(2)}) collective-permute-start(bf16[2,16,32,512]{3,2,1,0:T(8,128)(2,1)S(1)} %get-tuple-element.19), channel_id=1, source_target_pairs={{0,1},{1,2},{2,3},{4,5},{5,6},{6,7},{8,9},{9,10},{10,11},{12,13},{... | collective-permute-start | bytes 3145736 | tf_op jit(solution)/shard_map/ppermute | solution.py:557
  11.7 39.4 %collective-permute-start.1 = (bf16[2,16,32,512]{3,2,1,0:T(8,128)(2,1)}, bf16[2,16,32,512]{3,2,1,0:T(8,128)(2,1)}, u32[]{:S(2)}, u32[]{:S(2)}) collective-permute-start(bf16[2,16,32,512]{3,2,1,0:T(8,128)(2,1)} %get-tuple-element.16), channel_id=1, source_target_pairs={{1,0},{2,1},{3,2},{5,4},{6,5},{7,6},{9,8},{10,9},{11,10},{13,12},{... | collective-permute-start | bytes 3145736 | tf_op jit(solution)/shard_map/ppermute | solution.py:558
  14.2 44.2 %collective-permute-start = (bf16[2,16,32,512]{3,2,1,0:T(8,128)(2,1)S(1)}, bf16[2,16,32,512]{3,2,1,0:T(8,128)(2,1)}, u32[]{:S(2)}, u32[]{:S(2)}) collective-permute-start(bf16[2,16,32,512]{3,2,1,0:T(8,128)(2,1)S(1)} %get-tuple-element.14), channel_id=1, source_target_pairs={{1,0},{2,1},{3,2},{5,4},{6,5},{7,6},{9,8},{10,9},{11,10},{13,12},{... | collective-permute-start | bytes 3145736 | tf_op jit(solution)/shard_map/ppermute | solution.py:558
  40.5 10.4 %copy-start.6 = (s32[1024,2]{0,1:T(2,128)S(1)}, s32[1024,2]{0,1:T(2,128)}, u32[]{:S(2)}) copy-start(s32[1024,2]{0,1:T(2,128)} %param.16) | copy-start | bytes 24580
  40.5 29.3 %all-to-all-start.1 = ((bf16[32,32,512]{2,1,0:T(8,128)(2,1)}), bf16[32,32,512]{2,1,0:T(8,128)(2,1)S(1)}, u32[]{:S(2)}, u32[]{:S(2)}) async-start(bf16[32,32,512]{2,1,0:T(8,128)(2,1)} %upper.3), calls=%async_computation.1 | async-start | bytes 2097152 | tf_op jit(solution)/shard_map/all_to_all | solution.py:569
  69.9 24.7 %all-to-all-start = ((bf16[32,32,512]{2,1,0:T(8,128)(2,1)}), bf16[32,32,512]{2,1,0:T(8,128)(2,1)S(1)}, u32[]{:S(2)}, u32[]{:S(2)}) async-start(bf16[32,32,512]{2,1,0:T(8,128)(2,1)} %lower.3), calls=%async_computation | async-start | bytes 2097152 | tf_op jit(solution)/shard_map/all_to_all | solution.py:569
  99.5 19.0 %copy-start = (bf16[512,512]{1,0:T(8,128)(2,1)S(1)}, bf16[512,512]{1,0:T(8,128)(2,1)}, u32[]{:S(2)}) copy-start(bf16[512,512]{1,0:T(8,128)(2,1)} %constant.31.clone.ch_ref) | copy-start | bytes 1572868
  99.5 19.0 %copy-start.1 = (bf16[512,512]{1,0:T(8,128)(2,1)S(1)}, bf16[512,512]{1,0:T(8,128)(2,1)}, u32[]{:S(2)}) copy-start(bf16[512,512]{1,0:T(8,128)(2,1)} %constant.32.clone.cl_ref) | copy-start | bytes 1572868
  99.5 27.6 %copy-start.2 = (bf16[4,64,64]{2,1,0:T(8,128)(2,1)S(1)}, bf16[4,64,64]{2,1,0:T(8,128)(2,1)}, u32[]{:S(2)}) copy-start(bf16[4,64,64]{2,1,0:T(8,128)(2,1)} %constant.33.clone.high_ref) | copy-start | bytes 98308
  99.5 27.6 %copy-start.3 = (bf16[4,64,64]{2,1,0:T(8,128)(2,1)S(1)}, bf16[4,64,64]{2,1,0:T(8,128)(2,1)}, u32[]{:S(2)}) copy-start(bf16[4,64,64]{2,1,0:T(8,128)(2,1)} %constant.34.clone.low_ref) | copy-start | bytes 98308
  120.5 8.6 %collective-permute-start.4 = (bf16[10,16,512]{2,1,0:T(8,128)(2,1)S(1)}, bf16[10,16,512]{2,1,0:T(8,128)(2,1)S(1)}, u32[]{:S(2)}, u32[]{:S(2)}) collective-permute-start(bf16[10,16,512]{2,1,0:T(8,128)(2,1)S(1)} %get-tuple-element.24), channel_id=1, source_target_pairs={{0,1},{1,2},{2,3},{4,5},{5,6},{6,7},{8,9},{9,10},{10,11},{12,13},{... | collective-permute-start | bytes 491528 | tf_op jit(solution)/shard_map/ppermute | solution.py:542
  125.1 6.6 %collective-permute-start.5 = (bf16[10,16,512]{2,1,0:T(8,128)(2,1)S(1)}, bf16[10,16,512]{2,1,0:T(8,128)(2,1)S(1)}, u32[]{:S(2)}, u32[]{:S(2)}) collective-permute-start(bf16[10,16,512]{2,1,0:T(8,128)(2,1)S(1)} %get-tuple-element.25), channel_id=1, source_target_pairs={{1,0},{2,1},{3,2},{5,4},{6,5},{7,6},{9,8},{10,9},{11,10},{13,12},{... | collective-permute-start | bytes 491528 | tf_op jit(solution)/shard_map/ppermute | solution.py:542
  127.1 4.7 %copy-start.4 = (bf16[4,2,16,16]{3,2,1,0:T(8,128)(2,1)S(1)}, bf16[4,2,16,16]{3,2,1,0:T(8,128)(2,1)}, u32[]{:S(2)}) copy-start(bf16[4,2,16,16]{3,2,1,0:T(8,128)(2,1)} %constant.35.clone.high_ref) | copy-start | bytes 12292
  127.1 4.7 %copy-start.5 = (bf16[4,2,16,16]{3,2,1,0:T(8,128)(2,1)S(1)}, bf16[4,2,16,16]{3,2,1,0:T(8,128)(2,1)}, u32[]{:S(2)}) copy-start(bf16[4,2,16,16]{3,2,1,0:T(8,128)(2,1)} %constant.36.clone.low_ref) | copy-start | bytes 12292

commit v6 on v3

--- a/solution.py
+++ b/solution.py
@@ -429,72 +429,37 @@
     )(got, col_high, col_low)
 
 
-def inner_kernel(where_ref, series_ref, smooth_ref, high_ref, low_ref, corr_ref, atm_ref):
+def finish_kernel(where_ref, series_ref, smooth_ref, up_ref, dn_ref, high_ref, low_ref, corr_ref, atm_ref):
     table = (high_ref[0], low_ref[0])
     for d in range(series_ref.shape[0]):
-        atm = dot3(table, split2(smooth_ref[d]))
+        smooth, rest = split2(smooth_ref[d])
+        x = jnp.concatenate([up_ref[d], smooth, dn_ref[d]], axis=0)
+        atm = mm(table[0], x) + (mm(table[1], x) + mm(table[0][:, RADIUS:-RADIUS], rest))
         atm_ref[d] = atm
         corr_ref[d] = series_ref[d] - atm
 
 
-def inner(where, series, smooth, high, low):
+def finish(where, series, smooth, up, dn, high, low):
     dates, rows, cols = series.shape
-    g = 5
+    g = FINISH
     block = pl.BlockSpec((g, rows, cols), lambda i, w: (i, 0, 0))
+    halo = pl.BlockSpec((g, RADIUS, cols), lambda i, w: (i, 0, 0))
     table = pl.BlockSpec((1,) + high.shape[1:], lambda i, w: (w[0], 0, 0))
     return pl.pallas_call(
-        inner_kernel,
+        finish_kernel,
         grid_spec=pltpu.PrefetchScalarGridSpec(
             num_scalar_prefetch=1,
             grid=(dates // g,),
-            in_specs=[block, block, table, table],
-            out_specs=[block, block],
-        ),
-        out_shape=(pltpu.HBM((dates, rows, cols), F32),) * 2,
-        compiler_params=pltpu.CompilerParams(vmem_limit_bytes=24 << 20),
-        cost_estimate=pl.CostEstimate(
-            flops=dates * rows * cols * 1024, bytes_accessed=dates * rows * cols * 16, transcendentals=0
-        ),
-        name="inner",
-    )(where, series, smooth, high, low)
-
-
-def border_kernel(where_ref, corr_in, atm_in, up_ref, dn_ref, high_ref, low_ref, corr_ref, atm_ref):
-    def add(halo_ref):
-        for d in range(corr_in.shape[0]):
-            x = halo_ref[d]
-            more = mm(high_ref[0, 0], x) + mm(low_ref[0, 0], x)
-            atm_ref[d] = atm_in[d] + more
-            corr_ref[d] = corr_in[d] - more
-
-    @pl.when(pl.program_id(0) == 0)
-    def _():
-        add(up_ref)
-
-    @pl.when(pl.program_id(0) == 1)
-    def _():
-        add(dn_ref)
-
-
-def border(where, corrected, atmosphere, up, dn, high, low):
-    dates, rows, cols = corrected.shape
-    last = rows // RADIUS - 1
-    block = pl.BlockSpec((dates, RADIUS, cols), lambda i, w: (0, i * last, 0))
-    halo = pl.BlockSpec(up.shape, lambda i, w: (0, 0, 0))
-    table = pl.BlockSpec((1, 1) + high.shape[2:], lambda i, w: (w[0], i, 0, 0))
-    return pl.pallas_call(
-        border_kernel,
-        grid_spec=pltpu.PrefetchScalarGridSpec(
-            num_scalar_prefetch=1,
-            grid=(2,),
             in_specs=[block, block, halo, halo, table, table],
             out_specs=[block, block],
         ),
-        out_shape=(pltpu.HBM((dates, rows, cols), F32),) * 2,
-        input_output_aliases={1: 0, 2: 1},
+        out_shape=(jax.ShapeDtypeStruct((dates, rows, cols), F32),) * 2,
         compiler_params=pltpu.CompilerParams(vmem_limit_bytes=24 << 20),
-        name="border",
-    )(where, in_hbm(corrected), in_hbm(atmosphere), up, dn, high, low)
+        name="finish",
+    )(where, series, smooth, up, dn, high, low)
+
+
+FINISH = 5
 
 
 def neighbours(low_part, high_part, axis):
@@ -508,8 +473,6 @@
     n, rows, cols = ifg_real.shape
     rows_t, fwd, inv, back_up, back_dn = (jnp.asarray(t) for t in tables())
     col_t, row_t = blur_tables(rows * lax.axis_size("row"), rows, cols)
-    own = row_t[:, :, RADIUS : RADIUS + rows]
-    edges = np.stack([row_t[:, :RADIUS, :RADIUS], row_t[:, rows - RADIUS :, rows + RADIUS :]], axis=1)
     where = lax.axis_index("row").astype(jnp.int32).reshape(1)
 
     low = jnp.stack([ifg_real[:, :HALF], ifg_imag[:, :HALF]])
@@ -517,6 +480,7 @@
     above, below = neighbours(low, high, "row")
     u = centre(ifg_real, ifg_imag, rows_t, fwd, inv)
     p, g = projection(date_pairs)
+    u, p, g = lax.optimization_barrier((u, p, g))
     series = ()
     for upper, halo, back in ((True, above, back_up), (False, below, back_dn)):
         q = edge(upper, ifg_real, ifg_imag, halo, u, rows_t, fwd, inv, back)
@@ -528,8 +492,7 @@
     )
     series, smooth, low, high = gather(series.reshape(-1, LANES), *halves(col_t), rows, cols)
     up, dn = neighbours(low, high, "row")
-    corrected, atmosphere = inner(where, series, smooth, *halves(own))
-    return tuple(border(where, corrected, atmosphere, up, dn, *halves(edges)))
+    return tuple(finish(where, series, smooth, up, dn, *halves(row_t)))
 
 
 def solution(mesh):

time: 134 us -> 133 us (level)
  waiting for transfers between devices: 13.7 us -> 23.4 us
  starting transfers between devices: 33 us -> 27.1 us
  blocking collectives: 20.9 us -> 16.6 us
  Pallas kernels: 60.4 us -> 58.1 us
  other arithmetic: 1.74 us -> 3.08 us
    all_to_all x2, waiting for transfers between devices: 1.68 us -> 21 us  [on_device(): sines = lax.all_to_all(q, 'ifg', split_axis=0, concat_axis=0, tiled=True)]
    ppermute x2, waiting for transfers between devices: 9.25 us -> 0.01 us  [neighbours(): lax.ppermute(high_part, axis, forward)]
    ppermute x2, starting transfers between devices: 11.3 us -> 6.85 us  [neighbours(): lax.ppermute(high_part, axis, forward)]
    all_to_all x1, blocking collectives: 20.9 us -> 16.6 us  [on_device(): lax.all_to_all(series[0].reshape(devices, -1, LANES), 'ifg', split_axis=0...]
    all_to_all x2, starting transfers between devices: 17.9 us -> 14.2 us  [on_device(): sines = lax.all_to_all(q, 'ifg', split_axis=0, concat_axis=0, tiled=True)]
    pallas_call x2 -> x1, Pallas kernels: 4.35 us -> 2.02 us  [finish(): pl.pallas_call(finish_kernel, grid_spec=pltpu.PrefetchScalarGridSpec(num_...]
    ppermute x2, starting transfers between devices: 3.83 us -> 6.12 us  [neighbours(): lax.ppermute(low_part, axis, backward)]
    another operation x1, other arithmetic: 0.2 us -> 1.56 us  [on_device(): high = jnp.stack([ifg_real[:, rows - HALF:], ifg_imag[:, rows - HALF:]])]
  transfers between devices with their start and end apart: 6 -> 6, of which waited for: 3 -> 3; matrix products, arithmetic and copies ran while one was open for 1% -> 1% of each run, Pallas kernels for 38% -> 37%
where the time goes in v6:
time: 133 us; the launch traced here: 132 us
  Pallas kernels  58.1 us (44%)
  starting transfers between devices  27.1 us (20%)
  waiting for transfers between devices  23.4 us (18%)
  blocking collectives  16.6 us (12%)
  other arithmetic  3.08 us (2%)
  local copies, waits for them, and re-layouts  3.02 us (2%)
    pallas_call x2, Pallas kernels, edge(): pl.pallas_call(lambda *refs: edge_kernel(upper, *refs), grid=(n // g,), i...  24.1 us
    all_to_all x2, waiting for transfers between devices, on_device(): sines = lax.all_to_all(q, 'ifg', split_axis=0, concat_axis=0, tiled=True)  21 us
    all_to_all x1, blocking collectives, on_device(): lax.all_to_all(series[0].reshape(devices, -1, LANES), 'ifg', split_axis=0...  16.6 us
    all_to_all x2, starting transfers between devices, on_device(): sines = lax.all_to_all(q, 'ifg', split_axis=0, concat_axis=0, tiled=True)  14.2 us
    pallas_call x2, Pallas kernels, invert(): pl.pallas_call(invert_kernel, grid=(pixels // width,), in_specs=[pl.Block...  10.4 us
    pallas_call x1, Pallas kernels, centre(): pl.pallas_call(centre_kernel, grid=(n // g,), in_specs=[block, block, who...  10.2 us
    pallas_call x1, Pallas kernels, projection(): pl.pallas_call(projection_kernel, out_shape=(pltpu.HBM((NDATES, nifg), BF...  9.39 us
    ppermute x2, starting transfers between devices, neighbours(): lax.ppermute(high_part, axis, forward)  6.85 us
  transfers between devices with their start and end apart: 6, of which 3 were waited for; matrix products, arithmetic and copies ran while one was open for 1% of the time, Pallas kernels for 37%

profile of v6, /device:TPU:1, one launch (start us, length us, event | category | flops | bytes accessed | tf_op | source)
XLA Modules:
  0.0 132.1 jit_solution(15034270551954125886)
XLA Ops:
  0.6 2.8 %slice_bitcast_fusion = (bf16[1,32,32,512]{3,2,1,0:T(8,128)(2,1)S(1)}, bf16[1,32,32,512]{3,2,1,0:T(8,128)(2,1)S(1)}, bf16[1,32,32,512]{3,2,1,0:T(8,128)(2,1)S(1)}, bf16[1,32,32,512]{3,2,1,0:T(8,128)(2,1)S(1)}) fusion(bf16[32,64,512]{2,1,0:T(8,128)(2,1)} %refs_1_.3, bf16[32,64,512]{2,1,0:T(8,128)(2,1)} %refs_0_.3), kind=kLoop, calls=%fused_computation.2 | loop fusion | bytes 8388608 | tf_op jit(solution)/shard_map/stack | solution.py:479
  3.4 1.6 %pad_maximum_fusion.1 = bf16[2,32,32,512]{3,2,1,0:T(8,128)(2,1)} fusion(bf16[1,32,32,512]{3,2,1,0:T(8,128)(2,1)S(1)} %get-tuple-element.22, bf16[1,32,32,512]{3,2,1,0:T(8,128)(2,1)S(1)} %get-tuple-element.25), kind=kLoop, calls=%fused_computation.1 | loop fusion | flops 1048576 | bytes 4194304 | tf_op jit(solution)/shard_map/stack | solution.py:479
  5.0 4.9 %collective-permute-start.1 = (bf16[2,32,32,512]{3,2,1,0:T(8,128)(2,1)}, bf16[2,32,32,512]{3,2,1,0:T(8,128)(2,1)}, u32[]{:S(2)}, u32[]{:S(2)}) collective-permute-start(bf16[2,32,32,512]{3,2,1,0:T(8,128)(2,1)} %pad_maximum_fusion.1), channel_id=1, source_target_pairs={{0,1},{1,2},{2,3},{4,5},{5,6},{6,7},{8,9},{9,10},{10,11},{12,13},{... | collective-permute-start | bytes 6291464 | tf_op jit(solution)/shard_map/ppermute | solution.py:469
  9.9 1.5 %pad_maximum_fusion = bf16[2,32,32,512]{3,2,1,0:T(8,128)(2,1)} fusion(bf16[1,32,32,512]{3,2,1,0:T(8,128)(2,1)S(1)} %get-tuple-element.23, bf16[1,32,32,512]{3,2,1,0:T(8,128)(2,1)S(1)} %get-tuple-element.24), kind=kLoop, calls=%fused_computation | loop fusion | flops 1048576 | bytes 4194304 | tf_op jit(solution)/shard_map/stack | solution.py:478
  11.4 1.9 %collective-permute-start = (bf16[2,32,32,512]{3,2,1,0:T(8,128)(2,1)}, bf16[2,32,32,512]{3,2,1,0:T(8,128)(2,1)S(1)}, u32[]{:S(2)}, u32[]{:S(2)}) collective-permute-start(bf16[2,32,32,512]{3,2,1,0:T(8,128)(2,1)} %pad_maximum_fusion), channel_id=1, source_target_pairs={{1,0},{2,1},{3,2},{5,4},{6,5},{7,6},{9,8},{10,9},{11,10},{13,12},{... | collective-permute-start | bytes 6291464 | tf_op jit(solution)/shard_map/ppermute | solution.py:469
  13.4 0.2 copy.14.pairs_ref
  13.6 9.4 %projection.1 = (bf16[320,1024]{1,0:T(8,128)(2,1)}, bf16[1024,640]{1,0:T(8,128)(2,1)}) custom-call(s32[1024,2]{1,0:T(8,128)S(1)} %copy.14.pairs_ref, s32[2,1024]{1,0:T(2,128)S(1)} %bitcast.18), custom_call_target="tpu_custom_call" | custom-call | flops 20000000000 | bytes 4000000 | tf_op jit(solution)/shard_map/projection/pallas_call | solution.py:300
  23.0 10.2 %centre.1.refs_3_ = bf16[32,128,512]{2,1,0:T(8,128)(2,1)} custom-call(bf16[32,64,512]{2,1,0:T(8,128)(2,1)} %refs_0_.3, bf16[32,64,512]{2,1,0:T(8,128)(2,1)} %refs_1_.3, bf16[128,128]{1,0:T(8,128)(2,1)} %constant.22.clone.rows_ref.refs_4_, bf16[256,256]{1,0:T(8,128)(2,1)} %constant.23.clone.fwd_ref.refs_5_, bf16[256,256]{1,0:T(8,128)(2,1)} %constant.24.clone.inv_ref.refs_6_), custom_call_target="tpu_custom_call" | custom-call | flops 6979321856 | bytes 8388608 | tf_op jit(solution)/shard_map/centre/pallas_call | solution.py:146
  33.2 12.1 %upper.1 = bf16[32,32,512]{2,1,0:T(8,128)(2,1)} custom-call(bf16[32,64,512]{2,1,0:T(8,128)(2,1)} %refs_0_.3, bf16[32,64,512]{2,1,0:T(8,128)(2,1)} %refs_1_.3, bf16[2,32,32,512]{3,2,1,0:T(8,128)(2,1)} %collective-permute-done.1.refs_2_, bf16[32,128,512]{2,1,0:T(8,128)(2,1)} %centre.1.refs_3_, bf16[128,128]{1,0:T(8,128)(2,1)} %constant.22.clone.rows_ref.refs_4_, ...), custom_call_target="tpu_custom_call" | custom-call | flops 8053063680 | bytes 7340032 | tf_op jit(solution)/shard_map/upper/pallas_call | solution.py:195
  45.3 10.1 %all-to-all-start.1 = ((bf16[32,32,512]{2,1,0:T(8,128)(2,1)}), bf16[32,32,512]{2,1,0:T(8,128)(2,1)S(1)}, u32[]{:S(2)}, u32[]{:S(2)}) async-start(bf16[32,32,512]{2,1,0:T(8,128)(2,1)} %upper.1), calls=%async_computation.1 | async-start | bytes 2097152 | tf_op jit(solution)/shard_map/all_to_all | solution.py:487
  55.4 12.0 %lower.1 = bf16[32,32,512]{2,1,0:T(8,128)(2,1)} custom-call(bf16[32,64,512]{2,1,0:T(8,128)(2,1)} %refs_0_.3, bf16[32,64,512]{2,1,0:T(8,128)(2,1)} %refs_1_.3, bf16[2,32,32,512]{3,2,1,0:T(8,128)(2,1)S(1)} %collective-permute-done.refs_2_, bf16[32,128,512]{2,1,0:T(8,128)(2,1)} %centre.1.refs_3_, bf16[128,128]{1,0:T(8,128)(2,1)} %constant.22.clone.rows_ref.refs_4_, ...), custom_call_target="tpu_custom_call" | custom-call | flops 8053063680 | bytes 7340032 | tf_op jit(solution)/shard_map/lower/pallas_call | solution.py:195
  67.3 7.9 %all-to-all-done.1 = bf16[32,32,512]{2,1,0:T(8,128)(2,1)S(1)} async-done(((bf16[32,32,512]{2,1,0:T(8,128)(2,1)}), bf16[32,32,512]{2,1,0:T(8,128)(2,1)S(1)}, u32[]{:S(2)}, u32[]{:S(2)}) %all-to-all-start.1) | async-done | bytes 1048608 | tf_op jit(solution)/shard_map/all_to_all | solution.py:487
  75.3 4.1 %all-to-all-start = ((bf16[32,32,512]{2,1,0:T(8,128)(2,1)}), bf16[32,32,512]{2,1,0:T(8,128)(2,1)S(1)}, u32[]{:S(2)}, u32[]{:S(2)}) async-start(bf16[32,32,512]{2,1,0:T(8,128)(2,1)} %lower.1), calls=%async_computation | async-start | bytes 2097152 | tf_op jit(solution)/shard_map/all_to_all | solution.py:487
  79.4 5.5 %invert.1.refs_0_ = f32[1280,128]{1,0:T(8,128)} custom-call(bf16[1024,512]{1,0:T(8,128)(2,1)S(1)} %bitcast.15, bf16[320,1024]{1,0:T(8,128)(2,1)} %get-tuple-element.14.p_ref, bf16[1024,640]{1,0:T(8,128)(2,1)} %get-tuple-element.15.g_ref), custom_call_target="tpu_custom_call" | custom-call | flops 2348810240 | bytes 6000000 | tf_op jit(solution)/shard_map/invert/pallas_call | solution.py:361
  84.8 13.1 %all-to-all-done = bf16[32,32,512]{2,1,0:T(8,128)(2,1)S(1)} async-done(((bf16[32,32,512]{2,1,0:T(8,128)(2,1)}), bf16[32,32,512]{2,1,0:T(8,128)(2,1)S(1)}, u32[]{:S(2)}, u32[]{:S(2)}) %all-to-all-start) | async-done | bytes 1048608 | tf_op jit(solution)/shard_map/all_to_all | solution.py:487
  97.9 5.0 %invert_rest.1 = bf16[2560,128]{1,0:T(8,128)(2,1)S(1)} custom-call(bf16[1024,512]{1,0:T(8,128)(2,1)S(1)} %bitcast.16, bf16[320,1024]{1,0:T(8,128)(2,1)} %get-tuple-element.14.p_ref, bf16[1024,640]{1,0:T(8,128)(2,1)} %get-tuple-element.15.g_ref, f32[1280,128]{1,0:T(8,128)} %invert.1.refs_0_), custom_call_target="tpu_custom_call" | custom-call | flops 2348810240 | bytes 6000000 | tf_op jit(solution)/shard_map/invert_rest/pallas_call | solution.py:361
  102.9 0.0 copy-start.2
  102.9 0.0 copy-start.3
  102.9 16.6 %all_to_all.15 = bf16[32,80,128]{2,1,0:T(8,128)(2,1)S(1)} all-to-all(bf16[32,80,128]{2,1,0:T(8,128)(2,1)S(1)} %bitcast.17), channel_id=1, replica_groups=mesh['ifg'=32,'row'=4] {'ifg'}, dimensions={0} | all-to-all | bytes 1310720 | tf_op jit(solution)/shard_map/all_to_all | solution.py:490
  119.6 2.0 %gather.1 = (f32[10,64,512]{2,1,0:T(8,128)S(1)}, f32[10,64,512]{2,1,0:T(8,128)S(1)}, bf16[10,16,512]{2,1,0:T(8,128)(2,1)S(1)}, bf16[10,16,512]{2,1,0:T(8,128)(2,1)S(1)}) custom-call(bf16[2560,128]{1,0:T(8,128)(2,1)S(1)} %bitcast.14, bf16[512,512]{1,0:T(8,128)(2,1)S(1)} %copy-done, bf16[512,512]{1,0:T(8,128)(2,1)S(1)} %copy-done.1), custom_call_target="tpu_custom_call" | custom-call | tf_op jit(solution)/shard_map/gather/pallas_call | solution.py:423
  121.5 1.9 %collective-permute-start.2 = (bf16[10,16,512]{2,1,0:T(8,128)(2,1)S(1)}, bf16[10,16,512]{2,1,0:T(8,128)(2,1)S(1)}, u32[]{:S(2)}, u32[]{:S(2)}) collective-permute-start(bf16[10,16,512]{2,1,0:T(8,128)(2,1)S(1)} %get-tuple-element.18), channel_id=1, source_target_pairs={{0,1},{1,2},{2,3},{4,5},{5,6},{6,7},{8,9},{9,10},{10,11},{12,13},{... | collective-permute-start | bytes 491528 | tf_op jit(solution)/shard_map/ppermute | solution.py:469
  123.5 4.2 %collective-permute-start.3 = (bf16[10,16,512]{2,1,0:T(8,128)(2,1)S(1)}, bf16[10,16,512]{2,1,0:T(8,128)(2,1)S(1)}, u32[]{:S(2)}, u32[]{:S(2)}) collective-permute-start(bf16[10,16,512]{2,1,0:T(8,128)(2,1)S(1)} %get-tuple-element.19), channel_id=1, source_target_pairs={{1,0},{2,1},{3,2},{5,4},{6,5},{7,6},{9,8},{10,9},{11,10},{13,12},{... | collective-permute-start | bytes 491528 | tf_op jit(solution)/shard_map/ppermute | solution.py:469
  127.7 2.4 %collective-permute-done.3.dn_ref = bf16[10,16,512]{2,1,0:T(8,128)(2,1)S(1)} collective-permute-done((bf16[10,16,512]{2,1,0:T(8,128)(2,1)S(1)}, bf16[10,16,512]{2,1,0:T(8,128)(2,1)S(1)}, u32[]{:S(2)}, u32[]{:S(2)}) %collective-permute-start.3) | collective-permute-done | bytes 163872 | tf_op jit(solution)/shard_map/ppermute | solution.py:469
  130.1 2.0 %finish.1 = (f32[10,64,512]{2,1,0:T(8,128)}, f32[10,64,512]{2,1,0:T(8,128)}) custom-call(s32[1]{0:T(128)} %bitcast.where_ref, f32[10,64,512]{2,1,0:T(8,128)S(1)} %get-tuple-element.16.series_ref, f32[10,64,512]{2,1,0:T(8,128)S(1)} %get-tuple-element.17.smooth_ref, bf16[10,16,512]{2,1,0:T(8,128)(2,1)S(1)} %collective-permute-done.2.up_ref, ...), custom_call_target="tpu_custom_call" | custom-call | tf_op jit(solution)/shard_map/finish/pallas_call | solution.py:448
  (11 shorter events, 0.0 us)
Async XLA Ops:
  5.0 28.2 %collective-permute-start.1 = (bf16[2,32,32,512]{3,2,1,0:T(8,128)(2,1)}, bf16[2,32,32,512]{3,2,1,0:T(8,128)(2,1)}, u32[]{:S(2)}, u32[]{:S(2)}) collective-permute-start(bf16[2,32,32,512]{3,2,1,0:T(8,128)(2,1)} %pad_maximum_fusion.1), channel_id=1, source_target_pairs={{0,1},{1,2},{2,3},{4,5},{5,6},{6,7},{8,9},{9,10},{10,11},{12,13},{... | collective-permute-start | bytes 6291464 | tf_op jit(solution)/shard_map/ppermute | solution.py:469
  9.9 3.5 %copy-start.4 = (s32[1024,2]{0,1:T(2,128)S(1)}, s32[1024,2]{0,1:T(2,128)}, u32[]{:S(2)}) copy-start(s32[1024,2]{0,1:T(2,128)} %param.14) | copy-start | bytes 24580
  11.4 43.9 %collective-permute-start = (bf16[2,32,32,512]{3,2,1,0:T(8,128)(2,1)}, bf16[2,32,32,512]{3,2,1,0:T(8,128)(2,1)S(1)}, u32[]{:S(2)}, u32[]{:S(2)}) collective-permute-start(bf16[2,32,32,512]{3,2,1,0:T(8,128)(2,1)} %pad_maximum_fusion), channel_id=1, source_target_pairs={{1,0},{2,1},{3,2},{5,4},{6,5},{7,6},{9,8},{10,9},{11,10},{13,12},{... | collective-permute-start | bytes 6291464 | tf_op jit(solution)/shard_map/ppermute | solution.py:469
  45.3 30.0 %all-to-all-start.1 = ((bf16[32,32,512]{2,1,0:T(8,128)(2,1)}), bf16[32,32,512]{2,1,0:T(8,128)(2,1)S(1)}, u32[]{:S(2)}, u32[]{:S(2)}) async-start(bf16[32,32,512]{2,1,0:T(8,128)(2,1)} %upper.1), calls=%async_computation.1 | async-start | bytes 2097152 | tf_op jit(solution)/shard_map/all_to_all | solution.py:487
  75.3 22.7 %all-to-all-start = ((bf16[32,32,512]{2,1,0:T(8,128)(2,1)}), bf16[32,32,512]{2,1,0:T(8,128)(2,1)S(1)}, u32[]{:S(2)}, u32[]{:S(2)}) async-start(bf16[32,32,512]{2,1,0:T(8,128)(2,1)} %lower.1), calls=%async_computation | async-start | bytes 2097152 | tf_op jit(solution)/shard_map/all_to_all | solution.py:487
  97.9 21.6 %copy-start = (bf16[512,512]{1,0:T(8,128)(2,1)S(1)}, bf16[512,512]{1,0:T(8,128)(2,1)}, u32[]{:S(2)}) copy-start(bf16[512,512]{1,0:T(8,128)(2,1)} %constant.27.clone.ch_ref) | copy-start | bytes 1572868
  97.9 21.6 %copy-start.1 = (bf16[512,512]{1,0:T(8,128)(2,1)S(1)}, bf16[512,512]{1,0:T(8,128)(2,1)}, u32[]{:S(2)}) copy-start(bf16[512,512]{1,0:T(8,128)(2,1)} %constant.28.clone.cl_ref) | copy-start | bytes 1572868
  102.9 27.2 %copy-start.2 = (bf16[4,64,96]{2,1,0:T(8,128)(2,1)S(1)}, bf16[4,64,96]{2,1,0:T(8,128)(2,1)}, u32[]{:S(2)}) copy-start(bf16[4,64,96]{2,1,0:T(8,128)(2,1)} %constant.29.clone.high_ref) | copy-start | bytes 147460
  102.9 27.2 %copy-start.3 = (bf16[4,64,96]{2,1,0:T(8,128)(2,1)S(1)}, bf16[4,64,96]{2,1,0:T(8,128)(2,1)}, u32[]{:S(2)}) copy-start(bf16[4,64,96]{2,1,0:T(8,128)(2,1)} %constant.30.clone.low_ref) | copy-start | bytes 147460
  121.5 6.2 %collective-permute-start.2 = (bf16[10,16,512]{2,1,0:T(8,128)(2,1)S(1)}, bf16[10,16,512]{2,1,0:T(8,128)(2,1)S(1)}, u32[]{:S(2)}, u32[]{:S(2)}) collective-permute-start(bf16[10,16,512]{2,1,0:T(8,128)(2,1)S(1)} %get-tuple-element.18), channel_id=1, source_target_pairs={{0,1},{1,2},{2,3},{4,5},{5,6},{6,7},{8,9},{9,10},{10,11},{12,13},{... | collective-permute-start | bytes 491528 | tf_op jit(solution)/shard_map/ppermute | solution.py:469
  123.5 6.6 %collective-permute-start.3 = (bf16[10,16,512]{2,1,0:T(8,128)(2,1)S(1)}, bf16[10,16,512]{2,1,0:T(8,128)(2,1)S(1)}, u32[]{:S(2)}, u32[]{:S(2)}) collective-permute-start(bf16[10,16,512]{2,1,0:T(8,128)(2,1)S(1)} %get-tuple-element.19), channel_id=1, source_target_pairs={{1,0},{2,1},{3,2},{5,4},{6,5},{7,6},{9,8},{10,9},{11,10},{13,12},{... | collective-permute-start | bytes 491528 | tf_op jit(solution)/shard_map/ppermute | solution.py:469

commit v7 on v5

--- a/solution.py
+++ b/solution.py
@@ -467,72 +467,37 @@
     )(got, col_high, col_low)
 
 
-def inner_kernel(where_ref, series_ref, smooth_ref, high_ref, low_ref, corr_ref, atm_ref):
+def finish_kernel(where_ref, series_ref, smooth_ref, up_ref, dn_ref, high_ref, low_ref, corr_ref, atm_ref):
     table = (high_ref[0], low_ref[0])
     for d in range(series_ref.shape[0]):
-        atm = dot3(table, split2(smooth_ref[d]))
+        smooth, rest = split2(smooth_ref[d])
+        x = jnp.concatenate([up_ref[d], smooth, dn_ref[d]], axis=0)
+        atm = mm(table[0], x) + (mm(table[1], x) + mm(table[0][:, RADIUS:-RADIUS], rest))
         atm_ref[d] = atm
         corr_ref[d] = series_ref[d] - atm
 
 
-def inner(where, series, smooth, high, low):
+def finish(where, series, smooth, up, dn, high, low):
     dates, rows, cols = series.shape
-    g = 5
+    g = FINISH
     block = pl.BlockSpec((g, rows, cols), lambda i, w: (i, 0, 0))
+    halo = pl.BlockSpec((g, RADIUS, cols), lambda i, w: (i, 0, 0))
     table = pl.BlockSpec((1,) + high.shape[1:], lambda i, w: (w[0], 0, 0))
     return pl.pallas_call(
-        inner_kernel,
+        finish_kernel,
         grid_spec=pltpu.PrefetchScalarGridSpec(
             num_scalar_prefetch=1,
             grid=(dates // g,),
-            in_specs=[block, block, table, table],
-            out_specs=[block, block],
-        ),
-        out_shape=(pltpu.HBM((dates, rows, cols), F32),) * 2,
-        compiler_params=pltpu.CompilerParams(vmem_limit_bytes=24 << 20),
-        cost_estimate=pl.CostEstimate(
-            flops=dates * rows * cols * 1024, bytes_accessed=dates * rows * cols * 16, transcendentals=0
-        ),
-        name="inner",
-    )(where, series, smooth, high, low)
-
-
-def border_kernel(where_ref, corr_in, atm_in, up_ref, dn_ref, high_ref, low_ref, corr_ref, atm_ref):
-    def add(halo_ref):
-        for d in range(corr_in.shape[0]):
-            x = halo_ref[d]
-            more = mm(high_ref[0, 0], x) + mm(low_ref[0, 0], x)
-            atm_ref[d] = atm_in[d] + more
-            corr_ref[d] = corr_in[d] - more
-
-    @pl.when(pl.program_id(0) == 0)
-    def _():
-        add(up_ref)
-
-    @pl.when(pl.program_id(0) == 1)
-    def _():
-        add(dn_ref)
-
-
-def border(where, corrected, atmosphere, up, dn, high, low):
-    dates, rows, cols = corrected.shape
-    last = rows // RADIUS - 1
-    block = pl.BlockSpec((dates, RADIUS, cols), lambda i, w: (0, i * last, 0))
-    halo = pl.BlockSpec(up.shape, lambda i, w: (0, 0, 0))
-    table = pl.BlockSpec((1, 1) + high.shape[2:], lambda i, w: (w[0], i, 0, 0))
-    return pl.pallas_call(
-        border_kernel,
-        grid_spec=pltpu.PrefetchScalarGridSpec(
-            num_scalar_prefetch=1,
-            grid=(2,),
             in_specs=[block, block, halo, halo, table, table],
             out_specs=[block, block],
         ),
-        out_shape=(pltpu.HBM((dates, rows, cols), F32),) * 2,
-        input_output_aliases={1: 0, 2: 1},
+        out_shape=(jax.ShapeDtypeStruct((dates, rows, cols), F32),) * 2,
         compiler_params=pltpu.CompilerParams(vmem_limit_bytes=24 << 20),
-        name="border",
-    )(where, in_hbm(corrected), in_hbm(atmosphere), up, dn, high, low)
+        name="finish",
+    )(where, series, smooth, up, dn, high, low)
+
+
+FINISH = 5
 
 
 def neighbours(low_part, high_part, axis):
@@ -546,8 +511,6 @@
     n, rows, cols = ifg_real.shape
     rows_t, fwd, inv, back_up, back_dn = (jnp.asarray(t) for t in tables())
     col_t, row_t = blur_tables(rows * lax.axis_size("row"), rows, cols)
-    own = row_t[:, :, RADIUS : RADIUS + rows]
-    edges = np.stack([row_t[:, :RADIUS, :RADIUS], row_t[:, rows - RADIUS :, rows + RADIUS :]], axis=1)
     where = lax.axis_index("row").astype(jnp.int32).reshape(1)
 
     count = lax.axis_size("row")
@@ -574,8 +537,7 @@
     )
     series, smooth, low, high = gather(series.reshape(-1, LANES), *halves(col_t), rows, cols)
     up, dn = neighbours(low, high, "row")
-    corrected, atmosphere = inner(where, series, smooth, *halves(own))
-    return tuple(border(where, corrected, atmosphere, up, dn, *halves(edges)))
+    return tuple(finish(where, series, smooth, up, dn, *halves(row_t)))
 
 
 def solution(mesh):

time: 135 us -> 135 us (level)
  Pallas kernels: 69.1 us -> 66.8 us
  waiting for transfers between devices: 11.8 us -> 13.8 us
    pallas_call x2 -> x1, Pallas kernels: 4.34 us -> 2.04 us  [finish(): pl.pallas_call(finish_kernel, grid_spec=pltpu.PrefetchScalarGridSpec(num_...]
    ppermute x1, waiting for transfers between devices: 2.74 us -> 4.4 us  [neighbours(): lax.ppermute(low_part, axis, backward)]
  transfers between devices with their start and end apart: 8 -> 8, of which waited for: 3 -> 4; matrix products, arithmetic and copies ran while one was open for 0% -> 0% of each run, Pallas kernels for 41% -> 40%
where the time goes in v7:
time: 135 us; the launch traced here: 134 us
  Pallas kernels  66.8 us (49%)
  starting transfers between devices  33.2 us (25%)
  blocking collectives  19 us (14%)
  waiting for transfers between devices  13.8 us (10%)
    pallas_call x4, Pallas kernels, edge(): pl.pallas_call(lambda *refs: edge_kernel(upper, *refs), grid=(halo.shape[...  28.6 us
    all_to_all x1, blocking collectives, on_device(): lax.all_to_all(series[0].reshape(devices, -1, LANES), 'ifg', split_axis=0...  19 us
    all_to_all x2, starting transfers between devices, on_device(): sines = lax.all_to_all(part, 'ifg', split_axis=0, concat_axis=0, tiled=True)  15.4 us
    pallas_call x2, Pallas kernels, invert(): pl.pallas_call(invert_kernel, grid=(pixels // width,), in_specs=[pl.Block...  10.3 us
    pallas_call x1, Pallas kernels, centre(): pl.pallas_call(centre_kernel, grid=(n // g,), in_specs=[block, block, who...  10.3 us
    pallas_call x1, Pallas kernels, projection(): pl.pallas_call(projection_kernel, out_shape=(pltpu.HBM((NDATES, nifg), BF...  9.38 us
    all_to_all x2, waiting for transfers between devices, on_device(): sines = lax.all_to_all(part, 'ifg', split_axis=0, concat_axis=0, tiled=True)  9.09 us
    ppermute x2, starting transfers between devices, on_device(): above = [lax.ppermute(part, 'row', onward) for part in packed[2:]]  6.84 us
  transfers between devices with their start and end apart: 8, of which 4 were waited for; matrix products, arithmetic and copies ran while one was open for 0% of the time, Pallas kernels for 40%

profile of v7, /device:TPU:1, one launch (start us, length us, event | category | flops | bytes accessed | tf_op | source)
XLA Modules:
  0.0 133.9 jit_solution(11539108930653345659)
XLA Ops:
  0.6 4.2 %pack.1 = (bf16[2,16,32,512]{3,2,1,0:T(8,128)(2,1)}, bf16[2,16,32,512]{3,2,1,0:T(8,128)(2,1)S(1)}, bf16[2,16,32,512]{3,2,1,0:T(8,128)(2,1)S(1)}, bf16[2,16,32,512]{3,2,1,0:T(8,128)(2,1)S(1)}) custom-call(bf16[32,64,512]{2,1,0:T(8,128)(2,1)} %refs_0_.7, bf16[32,64,512]{2,1,0:T(8,128)(2,1)} %refs_1_.7), custom_call_target="tpu_custom_call" | custom-call | tf_op jit(solution)/shard_map/pack/pallas_call | solution.py:182
  4.9 4.9 %collective-permute-start.3 = (bf16[2,16,32,512]{3,2,1,0:T(8,128)(2,1)S(1)}, bf16[2,16,32,512]{3,2,1,0:T(8,128)(2,1)S(1)}, u32[]{:S(2)}, u32[]{:S(2)}) collective-permute-start(bf16[2,16,32,512]{3,2,1,0:T(8,128)(2,1)S(1)} %get-tuple-element.13.refs_0_), channel_id=1, source_target_pairs={{0,1},{1,2},{2,3},{4,5},{5,6},{6,7},{8,9},{9,10},{10,11},{12,13},{... | collective-permute-start | bytes 3145736 | tf_op jit(solution)/shard_map/ppermute | solution.py:520
  9.8 1.9 %collective-permute-start.2 = (bf16[2,16,32,512]{3,2,1,0:T(8,128)(2,1)S(1)}, bf16[2,16,32,512]{3,2,1,0:T(8,128)(2,1)S(1)}, u32[]{:S(2)}, u32[]{:S(2)}) collective-permute-start(bf16[2,16,32,512]{3,2,1,0:T(8,128)(2,1)S(1)} %get-tuple-element.17), channel_id=1, source_target_pairs={{0,1},{1,2},{2,3},{4,5},{5,6},{6,7},{8,9},{9,10},{10,11},{12,13},{... | collective-permute-start | bytes 3145736 | tf_op jit(solution)/shard_map/ppermute | solution.py:520
  11.7 2.5 %collective-permute-start.1 = (bf16[2,16,32,512]{3,2,1,0:T(8,128)(2,1)}, bf16[2,16,32,512]{3,2,1,0:T(8,128)(2,1)}, u32[]{:S(2)}, u32[]{:S(2)}) collective-permute-start(bf16[2,16,32,512]{3,2,1,0:T(8,128)(2,1)} %get-tuple-element.14), channel_id=1, source_target_pairs={{1,0},{2,1},{3,2},{5,4},{6,5},{7,6},{9,8},{10,9},{11,10},{13,12},{... | collective-permute-start | bytes 3145736 | tf_op jit(solution)/shard_map/ppermute | solution.py:521
  14.2 1.9 %collective-permute-start = (bf16[2,16,32,512]{3,2,1,0:T(8,128)(2,1)S(1)}, bf16[2,16,32,512]{3,2,1,0:T(8,128)(2,1)}, u32[]{:S(2)}, u32[]{:S(2)}) collective-permute-start(bf16[2,16,32,512]{3,2,1,0:T(8,128)(2,1)S(1)} %get-tuple-element.12), channel_id=1, source_target_pairs={{1,0},{2,1},{3,2},{5,4},{6,5},{7,6},{9,8},{10,9},{11,10},{13,12},{... | collective-permute-start | bytes 3145736 | tf_op jit(solution)/shard_map/ppermute | solution.py:521
  16.1 10.3 %centre.1.refs_3_ = bf16[32,128,512]{2,1,0:T(8,128)(2,1)} custom-call(bf16[32,64,512]{2,1,0:T(8,128)(2,1)} %refs_0_.7, bf16[32,64,512]{2,1,0:T(8,128)(2,1)} %refs_1_.7, bf16[128,128]{1,0:T(8,128)(2,1)} %constant.22.clone.rows_ref.refs_4_, bf16[256,256]{1,0:T(8,128)(2,1)} %constant.23.clone.fwd_ref.refs_5_, bf16[256,256]{1,0:T(8,128)(2,1)} %constant.24.clone.inv_ref.refs_6_, ...), custom_call_target="tpu_custom_call" | custom-call | flops 6979321856 | bytes 8388608 | tf_op jit(solution)/shard_map/centre/pallas_call | solution.py:147
  26.4 7.1 %upper.2.refs_8_ = bf16[32,32,512]{2,1,0:T(8,128)(2,1)} custom-call(bf16[32,64,512]{2,1,0:T(8,128)(2,1)} %refs_0_.7, bf16[32,64,512]{2,1,0:T(8,128)(2,1)} %refs_1_.7, bf16[2,16,32,512]{3,2,1,0:T(8,128)(2,1)S(1)} %collective-permute-done.3.refs_2_, bf16[32,128,512]{2,1,0:T(8,128)(2,1)} %centre.1.refs_3_, bf16[128,128]{1,0:T(8,128)(2,1)} %constant.22.clone.rows_ref.refs_4_, ...), custom_call_target="tpu_custom_call" | custom-call | flops 4026531840 | bytes 3670016 | tf_op jit(solution)/shard_map/upper/pallas_call | solution.py:230
  33.5 7.1 %upper.3 = bf16[32,32,512]{2,1,0:T(8,128)(2,1)} custom-call(bf16[32,64,512]{2,1,0:T(8,128)(2,1)} %refs_0_.7, bf16[32,64,512]{2,1,0:T(8,128)(2,1)} %refs_1_.7, bf16[2,16,32,512]{3,2,1,0:T(8,128)(2,1)S(1)} %collective-permute-done.2.refs_2_, bf16[32,128,512]{2,1,0:T(8,128)(2,1)} %centre.1.refs_3_, ...), custom_call_target="tpu_custom_call", output_to_operand_aliasing={{}: (8, {})} | custom-call | flops 4026531840 | bytes 3670016 | tf_op jit(solution)/shard_map/upper/pallas_call | solution.py:230
  40.6 10.4 %all-to-all-start.1 = ((bf16[32,32,512]{2,1,0:T(8,128)(2,1)}), bf16[32,32,512]{2,1,0:T(8,128)(2,1)S(1)}, u32[]{:S(2)}, u32[]{:S(2)}) async-start(bf16[32,32,512]{2,1,0:T(8,128)(2,1)} %upper.3), calls=%async_computation.1 | async-start | bytes 2097152 | tf_op jit(solution)/shard_map/all_to_all | solution.py:532
  51.2 7.2 %lower.2.refs_8_ = bf16[32,32,512]{2,1,0:T(8,128)(2,1)} custom-call(bf16[32,64,512]{2,1,0:T(8,128)(2,1)} %refs_0_.7, bf16[32,64,512]{2,1,0:T(8,128)(2,1)} %refs_1_.7, bf16[2,16,32,512]{3,2,1,0:T(8,128)(2,1)} %collective-permute-done.1.refs_2_, bf16[32,128,512]{2,1,0:T(8,128)(2,1)} %centre.1.refs_3_, bf16[128,128]{1,0:T(8,128)(2,1)} %constant.22.clone.rows_ref.refs_4_, ...), custom_call_target="tpu_custom_call" | custom-call | flops 4026531840 | bytes 3670016 | tf_op jit(solution)/shard_map/lower/pallas_call | solution.py:230
  58.4 7.2 %lower.3 = bf16[32,32,512]{2,1,0:T(8,128)(2,1)} custom-call(bf16[32,64,512]{2,1,0:T(8,128)(2,1)} %refs_0_.7, bf16[32,64,512]{2,1,0:T(8,128)(2,1)} %refs_1_.7, bf16[2,16,32,512]{3,2,1,0:T(8,128)(2,1)} %collective-permute-done.refs_2_, bf16[32,128,512]{2,1,0:T(8,128)(2,1)} %centre.1.refs_3_, ...), custom_call_target="tpu_custom_call", output_to_operand_aliasing={{}: (8, {})} | custom-call | flops 4026531840 | bytes 3670016 | tf_op jit(solution)/shard_map/lower/pallas_call | solution.py:230
  65.6 4.3 %all-to-all-done.1 = bf16[32,32,512]{2,1,0:T(8,128)(2,1)S(1)} async-done(((bf16[32,32,512]{2,1,0:T(8,128)(2,1)}), bf16[32,32,512]{2,1,0:T(8,128)(2,1)S(1)}, u32[]{:S(2)}, u32[]{:S(2)}) %all-to-all-start.1) | async-done | bytes 1048608 | tf_op jit(solution)/shard_map/all_to_all | solution.py:532
  69.9 5.0 %all-to-all-start = ((bf16[32,32,512]{2,1,0:T(8,128)(2,1)}), bf16[32,32,512]{2,1,0:T(8,128)(2,1)S(1)}, u32[]{:S(2)}, u32[]{:S(2)}) async-start(bf16[32,32,512]{2,1,0:T(8,128)(2,1)} %lower.3), calls=%async_computation | async-start | bytes 2097152 | tf_op jit(solution)/shard_map/all_to_all | solution.py:532
  74.9 9.4 %projection.1 = (bf16[320,1024]{1,0:T(8,128)(2,1)}, bf16[1024,640]{1,0:T(8,128)(2,1)}) custom-call(s32[1024,2]{1,0:T(8,128)S(1)} %copy.16.pairs_ref, s32[2,1024]{1,0:T(2,128)S(1)} %bitcast.10), custom_call_target="tpu_custom_call" | custom-call | flops 20000000000 | bytes 4000000 | tf_op jit(solution)/shard_map/projection/pallas_call | solution.py:338
  84.3 5.5 %invert.1.refs_0_ = f32[1280,128]{1,0:T(8,128)} custom-call(bf16[1024,512]{1,0:T(8,128)(2,1)S(1)} %bitcast.7, bf16[320,1024]{1,0:T(8,128)(2,1)} %get-tuple-element.15.p_ref, bf16[1024,640]{1,0:T(8,128)(2,1)} %get-tuple-element.16.g_ref), custom_call_target="tpu_custom_call" | custom-call | flops 2348810240 | bytes 6000000 | tf_op jit(solution)/shard_map/invert/pallas_call | solution.py:399
  89.8 4.8 %all-to-all-done = bf16[32,32,512]{2,1,0:T(8,128)(2,1)S(1)} async-done(((bf16[32,32,512]{2,1,0:T(8,128)(2,1)}), bf16[32,32,512]{2,1,0:T(8,128)(2,1)S(1)}, u32[]{:S(2)}, u32[]{:S(2)}) %all-to-all-start) | async-done | bytes 1048608 | tf_op jit(solution)/shard_map/all_to_all | solution.py:532
  94.6 4.9 %invert_rest.1 = bf16[2560,128]{1,0:T(8,128)(2,1)S(1)} custom-call(bf16[1024,512]{1,0:T(8,128)(2,1)S(1)} %bitcast.8, bf16[320,1024]{1,0:T(8,128)(2,1)} %get-tuple-element.15.p_ref, bf16[1024,640]{1,0:T(8,128)(2,1)} %get-tuple-element.16.g_ref, f32[1280,128]{1,0:T(8,128)} %invert.1.refs_0_), custom_call_target="tpu_custom_call" | custom-call | flops 2348810240 | bytes 6000000 | tf_op jit(solution)/shard_map/invert_rest/pallas_call | solution.py:399
  99.5 19.0 %all_to_all.15 = bf16[32,80,128]{2,1,0:T(8,128)(2,1)S(1)} all-to-all(bf16[32,80,128]{2,1,0:T(8,128)(2,1)S(1)} %bitcast.9), channel_id=1, replica_groups=mesh['ifg'=32,'row'=4] {'ifg'}, dimensions={0} | all-to-all | bytes 1310720 | tf_op jit(solution)/shard_map/all_to_all | solution.py:535
  118.5 2.0 %gather.1 = (f32[10,64,512]{2,1,0:T(8,128)S(1)}, f32[10,64,512]{2,1,0:T(8,128)S(1)}, bf16[10,16,512]{2,1,0:T(8,128)(2,1)S(1)}, bf16[10,16,512]{2,1,0:T(8,128)(2,1)S(1)}) custom-call(bf16[2560,128]{1,0:T(8,128)(2,1)S(1)} %bitcast.6, bf16[512,512]{1,0:T(8,128)(2,1)S(1)} %copy-done, bf16[512,512]{1,0:T(8,128)(2,1)S(1)} %copy-done.1), custom_call_target="tpu_custom_call" | custom-call | tf_op jit(solution)/shard_map/gather/pallas_call | solution.py:461
  120.5 4.7 %collective-permute-start.4 = (bf16[10,16,512]{2,1,0:T(8,128)(2,1)S(1)}, bf16[10,16,512]{2,1,0:T(8,128)(2,1)S(1)}, u32[]{:S(2)}, u32[]{:S(2)}) collective-permute-start(bf16[10,16,512]{2,1,0:T(8,128)(2,1)S(1)} %get-tuple-element.20), channel_id=1, source_target_pairs={{0,1},{1,2},{2,3},{4,5},{5,6},{6,7},{8,9},{9,10},{10,11},{12,13},{... | collective-permute-start | bytes 491528 | tf_op jit(solution)/shard_map/ppermute | solution.py:507
  125.2 1.9 %collective-permute-start.5 = (bf16[10,16,512]{2,1,0:T(8,128)(2,1)S(1)}, bf16[10,16,512]{2,1,0:T(8,128)(2,1)S(1)}, u32[]{:S(2)}, u32[]{:S(2)}) collective-permute-start(bf16[10,16,512]{2,1,0:T(8,128)(2,1)S(1)} %get-tuple-element.21), channel_id=1, source_target_pairs={{1,0},{2,1},{3,2},{5,4},{6,5},{7,6},{9,8},{10,9},{11,10},{13,12},{... | collective-permute-start | bytes 491528 | tf_op jit(solution)/shard_map/ppermute | solution.py:507
  127.1 0.3 collective-permute-done.4.up_ref
  127.4 4.4 %collective-permute-done.5.dn_ref = bf16[10,16,512]{2,1,0:T(8,128)(2,1)S(1)} collective-permute-done((bf16[10,16,512]{2,1,0:T(8,128)(2,1)S(1)}, bf16[10,16,512]{2,1,0:T(8,128)(2,1)S(1)}, u32[]{:S(2)}, u32[]{:S(2)}) %collective-permute-start.5) | collective-permute-done | bytes 163872 | tf_op jit(solution)/shard_map/ppermute | solution.py:507
  131.8 2.0 %finish.1 = (f32[10,64,512]{2,1,0:T(8,128)}, f32[10,64,512]{2,1,0:T(8,128)}) custom-call(s32[1]{0:T(128)} %bitcast.where_ref, f32[10,64,512]{2,1,0:T(8,128)S(1)} %get-tuple-element.18.series_ref, f32[10,64,512]{2,1,0:T(8,128)S(1)} %get-tuple-element.19.smooth_ref, bf16[10,16,512]{2,1,0:T(8,128)(2,1)S(1)} %collective-permute-done.4.up_ref, ...), custom_call_target="tpu_custom_call" | custom-call | tf_op jit(solution)/shard_map/finish/pallas_call | solution.py:486
  (15 shorter events, 0.3 us)
Async XLA Ops:
  4.9 21.5 %collective-permute-start.3 = (bf16[2,16,32,512]{3,2,1,0:T(8,128)(2,1)S(1)}, bf16[2,16,32,512]{3,2,1,0:T(8,128)(2,1)S(1)}, u32[]{:S(2)}, u32[]{:S(2)}) collective-permute-start(bf16[2,16,32,512]{3,2,1,0:T(8,128)(2,1)S(1)} %get-tuple-element.13.refs_0_), channel_id=1, source_target_pairs={{0,1},{1,2},{2,3},{4,5},{5,6},{6,7},{8,9},{9,10},{10,11},{12,13},{... | collective-permute-start | bytes 3145736 | tf_op jit(solution)/shard_map/ppermute | solution.py:520
  9.8 23.7 %collective-permute-start.2 = (bf16[2,16,32,512]{3,2,1,0:T(8,128)(2,1)S(1)}, bf16[2,16,32,512]{3,2,1,0:T(8,128)(2,1)S(1)}, u32[]{:S(2)}, u32[]{:S(2)}) collective-permute-start(bf16[2,16,32,512]{3,2,1,0:T(8,128)(2,1)S(1)} %get-tuple-element.17), channel_id=1, source_target_pairs={{0,1},{1,2},{2,3},{4,5},{5,6},{6,7},{8,9},{9,10},{10,11},{12,13},{... | collective-permute-start | bytes 3145736 | tf_op jit(solution)/shard_map/ppermute | solution.py:520
  11.7 39.5 %collective-permute-start.1 = (bf16[2,16,32,512]{3,2,1,0:T(8,128)(2,1)}, bf16[2,16,32,512]{3,2,1,0:T(8,128)(2,1)}, u32[]{:S(2)}, u32[]{:S(2)}) collective-permute-start(bf16[2,16,32,512]{3,2,1,0:T(8,128)(2,1)} %get-tuple-element.14), channel_id=1, source_target_pairs={{1,0},{2,1},{3,2},{5,4},{6,5},{7,6},{9,8},{10,9},{11,10},{13,12},{... | collective-permute-start | bytes 3145736 | tf_op jit(solution)/shard_map/ppermute | solution.py:521
  14.2 44.2 %collective-permute-start = (bf16[2,16,32,512]{3,2,1,0:T(8,128)(2,1)S(1)}, bf16[2,16,32,512]{3,2,1,0:T(8,128)(2,1)}, u32[]{:S(2)}, u32[]{:S(2)}) collective-permute-start(bf16[2,16,32,512]{3,2,1,0:T(8,128)(2,1)S(1)} %get-tuple-element.12), channel_id=1, source_target_pairs={{1,0},{2,1},{3,2},{5,4},{6,5},{7,6},{9,8},{10,9},{11,10},{13,12},{... | collective-permute-start | bytes 3145736 | tf_op jit(solution)/shard_map/ppermute | solution.py:521
  40.6 10.4 %copy-start.4 = (s32[1024,2]{0,1:T(2,128)S(1)}, s32[1024,2]{0,1:T(2,128)}, u32[]{:S(2)}) copy-start(s32[1024,2]{0,1:T(2,128)} %param.14) | copy-start | bytes 24580
  40.6 29.3 %all-to-all-start.1 = ((bf16[32,32,512]{2,1,0:T(8,128)(2,1)}), bf16[32,32,512]{2,1,0:T(8,128)(2,1)S(1)}, u32[]{:S(2)}, u32[]{:S(2)}) async-start(bf16[32,32,512]{2,1,0:T(8,128)(2,1)} %upper.3), calls=%async_computation.1 | async-start | bytes 2097152 | tf_op jit(solution)/shard_map/all_to_all | solution.py:532
  69.9 24.7 %all-to-all-start = ((bf16[32,32,512]{2,1,0:T(8,128)(2,1)}), bf16[32,32,512]{2,1,0:T(8,128)(2,1)S(1)}, u32[]{:S(2)}, u32[]{:S(2)}) async-start(bf16[32,32,512]{2,1,0:T(8,128)(2,1)} %lower.3), calls=%async_computation | async-start | bytes 2097152 | tf_op jit(solution)/shard_map/all_to_all | solution.py:532
  99.5 19.0 %copy-start = (bf16[512,512]{1,0:T(8,128)(2,1)S(1)}, bf16[512,512]{1,0:T(8,128)(2,1)}, u32[]{:S(2)}) copy-start(bf16[512,512]{1,0:T(8,128)(2,1)} %constant.27.clone.ch_ref) | copy-start | bytes 1572868
  99.5 19.0 %copy-start.1 = (bf16[512,512]{1,0:T(8,128)(2,1)S(1)}, bf16[512,512]{1,0:T(8,128)(2,1)}, u32[]{:S(2)}) copy-start(bf16[512,512]{1,0:T(8,128)(2,1)} %constant.28.clone.cl_ref) | copy-start | bytes 1572868
  99.5 32.3 %copy-start.2 = (bf16[4,64,96]{2,1,0:T(8,128)(2,1)S(1)}, bf16[4,64,96]{2,1,0:T(8,128)(2,1)}, u32[]{:S(2)}) copy-start(bf16[4,64,96]{2,1,0:T(8,128)(2,1)} %constant.29.clone.high_ref) | copy-start | bytes 147460
  99.5 32.3 %copy-start.3 = (bf16[4,64,96]{2,1,0:T(8,128)(2,1)S(1)}, bf16[4,64,96]{2,1,0:T(8,128)(2,1)}, u32[]{:S(2)}) copy-start(bf16[4,64,96]{2,1,0:T(8,128)(2,1)} %constant.30.clone.low_ref) | copy-start | bytes 147460
  120.5 6.9 %collective-permute-start.4 = (bf16[10,16,512]{2,1,0:T(8,128)(2,1)S(1)}, bf16[10,16,512]{2,1,0:T(8,128)(2,1)S(1)}, u32[]{:S(2)}, u32[]{:S(2)}) collective-permute-start(bf16[10,16,512]{2,1,0:T(8,128)(2,1)S(1)} %get-tuple-element.20), channel_id=1, source_target_pairs={{0,1},{1,2},{2,3},{4,5},{5,6},{6,7},{8,9},{9,10},{10,11},{12,13},{... | collective-permute-start | bytes 491528 | tf_op jit(solution)/shard_map/ppermute | solution.py:507
  125.2 6.6 %collective-permute-start.5 = (bf16[10,16,512]{2,1,0:T(8,128)(2,1)S(1)}, bf16[10,16,512]{2,1,0:T(8,128)(2,1)S(1)}, u32[]{:S(2)}, u32[]{:S(2)}) collective-permute-start(bf16[10,16,512]{2,1,0:T(8,128)(2,1)S(1)} %get-tuple-element.21), channel_id=1, source_target_pairs={{1,0},{2,1},{3,2},{5,4},{6,5},{7,6},{9,8},{10,9},{11,10},{13,12},{... | collective-permute-start | bytes 491528 | tf_op jit(solution)/shard_map/ppermute | solution.py:507

commit v8 on v6

--- a/solution.py
+++ b/solution.py
@@ -264,7 +264,7 @@
 
     start = [band[j * 8 : (j + 1) * 8, :] for j in range(BAND + 1)]
     start += [unit(j) for j in range(BAND + 1)]
-    lax.fori_loop(0, NDATES, down, tuple(start), unroll=4)
+    lax.fori_loop(0, NDATES, down, tuple(start), unroll=8)
 
     def up(t, carry):
         i = NDATES - 1 - t
@@ -277,7 +277,7 @@
         return (x,) + carry[:-1]
 
     zero = band[pl.ds((NDATES + BAND) * 8, 8), :]
-    lax.fori_loop(0, NDATES, up, (zero,) * BAND, unroll=8)
+    lax.fori_loop(0, NDATES, up, (zero,) * BAND, unroll=16)
 
     total = jnp.zeros((NDATES, nifg), F32)
     inverse = jnp.concatenate(

time: 133 us -> 133 us (level)
  no operation moved by 1% of the time
where the time goes in v8:
time: 133 us; the launch traced here: 132 us
  Pallas kernels  58 us (44%)
  starting transfers between devices  27.2 us (20%)
  waiting for transfers between devices  23.6 us (18%)
  blocking collectives  16.6 us (12%)
  other arithmetic  3.08 us (2%)
  local copies, waits for them, and re-layouts  3.02 us (2%)
    pallas_call x2, Pallas kernels, edge(): pl.pallas_call(lambda *refs: edge_kernel(upper, *refs), grid=(n // g,), i...  24 us
    all_to_all x2, waiting for transfers between devices, on_device(): sines = lax.all_to_all(q, 'ifg', split_axis=0, concat_axis=0, tiled=True)  21.2 us
    all_to_all x1, blocking collectives, on_device(): lax.all_to_all(series[0].reshape(devices, -1, LANES), 'ifg', split_axis=0...  16.6 us
    all_to_all x2, starting transfers between devices, on_device(): sines = lax.all_to_all(q, 'ifg', split_axis=0, concat_axis=0, tiled=True)  14.2 us
    pallas_call x2, Pallas kernels, invert(): pl.pallas_call(invert_kernel, grid=(pixels // width,), in_specs=[pl.Block...  10.4 us
    pallas_call x1, Pallas kernels, centre(): pl.pallas_call(centre_kernel, grid=(n // g,), in_specs=[block, block, who...  10.2 us
    pallas_call x1, Pallas kernels, projection(): pl.pallas_call(projection_kernel, out_shape=(pltpu.HBM((NDATES, nifg), BF...  9.33 us
    ppermute x2, starting transfers between devices, neighbours(): lax.ppermute(high_part, axis, forward)  6.85 us
  transfers between devices with their start and end apart: 6, of which 3 were waited for; matrix products, arithmetic and copies ran while one was open for 1% of the time, Pallas kernels for 37%

profile of v8, /device:TPU:1, one launch (start us, length us, event | category | flops | bytes accessed | tf_op | source)
XLA Modules:
  0.0 132.2 jit_solution(11158054174760141289)
XLA Ops:
  0.6 2.8 %slice_bitcast_fusion = (bf16[1,32,32,512]{3,2,1,0:T(8,128)(2,1)S(1)}, bf16[1,32,32,512]{3,2,1,0:T(8,128)(2,1)S(1)}, bf16[1,32,32,512]{3,2,1,0:T(8,128)(2,1)S(1)}, bf16[1,32,32,512]{3,2,1,0:T(8,128)(2,1)S(1)}) fusion(bf16[32,64,512]{2,1,0:T(8,128)(2,1)} %refs_1_.3, bf16[32,64,512]{2,1,0:T(8,128)(2,1)} %refs_0_.3), kind=kLoop, calls=%fused_computation.2 | loop fusion | bytes 8388608 | tf_op jit(solution)/shard_map/stack | solution.py:479
  3.4 1.6 %pad_maximum_fusion.1 = bf16[2,32,32,512]{3,2,1,0:T(8,128)(2,1)} fusion(bf16[1,32,32,512]{3,2,1,0:T(8,128)(2,1)S(1)} %get-tuple-element.22, bf16[1,32,32,512]{3,2,1,0:T(8,128)(2,1)S(1)} %get-tuple-element.25), kind=kLoop, calls=%fused_computation.1 | loop fusion | flops 1048576 | bytes 4194304 | tf_op jit(solution)/shard_map/stack | solution.py:479
  5.0 4.9 %collective-permute-start.1 = (bf16[2,32,32,512]{3,2,1,0:T(8,128)(2,1)}, bf16[2,32,32,512]{3,2,1,0:T(8,128)(2,1)}, u32[]{:S(2)}, u32[]{:S(2)}) collective-permute-start(bf16[2,32,32,512]{3,2,1,0:T(8,128)(2,1)} %pad_maximum_fusion.1), channel_id=1, source_target_pairs={{0,1},{1,2},{2,3},{4,5},{5,6},{6,7},{8,9},{9,10},{10,11},{12,13},{... | collective-permute-start | bytes 6291464 | tf_op jit(solution)/shard_map/ppermute | solution.py:469
  9.9 1.5 %pad_maximum_fusion = bf16[2,32,32,512]{3,2,1,0:T(8,128)(2,1)} fusion(bf16[1,32,32,512]{3,2,1,0:T(8,128)(2,1)S(1)} %get-tuple-element.23, bf16[1,32,32,512]{3,2,1,0:T(8,128)(2,1)S(1)} %get-tuple-element.24), kind=kLoop, calls=%fused_computation | loop fusion | flops 1048576 | bytes 4194304 | tf_op jit(solution)/shard_map/stack | solution.py:478
  11.4 1.9 %collective-permute-start = (bf16[2,32,32,512]{3,2,1,0:T(8,128)(2,1)}, bf16[2,32,32,512]{3,2,1,0:T(8,128)(2,1)S(1)}, u32[]{:S(2)}, u32[]{:S(2)}) collective-permute-start(bf16[2,32,32,512]{3,2,1,0:T(8,128)(2,1)} %pad_maximum_fusion), channel_id=1, source_target_pairs={{1,0},{2,1},{3,2},{5,4},{6,5},{7,6},{9,8},{10,9},{11,10},{13,12},{... | collective-permute-start | bytes 6291464 | tf_op jit(solution)/shard_map/ppermute | solution.py:469
  13.4 0.2 copy.14.pairs_ref
  13.6 9.3 %projection.1 = (bf16[320,1024]{1,0:T(8,128)(2,1)}, bf16[1024,640]{1,0:T(8,128)(2,1)}) custom-call(s32[1024,2]{1,0:T(8,128)S(1)} %copy.14.pairs_ref, s32[2,1024]{1,0:T(2,128)S(1)} %bitcast.18), custom_call_target="tpu_custom_call" | custom-call | flops 20000000000 | bytes 4000000 | tf_op jit(solution)/shard_map/projection/pallas_call | solution.py:300
  22.9 10.2 %centre.1.refs_3_ = bf16[32,128,512]{2,1,0:T(8,128)(2,1)} custom-call(bf16[32,64,512]{2,1,0:T(8,128)(2,1)} %refs_0_.3, bf16[32,64,512]{2,1,0:T(8,128)(2,1)} %refs_1_.3, bf16[128,128]{1,0:T(8,128)(2,1)} %constant.22.clone.rows_ref.refs_4_, bf16[256,256]{1,0:T(8,128)(2,1)} %constant.23.clone.fwd_ref.refs_5_, bf16[256,256]{1,0:T(8,128)(2,1)} %constant.24.clone.inv_ref.refs_6_), custom_call_target="tpu_custom_call" | custom-call | flops 6979321856 | bytes 8388608 | tf_op jit(solution)/shard_map/centre/pallas_call | solution.py:146
  33.1 0.0 collective-permute-done.1.refs_2_
  33.2 12.1 %upper.1 = bf16[32,32,512]{2,1,0:T(8,128)(2,1)} custom-call(bf16[32,64,512]{2,1,0:T(8,128)(2,1)} %refs_0_.3, bf16[32,64,512]{2,1,0:T(8,128)(2,1)} %refs_1_.3, bf16[2,32,32,512]{3,2,1,0:T(8,128)(2,1)} %collective-permute-done.1.refs_2_, bf16[32,128,512]{2,1,0:T(8,128)(2,1)} %centre.1.refs_3_, bf16[128,128]{1,0:T(8,128)(2,1)} %constant.22.clone.rows_ref.refs_4_, ...), custom_call_target="tpu_custom_call" | custom-call | flops 8053063680 | bytes 7340032 | tf_op jit(solution)/shard_map/upper/pallas_call | solution.py:195
  45.2 10.1 %all-to-all-start.1 = ((bf16[32,32,512]{2,1,0:T(8,128)(2,1)}), bf16[32,32,512]{2,1,0:T(8,128)(2,1)S(1)}, u32[]{:S(2)}, u32[]{:S(2)}) async-start(bf16[32,32,512]{2,1,0:T(8,128)(2,1)} %upper.1), calls=%async_computation.1 | async-start | bytes 2097152 | tf_op jit(solution)/shard_map/all_to_all | solution.py:487
  55.3 12.0 %lower.1 = bf16[32,32,512]{2,1,0:T(8,128)(2,1)} custom-call(bf16[32,64,512]{2,1,0:T(8,128)(2,1)} %refs_0_.3, bf16[32,64,512]{2,1,0:T(8,128)(2,1)} %refs_1_.3, bf16[2,32,32,512]{3,2,1,0:T(8,128)(2,1)S(1)} %collective-permute-done.refs_2_, bf16[32,128,512]{2,1,0:T(8,128)(2,1)} %centre.1.refs_3_, bf16[128,128]{1,0:T(8,128)(2,1)} %constant.22.clone.rows_ref.refs_4_, ...), custom_call_target="tpu_custom_call" | custom-call | flops 8053063680 | bytes 7340032 | tf_op jit(solution)/shard_map/lower/pallas_call | solution.py:195
  67.3 7.9 %all-to-all-done.1 = bf16[32,32,512]{2,1,0:T(8,128)(2,1)S(1)} async-done(((bf16[32,32,512]{2,1,0:T(8,128)(2,1)}), bf16[32,32,512]{2,1,0:T(8,128)(2,1)S(1)}, u32[]{:S(2)}, u32[]{:S(2)}) %all-to-all-start.1) | async-done | bytes 1048608 | tf_op jit(solution)/shard_map/all_to_all | solution.py:487
  75.2 4.1 %all-to-all-start = ((bf16[32,32,512]{2,1,0:T(8,128)(2,1)}), bf16[32,32,512]{2,1,0:T(8,128)(2,1)S(1)}, u32[]{:S(2)}, u32[]{:S(2)}) async-start(bf16[32,32,512]{2,1,0:T(8,128)(2,1)} %lower.1), calls=%async_computation | async-start | bytes 2097152 | tf_op jit(solution)/shard_map/all_to_all | solution.py:487
  79.3 5.5 %invert.1.refs_0_ = f32[1280,128]{1,0:T(8,128)} custom-call(bf16[1024,512]{1,0:T(8,128)(2,1)S(1)} %bitcast.15, bf16[320,1024]{1,0:T(8,128)(2,1)} %get-tuple-element.14.p_ref, bf16[1024,640]{1,0:T(8,128)(2,1)} %get-tuple-element.15.g_ref), custom_call_target="tpu_custom_call" | custom-call | flops 2348810240 | bytes 6000000 | tf_op jit(solution)/shard_map/invert/pallas_call | solution.py:361
  84.8 13.3 %all-to-all-done = bf16[32,32,512]{2,1,0:T(8,128)(2,1)S(1)} async-done(((bf16[32,32,512]{2,1,0:T(8,128)(2,1)}), bf16[32,32,512]{2,1,0:T(8,128)(2,1)S(1)}, u32[]{:S(2)}, u32[]{:S(2)}) %all-to-all-start) | async-done | bytes 1048608 | tf_op jit(solution)/shard_map/all_to_all | solution.py:487
  98.1 5.0 %invert_rest.1 = bf16[2560,128]{1,0:T(8,128)(2,1)S(1)} custom-call(bf16[1024,512]{1,0:T(8,128)(2,1)S(1)} %bitcast.16, bf16[320,1024]{1,0:T(8,128)(2,1)} %get-tuple-element.14.p_ref, bf16[1024,640]{1,0:T(8,128)(2,1)} %get-tuple-element.15.g_ref, f32[1280,128]{1,0:T(8,128)} %invert.1.refs_0_), custom_call_target="tpu_custom_call" | custom-call | flops 2348810240 | bytes 6000000 | tf_op jit(solution)/shard_map/invert_rest/pallas_call | solution.py:361
  103.1 0.0 copy-start.3
  103.1 16.6 %all_to_all.15 = bf16[32,80,128]{2,1,0:T(8,128)(2,1)S(1)} all-to-all(bf16[32,80,128]{2,1,0:T(8,128)(2,1)S(1)} %bitcast.17), channel_id=1, replica_groups=mesh['ifg'=32,'row'=4] {'ifg'}, dimensions={0} | all-to-all | bytes 1310720 | tf_op jit(solution)/shard_map/all_to_all | solution.py:490
  119.7 2.0 %gather.1 = (f32[10,64,512]{2,1,0:T(8,128)S(1)}, f32[10,64,512]{2,1,0:T(8,128)S(1)}, bf16[10,16,512]{2,1,0:T(8,128)(2,1)S(1)}, bf16[10,16,512]{2,1,0:T(8,128)(2,1)S(1)}) custom-call(bf16[2560,128]{1,0:T(8,128)(2,1)S(1)} %bitcast.14, bf16[512,512]{1,0:T(8,128)(2,1)S(1)} %copy-done, bf16[512,512]{1,0:T(8,128)(2,1)S(1)} %copy-done.1), custom_call_target="tpu_custom_call" | custom-call | tf_op jit(solution)/shard_map/gather/pallas_call | solution.py:423
  121.6 1.9 %collective-permute-start.2 = (bf16[10,16,512]{2,1,0:T(8,128)(2,1)S(1)}, bf16[10,16,512]{2,1,0:T(8,128)(2,1)S(1)}, u32[]{:S(2)}, u32[]{:S(2)}) collective-permute-start(bf16[10,16,512]{2,1,0:T(8,128)(2,1)S(1)} %get-tuple-element.18), channel_id=1, source_target_pairs={{0,1},{1,2},{2,3},{4,5},{5,6},{6,7},{8,9},{9,10},{10,11},{12,13},{... | collective-permute-start | bytes 491528 | tf_op jit(solution)/shard_map/ppermute | solution.py:469
  123.6 4.2 %collective-permute-start.3 = (bf16[10,16,512]{2,1,0:T(8,128)(2,1)S(1)}, bf16[10,16,512]{2,1,0:T(8,128)(2,1)S(1)}, u32[]{:S(2)}, u32[]{:S(2)}) collective-permute-start(bf16[10,16,512]{2,1,0:T(8,128)(2,1)S(1)} %get-tuple-element.19), channel_id=1, source_target_pairs={{1,0},{2,1},{3,2},{5,4},{6,5},{7,6},{9,8},{10,9},{11,10},{13,12},{... | collective-permute-start | bytes 491528 | tf_op jit(solution)/shard_map/ppermute | solution.py:469
  127.8 2.4 %collective-permute-done.3.dn_ref = bf16[10,16,512]{2,1,0:T(8,128)(2,1)S(1)} collective-permute-done((bf16[10,16,512]{2,1,0:T(8,128)(2,1)S(1)}, bf16[10,16,512]{2,1,0:T(8,128)(2,1)S(1)}, u32[]{:S(2)}, u32[]{:S(2)}) %collective-permute-start.3) | collective-permute-done | bytes 163872 | tf_op jit(solution)/shard_map/ppermute | solution.py:469
  130.2 2.0 %finish.1 = (f32[10,64,512]{2,1,0:T(8,128)}, f32[10,64,512]{2,1,0:T(8,128)}) custom-call(s32[1]{0:T(128)} %bitcast.where_ref, f32[10,64,512]{2,1,0:T(8,128)S(1)} %get-tuple-element.16.series_ref, f32[10,64,512]{2,1,0:T(8,128)S(1)} %get-tuple-element.17.smooth_ref, bf16[10,16,512]{2,1,0:T(8,128)(2,1)S(1)} %collective-permute-done.2.up_ref, ...), custom_call_target="tpu_custom_call" | custom-call | tf_op jit(solution)/shard_map/finish/pallas_call | solution.py:448
  (11 shorter events, 0.0 us)
Async XLA Ops:
  5.0 28.2 %collective-permute-start.1 = (bf16[2,32,32,512]{3,2,1,0:T(8,128)(2,1)}, bf16[2,32,32,512]{3,2,1,0:T(8,128)(2,1)}, u32[]{:S(2)}, u32[]{:S(2)}) collective-permute-start(bf16[2,32,32,512]{3,2,1,0:T(8,128)(2,1)} %pad_maximum_fusion.1), channel_id=1, source_target_pairs={{0,1},{1,2},{2,3},{4,5},{5,6},{6,7},{8,9},{9,10},{10,11},{12,13},{... | collective-permute-start | bytes 6291464 | tf_op jit(solution)/shard_map/ppermute | solution.py:469
  9.9 3.5 %copy-start.4 = (s32[1024,2]{0,1:T(2,128)S(1)}, s32[1024,2]{0,1:T(2,128)}, u32[]{:S(2)}) copy-start(s32[1024,2]{0,1:T(2,128)} %param.14) | copy-start | bytes 24580
  11.4 43.9 %collective-permute-start = (bf16[2,32,32,512]{3,2,1,0:T(8,128)(2,1)}, bf16[2,32,32,512]{3,2,1,0:T(8,128)(2,1)S(1)}, u32[]{:S(2)}, u32[]{:S(2)}) collective-permute-start(bf16[2,32,32,512]{3,2,1,0:T(8,128)(2,1)} %pad_maximum_fusion), channel_id=1, source_target_pairs={{1,0},{2,1},{3,2},{5,4},{6,5},{7,6},{9,8},{10,9},{11,10},{13,12},{... | collective-permute-start | bytes 6291464 | tf_op jit(solution)/shard_map/ppermute | solution.py:469
  45.2 30.0 %all-to-all-start.1 = ((bf16[32,32,512]{2,1,0:T(8,128)(2,1)}), bf16[32,32,512]{2,1,0:T(8,128)(2,1)S(1)}, u32[]{:S(2)}, u32[]{:S(2)}) async-start(bf16[32,32,512]{2,1,0:T(8,128)(2,1)} %upper.1), calls=%async_computation.1 | async-start | bytes 2097152 | tf_op jit(solution)/shard_map/all_to_all | solution.py:487
  75.2 22.8 %all-to-all-start = ((bf16[32,32,512]{2,1,0:T(8,128)(2,1)}), bf16[32,32,512]{2,1,0:T(8,128)(2,1)S(1)}, u32[]{:S(2)}, u32[]{:S(2)}) async-start(bf16[32,32,512]{2,1,0:T(8,128)(2,1)} %lower.1), calls=%async_computation | async-start | bytes 2097152 | tf_op jit(solution)/shard_map/all_to_all | solution.py:487
  98.1 21.6 %copy-start = (bf16[512,512]{1,0:T(8,128)(2,1)S(1)}, bf16[512,512]{1,0:T(8,128)(2,1)}, u32[]{:S(2)}) copy-start(bf16[512,512]{1,0:T(8,128)(2,1)} %constant.27.clone.ch_ref) | copy-start | bytes 1572868
  98.1 21.6 %copy-start.1 = (bf16[512,512]{1,0:T(8,128)(2,1)S(1)}, bf16[512,512]{1,0:T(8,128)(2,1)}, u32[]{:S(2)}) copy-start(bf16[512,512]{1,0:T(8,128)(2,1)} %constant.28.clone.cl_ref) | copy-start | bytes 1572868
  103.0 27.2 %copy-start.2 = (bf16[4,64,96]{2,1,0:T(8,128)(2,1)S(1)}, bf16[4,64,96]{2,1,0:T(8,128)(2,1)}, u32[]{:S(2)}) copy-start(bf16[4,64,96]{2,1,0:T(8,128)(2,1)} %constant.29.clone.high_ref) | copy-start | bytes 147460
  103.1 27.2 %copy-start.3 = (bf16[4,64,96]{2,1,0:T(8,128)(2,1)S(1)}, bf16[4,64,96]{2,1,0:T(8,128)(2,1)}, u32[]{:S(2)}) copy-start(bf16[4,64,96]{2,1,0:T(8,128)(2,1)} %constant.30.clone.low_ref) | copy-start | bytes 147460
  121.6 6.2 %collective-permute-start.2 = (bf16[10,16,512]{2,1,0:T(8,128)(2,1)S(1)}, bf16[10,16,512]{2,1,0:T(8,128)(2,1)S(1)}, u32[]{:S(2)}, u32[]{:S(2)}) collective-permute-start(bf16[10,16,512]{2,1,0:T(8,128)(2,1)S(1)} %get-tuple-element.18), channel_id=1, source_target_pairs={{0,1},{1,2},{2,3},{4,5},{5,6},{6,7},{8,9},{9,10},{10,11},{12,13},{... | collective-permute-start | bytes 491528 | tf_op jit(solution)/shard_map/ppermute | solution.py:469
  123.6 6.6 %collective-permute-start.3 = (bf16[10,16,512]{2,1,0:T(8,128)(2,1)S(1)}, bf16[10,16,512]{2,1,0:T(8,128)(2,1)S(1)}, u32[]{:S(2)}, u32[]{:S(2)}) collective-permute-start(bf16[10,16,512]{2,1,0:T(8,128)(2,1)S(1)} %get-tuple-element.19), channel_id=1, source_target_pairs={{1,0},{2,1},{3,2},{5,4},{6,5},{7,6},{9,8},{10,9},{11,10},{13,12},{... | collective-permute-start | bytes 491528 | tf_op jit(solution)/shard_map/ppermute | solution.py:469
